TPU v7x, 32 devices: a whole 2x2x4 slice. The times are simulated.
32 devices in a mesh: groups: 2 (over y), gx: 16 (over z, x, core).
Axes of the slice: x: 2, y: 2, z: 4, core: 2. Of those that a mesh axis runs over, the one named last changes fastest.
Arguments:
- populations: float32 [19, 128, 8192], P(None, ('groups', 'gx')), parts along dimension 1, as said below
- relax_class: int32 [128, 8192], P(('groups', 'gx')), parts along dimension 0, may hold values from 0 to 3
- cotangent: float32 [19, 128, 8192], P(None, ('groups', 'gx')), parts along dimension 1, may hold values from -6 to 6
Outputs:
- final_populations: float32 [19, 128, 8192], P(None, ('groups', 'gx')), parts along dimension 1
- initial_gradient: float32 [19, 128, 8192], P(None, ('groups', 'gx')), parts along dimension 1
There are 2 independent parts, one for each index of `groups`. A program takes and returns all parts, laid end to end along the dimension named above; each array names one. Nothing has to cross between parts.
Inputs may be any that keep to these rules, and one draw needn't show every extreme that they name: populations in direction k lie between 0.5 w_k and 1.5 w_k, w_k the lattice weights.
All inputs are finite; a program needn't handle non-finite values.
Results may differ from a plain program's by a relative error of at most 0.0001.
Values sent between devices are 32-bit elements; how exact they have to be, the bound alone decides.
No kernel may reach another device: no remote copies, remote signals or barrier semaphores. Data moves between devices by JAX's collectives and lax.ppermute only.
A program may use at most 64 MiB of HBM per device.

v0:
```python
import jax
import jax.numpy as jnp
from jax import lax
from jax.experimental import pallas as pl
from jax.experimental.pallas import tpu as pltpu
from jax.sharding import PartitionSpec as P

PLANES, ROWS, LANES, BLOCKS = 4, 64, 128, 8
SPEEDS = [
    (0, 0, 0), (1, 0, 0), (-1, 0, 0), (0, 1, 0), (0, -1, 0), (0, 0, 1), (0, 0, -1),
    (1, 1, 0), (-1, -1, 0), (1, -1, 0), (-1, 1, 0), (1, 0, 1), (-1, 0, -1),
    (1, 0, -1), (-1, 0, 1), (0, 1, 1), (0, -1, -1), (0, 1, -1), (0, -1, 1),
]
RATES = [1.0 / 1.0, 1.0 / 1.25, 1.0 / 1.6, 1.0 / 2.4]
MIRROR = [SPEEDS.index((-cx, cy, cz)) for cx, cy, cz in SPEEDS]
PLUS = [k for k in range(19) if SPEEDS[k][0] == 1]
MINUS = [MIRROR[k] for k in PLUS]
F32 = jnp.float32


def iotas():
    lane = lax.broadcasted_iota(jnp.int32, (8, LANES), 1)
    row = lax.broadcasted_iota(jnp.int32, (8, LANES), 0)
    return {"high": lane >= 64, "first": lane % 64 == 0, "last": lane % 64 == 63,
            "top": row == 0, "bottom": row == 7}


def block(r):
    return pl.ds(pl.multiple_of(r * 8, 8), 8)


def shifted(ref, index, r, cy, cz, m):
    here = ref[index + (block(r), slice(None))]
    turn = 0
    if cy == 1:
        edge = ref[index + (pl.ds(lax.rem(r + 7, 8) * 8 + 7, 1), slice(None))]
        other = jnp.where(m["top"], edge, pltpu.roll(here, 1, 0))
        here, turn = jnp.where(m["high"], other, here), 64
    elif cy == -1:
        edge = ref[index + (pl.ds(lax.rem(r + 1, 8) * 8, 1), slice(None))]
        other = jnp.where(m["bottom"], edge, pltpu.roll(here, 7, 0))
        here, turn = jnp.where(m["high"], here, other), 64
    if cz == 0:
        return pltpu.roll(here, turn, 1) if turn else here
    main = pltpu.roll(here, (turn + cz) % LANES, 1)
    wrapped = pltpu.roll(here, (turn + cz + 64) % LANES, 1)
    return jnp.where(m["first"] if cz == 1 else m["last"], wrapped, main)


def moments(f):
    s = [f[k] + f[k + 1] for k in range(1, 19, 2)]
    d = [f[k] - f[k + 1] for k in range(1, 19, 2)]
    rho = f[0] + ((s[0] + s[1]) + (s[2] + s[3])) + ((s[4] + s[5]) + (s[6] + s[7])) + s[8]
    jx = d[0] + ((d[3] + d[4]) + (d[5] + d[6]))
    jy = d[1] + ((d[3] - d[4]) + (d[7] + d[8]))
    jz = d[2] + ((d[5] - d[6]) + (d[7] - d[8]))
    return rho, jx, jy, jz


def along(k, v):
    total = None
    for c, x in zip(SPEEDS[k], v):
        if c:
            x = x if c == 1 else -x
            total = x if total is None else (total + x)
    return total


def along_odd(k, v):
    total = None
    for c, x in zip(SPEEDS[k], v):
        if c:
            total = x if total is None else (total + x if c == 1 else total - x)
    return total


def relaxed(f, rho, u, om):
    keep = 1.0 - om
    wr = om * rho
    shape = 1.0 - 1.5 * (u[0] * u[0] + u[1] * u[1] + u[2] * u[2])
    out = [None] * 19
    out[0] = keep * f[0] + (wr * (1.0 / 3.0)) * shape
    for first, last, w in ((1, 7, 1.0 / 18.0), (7, 19, 1.0 / 36.0)):
        part = wr * w
        base, lin, quad = part * shape, part * 3.0, part * 4.5
        for k in range(first, last, 2):
            a = along_odd(k, u)
            even, odd = base + quad * (a * a), lin * a
            out[k] = keep * f[k] + (even + odd)
            out[k + 1] = keep * f[k + 1] + (even - odd)
    return out


def adjoint(mu, u, om):
    s = [None] + [mu[k] + mu[k + 1] for k in range(1, 19, 2)]
    d = [None] + [mu[k] - mu[k + 1] for k in range(1, 19, 2)]
    a, b = 1.0 / 18.0, 1.0 / 36.0
    s45, s67, s89 = s[4] + s[5], s[6] + s[7], s[8] + s[9]
    xx = a * s[1] + b * (s45 + s67)
    yy = a * s[2] + b * (s45 + s89)
    zz = a * s[3] + b * (s67 + s89)
    m0 = (1.0 / 3.0) * mu[0] + a * ((s[1] + s[2]) + s[3]) + b * ((s45 + s67) + s89)
    xy, xz, yz = b * (s[4] - s[5]), b * (s[6] - s[7]), b * (s[8] - s[9])
    mx = a * d[1] + b * ((d[4] + d[5]) + (d[6] + d[7]))
    my = a * d[2] + b * ((d[4] - d[5]) + (d[8] + d[9]))
    mz = a * d[3] + b * ((d[6] - d[7]) + (d[8] - d[9]))
    vx = xx * u[0] + xy * u[1] + xz * u[2]
    vy = xy * u[0] + yy * u[1] + yz * u[2]
    vz = xz * u[0] + yz * u[1] + zz * u[2]
    uu = u[0] * u[0] + u[1] * u[1] + u[2] * u[2]
    rho_part = om * (m0 + 1.5 * (m0 * uu) - 4.5 * (u[0] * vx + u[1] * vy + u[2] * vz))
    om3 = 3.0 * om
    flow = [
        om3 * (mx + 3.0 * vx - u[0] * m0),
        om3 * (my + 3.0 * vy - u[1] * m0),
        om3 * (mz + 3.0 * vz - u[2] * m0),
    ]
    keep = 1.0 - om
    out = [None] * 19
    out[0] = keep * mu[0] + rho_part
    for k in range(1, 19, 2):
        g = along_odd(k, flow)
        out[k] = keep * mu[k] + (rho_part + g)
        out[k + 1] = keep * mu[k + 1] + (rho_part - g)
    return out


def pulled(own, far, near, p, r, sign, m):
    plus, minus = (PLUS, MINUS) if sign == 1 else (MINUS, PLUS)
    out = []
    for k in range(19):
        cx, cy, cz = (sign * c for c in SPEEDS[k])
        source = p - cx
        if source < 0:
            out.append(shifted(far, (plus.index(k),), r, cy, cz, m))
        elif source >= PLANES:
            out.append(shifted(near, (minus.index(k),), r, cy, cz, m))
        else:
            out.append(shifted(own, (k, source), r, cy, cz, m))
    return out


def put_edges(values, p, r, far_ref, near_ref, far_set, near_set, offset=0):
    if p == 0:
        for i, k in enumerate(far_set):
            far_ref[offset + i, block(r), :] = values[k]
    if p == PLANES - 1:
        for i, k in enumerate(near_set):
            near_ref[offset + i, block(r), :] = values[k]


def native(flip, k, p, r):
    kk = k if MIRROR[k] == k else jnp.where(flip == 1, MIRROR[k], k)
    x = jnp.where(flip == 1, PLANES - 1 - p, p)
    return kk, pl.ds(r * (8 * PLANES) + x, 8, stride=PLANES)


def loop(body):
    lax.fori_loop(0, BLOCKS, lambda r, c: (body(r), c)[1], 0)


def chunk(ref, r):
    rows = 8 * PLANES
    return ref.at[:, pl.ds(pl.multiple_of(r * rows, rows), rows), :]


def copy_in(hbm, vmem, sem, r):
    return pltpu.make_async_copy(chunk(hbm, r), chunk(vmem, r), sem.at[r])


def flipped():
    return lax.rem(lax.axis_index("gx"), 2)


def put_velocity(u_ref, u, p, r):
    for i in range(3):
        u_ref[i, p, block(r), :] = u[i]


def get_velocity(u_ref, p, r):
    return [u_ref[i, p, block(r), :] for i in range(3)]


def collide_first(pops, classes, post, u0, om_ref, far_out, near_out, hold, sem):
    flip = flipped()
    loop(lambda r: copy_in(pops, hold, sem, r).start())

    def body(r):
        copy_in(pops, hold, sem, r).wait()
        for p in range(PLANES):
            f = []
            for k in range(19):
                kk, rows = native(flip, k, p, r)
                f.append(hold[kk, rows, :])
            cls = classes[native(flip, 0, p, r)[1], :]
            om = jnp.zeros((8, LANES), F32)
            for entry in range(4):
                om = jnp.where(cls == entry, RATES[entry], om)
            om_ref[p, block(r), :] = om
            rho, jx, jy, jz = moments(f)
            inv = 1.0 / rho
            u = [jx * inv, jy * inv, jz * inv]
            put_velocity(u0, u, p, r)
            out = relaxed(f, rho, u, om)
            for k in range(19):
                post[k, p, block(r), :] = out[k]
            put_edges(out, p, r, far_out, near_out, MINUS, PLUS)

    loop(body)


def canonical_cotangent(cot, own, far_out, near_out):
    flip = flipped()

    def body(r):
        for p in range(PLANES):
            values = []
            for k in range(19):
                kk, rows = native(flip, k, p, r)
                values.append(cot[kk, rows, :])
                own[k, p, block(r), :] = values[k]
            put_edges(values, p, r, far_out, near_out, PLUS, MINUS)

    loop(body)


def forward_step(own, far, near, om_ref, post, u_ref, far_out, near_out):
    m = iotas()

    def body(r):
        for p in range(PLANES):
            f = pulled(own, far, near, p, r, 1, m)
            rho, jx, jy, jz = moments(f)
            inv = 1.0 / rho
            u = [jx * inv, jy * inv, jz * inv]
            put_velocity(u_ref, u, p, r)
            out = relaxed(f, rho, u, om_ref[p, block(r), :])
            for k in range(19):
                post[k, p, block(r), :] = out[k]
            put_edges(out, p, r, far_out, near_out, MINUS, PLUS)

    loop(body)


def adjoint_step(own, far, near, om_ref, u_ref, lam, far_out, near_out):
    m = iotas()

    def body(r):
        for p in range(PLANES):
            mu = pulled(own, far, near, p, r, -1, m)
            out = adjoint(mu, get_velocity(u_ref, p, r), om_ref[p, block(r), :])
            for k in range(19):
                lam[k, p, block(r), :] = out[k]
            put_edges(out, p, r, far_out, near_out, PLUS, MINUS)

    loop(body)


def stream_last(own, far, near, final, hold, sem):
    flip, m = flipped(), iotas()

    def body(r):
        for p in range(PLANES):
            f = pulled(own, far, near, p, r, 1, m)
            for k in range(19):
                kk, rows = native(flip, k, p, r)
                hold[kk, rows, :] = f[k]
        pltpu.make_async_copy(chunk(hold, r), chunk(final, r), sem.at[r]).start()

    loop(body)
    loop(lambda r: pltpu.make_async_copy(chunk(hold, r), chunk(final, r), sem.at[r]).wait())


def adjoint_last(own, far, near, om_ref, u_ref, grad, hold, sem):
    flip, m = flipped(), iotas()

    def body(r):
        for p in range(PLANES):
            mu = pulled(own, far, near, p, r, -1, m)
            out = adjoint(mu, get_velocity(u_ref, p, r), om_ref[p, block(r), :])
            for k in range(19):
                kk, rows = native(flip, k, p, r)
                hold[kk, rows, :] = out[k]
        pltpu.make_async_copy(chunk(hold, r), chunk(grad, r), sem.at[r]).start()

    loop(body)
    loop(lambda r: pltpu.make_async_copy(chunk(hold, r), chunk(grad, r), sem.at[r]).wait())


INSIDE = pl.BlockSpec(memory_space=pltpu.VMEM)
OUTSIDE = pl.BlockSpec(memory_space=pltpu.HBM)
FULL = (19, PLANES, ROWS, LANES)
VELOCITY = (3, PLANES, ROWS, LANES)
RELAX = (PLANES, ROWS, LANES)
EDGE = (5, ROWS, LANES)
NATIVE = (19, PLANES * ROWS, LANES)
STAGED = [pltpu.VMEM(NATIVE, F32), pltpu.SemaphoreType.DMA((BLOCKS,))]


def kernel(body, outs, scratch=(), flops=0):
    def call(*args):
        specs = [INSIDE if inside else OUTSIDE for _, inside in args]
        args = [
            pltpu.with_memory_space_constraint(x, pltpu.VMEM if inside else pltpu.HBM)
            for x, inside in args
        ]
        return pl.pallas_call(
            body,
            in_specs=specs,
            out_specs=[INSIDE if inside else OUTSIDE for _, inside in outs],
            out_shape=[
                pltpu.VMEM(s, F32) if inside else jax.ShapeDtypeStruct(s, F32) for s, inside in outs
            ],
            scratch_shapes=list(scratch),
            compiler_params=pltpu.CompilerParams(vmem_limit_bytes=16 * 2**20),
        )(*args)

    return call


def local(populations, relax_class, cotangent):
    count = lax.axis_size("gx")
    near_pairs = [(i, i ^ 1) for i in range(count)]
    far_pairs = [(i, (i + 1 if i % 2 else i - 1) % count) for i in range(count)]

    def exchange(far, near):
        return lax.ppermute(far, "gx", far_pairs), lax.ppermute(near, "gx", near_pairs)

    def to_native(x):
        lead = x.shape[:-2]
        x = x.reshape(lead + (PLANES, ROWS, LANES))
        return jnp.swapaxes(x, -3, -2).reshape(lead + (PLANES * ROWS, LANES))

    def from_native(x):
        return jnp.swapaxes(x.reshape(19, ROWS, PLANES, LANES), 1, 2).reshape(populations.shape)

    pops, classes, cot = to_native(populations), to_native(relax_class), to_native(cotangent)
    edges = [(EDGE, 1), (EDGE, 1)]
    post0, u0, om, far, near = kernel(
        collide_first, [(FULL, 1), (VELOCITY, 1), (RELAX, 1)] + edges, STAGED
    )((pops, 0), (classes, 1))
    far0, near0 = exchange(far, near)
    lam3, far, near = kernel(canonical_cotangent, [(FULL, 1)] + edges)((cot, 1))
    farc, nearc = exchange(far, near)
    step = kernel(forward_step, [(FULL, 1), (VELOCITY, 1)] + edges)
    back = kernel(adjoint_step, [(FULL, 1)] + edges)
    post1, u1, far, near = step((post0, 1), (far0, 1), (near0, 1), (om, 1))
    far1, near1 = exchange(far, near)
    post2, u2, far, near = step((post1, 1), (far1, 1), (near1, 1), (om, 1))
    far2, near2 = exchange(far, near)
    lam2, far, near = back((lam3, 1), (farc, 1), (nearc, 1), (om, 1), (u2, 1))
    farb, nearb = exchange(far, near)
    lam1, far, near = back((lam2, 1), (farb, 1), (nearb, 1), (om, 1), (u1, 1))
    fara, neara = exchange(far, near)
    (final,) = kernel(stream_last, [(NATIVE, 0)], STAGED)((post2, 1), (far2, 1), (near2, 1))
    (grad,) = kernel(adjoint_last, [(NATIVE, 0)], STAGED)(
        (lam1, 1), (fara, 1), (neara, 1), (om, 1), (u0, 1)
    )
    return from_native(final), from_native(grad)


def solution(mesh):
    return jax.shard_map(
        local,
        mesh=mesh,
        in_specs=(
            P(None, ("groups", "gx"), None),
            P(("groups", "gx"), None),
            P(None, ("groups", "gx"), None),
        ),
        out_specs=(P(None, ("groups", "gx"), None), P(None, ("groups", "gx"), None)),
        check_vma=False,
    )
```

profile of v0, /device:TPU:0, one launch (start us, length us, event | category | flops | bytes accessed | tf_op | source)
XLA Modules:
  0.0 47.5 jit_solution(17532012014681158621)
XLA Ops:
  0.6 1.0 %copy-done.1 = s32[4,8192]{1,0:T(4,128)S(1)} copy-done((s32[4,8192]{1,0:T(4,128)S(1)}, s32[4,8192]{1,0:T(4,128)}, u32[]{:S(2)}) %copy-start.1) | copy-done | bytes 131096
  1.7 2.1 %shard_map.50 = (f32[19,4,64,128]{3,2,1,0:T(8,128)S(1)}, f32[3,4,64,128]{3,2,1,0:T(8,128)S(1)}, f32[4,64,128]{2,1,0:T(8,128)S(1)}, f32[5,64,128]{2,1,0:T(8,128)S(1)}, f32[5,64,128]{2,1,0:T(8,128)S(1)}) custom-call(f32[19,256,128]{2,1,0:T(8,128)} %bitcast.27, s32[256,128]{1,0:T(8,128)S(1)} %bitcast.26), custom_call_target="tpu_custom_call" | custom-call | tf_op jit(solution)/shard_map/pallas_call | solution.py:307
  3.8 5.5 %collective-permute-start = (f32[5,64,128]{2,1,0:T(8,128)S(1)}, f32[5,64,128]{2,1,0:T(8,128)S(1)}, u32[]{:S(2)}, u32[]{:S(2)}) collective-permute-start(f32[5,64,128]{2,1,0:T(8,128)S(1)} %get-tuple-element.25), channel_id=1, source_target_pairs={{0,15},{1,2},{2,1},{3,4},{4,3},{5,6},{6,5},{7,8},{8,7},{9,10},{10,... | collective-permute-start | bytes 491528 | tf_op jit(solution)/shard_map/ppermute | solution.py:327
  9.2 0.0 collective-permute-start.1
  9.3 0.5 shard_map.54
  9.7 2.5 %collective-permute-done.far = f32[5,64,128]{2,1,0:T(8,128)S(1)} collective-permute-done((f32[5,64,128]{2,1,0:T(8,128)S(1)}, f32[5,64,128]{2,1,0:T(8,128)S(1)}, u32[]{:S(2)}, u32[]{:S(2)}) %collective-permute-start) | collective-permute-done | bytes 163872 | tf_op jit(solution)/shard_map/ppermute | solution.py:327
  12.3 2.0 %shard_map.51 = (f32[19,4,64,128]{3,2,1,0:T(8,128)S(1)}, f32[3,4,64,128]{3,2,1,0:T(8,128)S(1)}, f32[5,64,128]{2,1,0:T(8,128)S(1)}, f32[5,64,128]{2,1,0:T(8,128)S(1)}) custom-call(f32[19,4,64,128]{3,2,1,0:T(8,128)S(1)} %get-tuple-element.24.own, f32[5,64,128]{2,1,0:T(8,128)S(1)} %collective-permute-done.far, f32[5,64,128]{2,1,0:T(8,128)S(1)} %collective-permute-done.1.near, ...), custom_call_target="tpu_custom_call" | custom-call | tf_op jit(solution)/shard_map/pallas_call | solution.py:307
  14.2 4.5 %collective-permute-start.2 = (f32[5,64,128]{2,1,0:T(8,128)S(1)}, f32[5,64,128]{2,1,0:T(8,128)S(1)}, u32[]{:S(2)}, u32[]{:S(2)}) collective-permute-start(f32[5,64,128]{2,1,0:T(8,128)S(1)} %get-tuple-element.29), channel_id=1, source_target_pairs={{0,15},{1,2},{2,1},{3,4},{4,3},{5,6},{6,5},{7,8},{8,7},{9,10},{10,... | collective-permute-start | bytes 491528 | tf_op jit(solution)/shard_map/ppermute | solution.py:327
  18.7 0.0 collective-permute-start.3
  18.7 0.2 collective-permute-start.6
  18.9 0.4 collective-permute-start.7
  19.2 2.5 %collective-permute-done.2.far = f32[5,64,128]{2,1,0:T(8,128)S(1)} collective-permute-done((f32[5,64,128]{2,1,0:T(8,128)S(1)}, f32[5,64,128]{2,1,0:T(8,128)S(1)}, u32[]{:S(2)}, u32[]{:S(2)}) %collective-permute-start.2) | collective-permute-done | bytes 163872 | tf_op jit(solution)/shard_map/ppermute | solution.py:327
  21.7 2.0 %shard_map.52 = (f32[19,4,64,128]{3,2,1,0:T(8,128)S(1)}, f32[3,4,64,128]{3,2,1,0:T(8,128)S(1)}, f32[5,64,128]{2,1,0:T(8,128)S(1)}, f32[5,64,128]{2,1,0:T(8,128)S(1)}) custom-call(f32[19,4,64,128]{3,2,1,0:T(8,128)S(1)} %get-tuple-element.28.own, f32[5,64,128]{2,1,0:T(8,128)S(1)} %collective-permute-done.2.far, f32[5,64,128]{2,1,0:T(8,128)S(1)} %collective-permute-done.3.near, ...), custom_call_target="tpu_custom_call" | custom-call | tf_op jit(solution)/shard_map/pallas_call | solution.py:307
  23.7 2.5 %collective-permute-done.6.far = f32[5,64,128]{2,1,0:T(8,128)S(1)} collective-permute-done((f32[5,64,128]{2,1,0:T(8,128)S(1)}, f32[5,64,128]{2,1,0:T(8,128)S(1)}, u32[]{:S(2)}, u32[]{:S(2)}) %collective-permute-start.6) | collective-permute-done | bytes 163872 | tf_op jit(solution)/shard_map/ppermute | solution.py:327
  26.2 0.0 collective-permute-done.7.near
  26.2 1.8 %shard_map.55 = (f32[19,4,64,128]{3,2,1,0:T(8,128)S(1)}, f32[5,64,128]{2,1,0:T(8,128)S(1)}, f32[5,64,128]{2,1,0:T(8,128)S(1)}) custom-call(f32[19,4,64,128]{3,2,1,0:T(8,128)S(1)} %get-tuple-element.34.own, f32[5,64,128]{2,1,0:T(8,128)S(1)} %collective-permute-done.6.far, f32[5,64,128]{2,1,0:T(8,128)S(1)} %collective-permute-done.7.near, ...), custom_call_target="tpu_custom_call" | custom-call | tf_op jit(solution)/shard_map/pallas_call | solution.py:307
  28.0 2.0 %collective-permute-start.8 = (f32[5,64,128]{2,1,0:T(8,128)S(1)}, f32[5,64,128]{2,1,0:T(8,128)S(1)}, u32[]{:S(2)}, u32[]{:S(2)}) collective-permute-start(f32[5,64,128]{2,1,0:T(8,128)S(1)} %get-tuple-element.39), channel_id=1, source_target_pairs={{0,15},{1,2},{2,1},{3,4},{4,3},{5,6},{6,5},{7,8},{8,7},{9,10},{10,... | collective-permute-start | bytes 491528 | tf_op jit(solution)/shard_map/ppermute | solution.py:327
  30.1 2.5 %collective-permute-start.4 = (f32[5,64,128]{2,1,0:T(8,128)S(1)}, f32[5,64,128]{2,1,0:T(8,128)S(1)}, u32[]{:S(2)}, u32[]{:S(2)}) collective-permute-start(f32[5,64,128]{2,1,0:T(8,128)S(1)} %get-tuple-element.32), channel_id=1, source_target_pairs={{0,15},{1,2},{2,1},{3,4},{4,3},{5,6},{6,5},{7,8},{8,7},{9,10},{10,... | collective-permute-start | bytes 491528 | tf_op jit(solution)/shard_map/ppermute | solution.py:327
  32.5 3.1 %collective-permute-done.8.far = f32[5,64,128]{2,1,0:T(8,128)S(1)} collective-permute-done((f32[5,64,128]{2,1,0:T(8,128)S(1)}, f32[5,64,128]{2,1,0:T(8,128)S(1)}, u32[]{:S(2)}, u32[]{:S(2)}) %collective-permute-start.8) | collective-permute-done | bytes 163872 | tf_op jit(solution)/shard_map/ppermute | solution.py:327
  35.6 1.8 %shard_map.56 = (f32[19,4,64,128]{3,2,1,0:T(8,128)S(1)}, f32[5,64,128]{2,1,0:T(8,128)S(1)}, f32[5,64,128]{2,1,0:T(8,128)S(1)}) custom-call(f32[19,4,64,128]{3,2,1,0:T(8,128)S(1)} %get-tuple-element.38.own, f32[5,64,128]{2,1,0:T(8,128)S(1)} %collective-permute-done.8.far, f32[5,64,128]{2,1,0:T(8,128)S(1)} %collective-permute-done.9.near, ...), custom_call_target="tpu_custom_call" | custom-call | tf_op jit(solution)/shard_map/pallas_call | solution.py:307
  37.5 2.1 %collective-permute-start.10 = (f32[5,64,128]{2,1,0:T(8,128)S(1)}, f32[5,64,128]{2,1,0:T(8,128)S(1)}, u32[]{:S(2)}, u32[]{:S(2)}) collective-permute-start(f32[5,64,128]{2,1,0:T(8,128)S(1)} %get-tuple-element.43), channel_id=1, source_target_pairs={{0,15},{1,2},{2,1},{3,4},{4,3},{5,6},{6,5},{7,8},{8,7},{9,10},{10,... | collective-permute-start | bytes 491528 | tf_op jit(solution)/shard_map/ppermute | solution.py:327
  39.5 2.2 %shard_map.53 = f32[19,256,128]{2,1,0:T(8,128)} custom-call(f32[19,4,64,128]{3,2,1,0:T(8,128)S(1)} %get-tuple-element.31.own, f32[5,64,128]{2,1,0:T(8,128)S(1)} %collective-permute-done.4.far, f32[5,64,128]{2,1,0:T(8,128)S(1)} %collective-permute-done.5.near), custom_call_target="tpu_custom_call" | custom-call | tf_op jit(solution)/shard_map/pallas_call | solution.py:307
  41.8 3.2 %collective-permute-done.10.far = f32[5,64,128]{2,1,0:T(8,128)S(1)} collective-permute-done((f32[5,64,128]{2,1,0:T(8,128)S(1)}, f32[5,64,128]{2,1,0:T(8,128)S(1)}, u32[]{:S(2)}, u32[]{:S(2)}) %collective-permute-start.10) | collective-permute-done | bytes 163872 | tf_op jit(solution)/shard_map/ppermute | solution.py:327
  45.0 2.6 %shard_map.57 = f32[19,256,128]{2,1,0:T(8,128)} custom-call(f32[19,4,64,128]{3,2,1,0:T(8,128)S(1)} %get-tuple-element.42.own, f32[5,64,128]{2,1,0:T(8,128)S(1)} %collective-permute-done.10.far, f32[5,64,128]{2,1,0:T(8,128)S(1)} %collective-permute-done.11.near, f32[4,64,128]{2,1,0:T(8,128)S(1)} %get-tuple-element.27.om_ref, ...), custom_call_target="tpu_custom_call" | custom-call | tf_op jit(solution)/shard_map/pallas_call | solution.py:307
  (12 shorter events, 0.0 us)
Async XLA Ops:
  0.6 8.6 %copy-start = (f32[19,4,8192]{2,1,0:T(4,128)S(1)}, f32[19,4,8192]{2,1,0:T(4,128)}, u32[]{:S(2)}) copy-start(f32[19,4,8192]{2,1,0:T(4,128)} %param.5) | copy-start | bytes 7471108
  0.6 1.1 %copy-start.1 = (s32[4,8192]{1,0:T(4,128)S(1)}, s32[4,8192]{1,0:T(4,128)}, u32[]{:S(2)}) copy-start(s32[4,8192]{1,0:T(4,128)} %param.4) | copy-start | bytes 393220
  3.8 8.5 %collective-permute-start = (f32[5,64,128]{2,1,0:T(8,128)S(1)}, f32[5,64,128]{2,1,0:T(8,128)S(1)}, u32[]{:S(2)}, u32[]{:S(2)}) collective-permute-start(f32[5,64,128]{2,1,0:T(8,128)S(1)} %get-tuple-element.25), channel_id=1, source_target_pairs={{0,15},{1,2},{2,1},{3,4},{4,3},{5,6},{6,5},{7,8},{8,7},{9,10},{10,... | collective-permute-start | bytes 491528 | tf_op jit(solution)/shard_map/ppermute | solution.py:327
  9.2 3.0 %collective-permute-start.1 = (f32[5,64,128]{2,1,0:T(8,128)S(1)}, f32[5,64,128]{2,1,0:T(8,128)S(1)}, u32[]{:S(2)}, u32[]{:S(2)}) collective-permute-start(f32[5,64,128]{2,1,0:T(8,128)S(1)} %get-tuple-element.26), channel_id=1, source_target_pairs={{0,1},{1,0},{2,3},{3,2},{4,5},{5,4},{6,7},{7,6},{8,9},{9,8},{10,11... | collective-permute-start | bytes 491528 | tf_op jit(solution)/shard_map/ppermute | solution.py:327
  14.2 7.5 %collective-permute-start.2 = (f32[5,64,128]{2,1,0:T(8,128)S(1)}, f32[5,64,128]{2,1,0:T(8,128)S(1)}, u32[]{:S(2)}, u32[]{:S(2)}) collective-permute-start(f32[5,64,128]{2,1,0:T(8,128)S(1)} %get-tuple-element.29), channel_id=1, source_target_pairs={{0,15},{1,2},{2,1},{3,4},{4,3},{5,6},{6,5},{7,8},{8,7},{9,10},{10,... | collective-permute-start | bytes 491528 | tf_op jit(solution)/shard_map/ppermute | solution.py:327
  18.7 3.0 %collective-permute-start.3 = (f32[5,64,128]{2,1,0:T(8,128)S(1)}, f32[5,64,128]{2,1,0:T(8,128)S(1)}, u32[]{:S(2)}, u32[]{:S(2)}) collective-permute-start(f32[5,64,128]{2,1,0:T(8,128)S(1)} %get-tuple-element.30), channel_id=1, source_target_pairs={{0,1},{1,0},{2,3},{3,2},{4,5},{5,4},{6,7},{7,6},{8,9},{9,8},{10,11... | collective-permute-start | bytes 491528 | tf_op jit(solution)/shard_map/ppermute | solution.py:327
  18.7 7.4 %collective-permute-start.6 = (f32[5,64,128]{2,1,0:T(8,128)S(1)}, f32[5,64,128]{2,1,0:T(8,128)S(1)}, u32[]{:S(2)}, u32[]{:S(2)}) collective-permute-start(f32[5,64,128]{2,1,0:T(8,128)S(1)} %get-tuple-element.35), channel_id=1, source_target_pairs={{0,15},{1,2},{2,1},{3,4},{4,3},{5,6},{6,5},{7,8},{8,7},{9,10},{10,... | collective-permute-start | bytes 491528 | tf_op jit(solution)/shard_map/ppermute | solution.py:327
  18.9 7.3 %collective-permute-start.7 = (f32[5,64,128]{2,1,0:T(8,128)S(1)}, f32[5,64,128]{2,1,0:T(8,128)S(1)}, u32[]{:S(2)}, u32[]{:S(2)}) collective-permute-start(f32[5,64,128]{2,1,0:T(8,128)S(1)} %get-tuple-element.36), channel_id=1, source_target_pairs={{0,1},{1,0},{2,3},{3,2},{4,5},{5,4},{6,7},{7,6},{8,9},{9,8},{10,11... | collective-permute-start | bytes 491528 | tf_op jit(solution)/shard_map/ppermute | solution.py:327
  28.0 7.6 %collective-permute-start.8 = (f32[5,64,128]{2,1,0:T(8,128)S(1)}, f32[5,64,128]{2,1,0:T(8,128)S(1)}, u32[]{:S(2)}, u32[]{:S(2)}) collective-permute-start(f32[5,64,128]{2,1,0:T(8,128)S(1)} %get-tuple-element.39), channel_id=1, source_target_pairs={{0,15},{1,2},{2,1},{3,4},{4,3},{5,6},{6,5},{7,8},{8,7},{9,10},{10,... | collective-permute-start | bytes 491528 | tf_op jit(solution)/shard_map/ppermute | solution.py:327
  30.1 5.6 %collective-permute-start.9 = (f32[5,64,128]{2,1,0:T(8,128)S(1)}, f32[5,64,128]{2,1,0:T(8,128)S(1)}, u32[]{:S(2)}, u32[]{:S(2)}) collective-permute-start(f32[5,64,128]{2,1,0:T(8,128)S(1)} %get-tuple-element.40), channel_id=1, source_target_pairs={{0,1},{1,0},{2,3},{3,2},{4,5},{5,4},{6,7},{7,6},{8,9},{9,8},{10,11... | collective-permute-start | bytes 491528 | tf_op jit(solution)/shard_map/ppermute | solution.py:327
  30.1 9.5 %collective-permute-start.4 = (f32[5,64,128]{2,1,0:T(8,128)S(1)}, f32[5,64,128]{2,1,0:T(8,128)S(1)}, u32[]{:S(2)}, u32[]{:S(2)}) collective-permute-start(f32[5,64,128]{2,1,0:T(8,128)S(1)} %get-tuple-element.32), channel_id=1, source_target_pairs={{0,15},{1,2},{2,1},{3,4},{4,3},{5,6},{6,5},{7,8},{8,7},{9,10},{10,... | collective-permute-start | bytes 491528 | tf_op jit(solution)/shard_map/ppermute | solution.py:327
  32.5 7.0 %collective-permute-start.5 = (f32[5,64,128]{2,1,0:T(8,128)S(1)}, f32[5,64,128]{2,1,0:T(8,128)S(1)}, u32[]{:S(2)}, u32[]{:S(2)}) collective-permute-start(f32[5,64,128]{2,1,0:T(8,128)S(1)} %get-tuple-element.33), channel_id=1, source_target_pairs={{0,1},{1,0},{2,3},{3,2},{4,5},{5,4},{6,7},{7,6},{8,9},{9,8},{10,11... | collective-permute-start | bytes 491528 | tf_op jit(solution)/shard_map/ppermute | solution.py:327
  37.5 7.5 %collective-permute-start.10 = (f32[5,64,128]{2,1,0:T(8,128)S(1)}, f32[5,64,128]{2,1,0:T(8,128)S(1)}, u32[]{:S(2)}, u32[]{:S(2)}) collective-permute-start(f32[5,64,128]{2,1,0:T(8,128)S(1)} %get-tuple-element.43), channel_id=1, source_target_pairs={{0,15},{1,2},{2,1},{3,4},{4,3},{5,6},{6,5},{7,8},{8,7},{9,10},{10,... | collective-permute-start | bytes 491528 | tf_op jit(solution)/shard_map/ppermute | solution.py:327
  39.5 5.5 %collective-permute-start.11 = (f32[5,64,128]{2,1,0:T(8,128)S(1)}, f32[5,64,128]{2,1,0:T(8,128)S(1)}, u32[]{:S(2)}, u32[]{:S(2)}) collective-permute-start(f32[5,64,128]{2,1,0:T(8,128)S(1)} %get-tuple-element.44), channel_id=1, source_target_pairs={{0,1},{1,0},{2,3},{3,2},{4,5},{5,4},{6,7},{7,6},{8,9},{9,8},{10,11... | collective-permute-start | bytes 491528 | tf_op jit(solution)/shard_map/ppermute | solution.py:327
where the time goes:
time: 47.7 us; the launch traced here: 47.5 us
  starting transfers between devices  17.1 us (36%)
  Pallas kernels  14.9 us (31%)
  waiting for transfers between devices  13.8 us (29%)
  local copies, waits for them, and re-layouts  1.05 us (2%)
  between operations  0.72 us (2%)
    ppermute x6, starting transfers between devices, exchange(): lax.ppermute(far, 'gx', far_pairs)  16.7 us
    pallas_call x8, Pallas kernels, call(): pl.pallas_call(body, in_specs=specs, out_specs=[INSIDE if inside else OUT...  14.9 us
    ppermute x6, waiting for transfers between devices, exchange(): lax.ppermute(far, 'gx', far_pairs)  13.8 us
    unnamed x4, local copies, waits for them, and re-layouts  1.05 us
  transfers between devices with their start and end apart: 12, of which 5 were waited for; matrix products, arithmetic and copies ran while one was open for 0% of the time, Pallas kernels for 14%

commit v1 on v0

v1 whole, which is shorter than its diff:
```python
import jax
import jax.numpy as jnp
from jax import lax
from jax.experimental import pallas as pl
from jax.experimental.pallas import tpu as pltpu
from jax.sharding import PartitionSpec as P

PLANES, ROWS, LANES, BLOCKS = 4, 64, 128, 8
SPEEDS = [
    (0, 0, 0), (1, 0, 0), (-1, 0, 0), (0, 1, 0), (0, -1, 0), (0, 0, 1), (0, 0, -1),
    (1, 1, 0), (-1, -1, 0), (1, -1, 0), (-1, 1, 0), (1, 0, 1), (-1, 0, -1),
    (1, 0, -1), (-1, 0, 1), (0, 1, 1), (0, -1, -1), (0, 1, -1), (0, -1, 1),
]
RATES = [1.0 / 1.0, 1.0 / 1.25, 1.0 / 1.6, 1.0 / 2.4]
MIRROR = [SPEEDS.index((-cx, cy, cz)) for cx, cy, cz in SPEEDS]
PLUS = [k for k in range(19) if SPEEDS[k][0] == 1]
MINUS = [MIRROR[k] for k in PLUS]
F32 = jnp.float32


def iotas():
    lane = lax.broadcasted_iota(jnp.int32, (8, LANES), 1)
    row = lax.broadcasted_iota(jnp.int32, (8, LANES), 0)
    return {"high": lane >= 64, "first": lane % 64 == 0, "last": lane % 64 == 63,
            "top": row == 0, "bottom": row == 7}


def block(r):
    return pl.ds(pl.multiple_of(r * 8, 8), 8)


def shifted(ref, index, r, cy, cz, m):
    here = ref[index + (block(r), slice(None))]
    turn = 0
    if cy == 1:
        edge = ref[index + (pl.ds(lax.rem(r + 7, 8) * 8 + 7, 1), slice(None))]
        other = jnp.where(m["top"], edge, pltpu.roll(here, 1, 0))
        here, turn = jnp.where(m["high"], other, here), 64
    elif cy == -1:
        edge = ref[index + (pl.ds(lax.rem(r + 1, 8) * 8, 1), slice(None))]
        other = jnp.where(m["bottom"], edge, pltpu.roll(here, 7, 0))
        here, turn = jnp.where(m["high"], here, other), 64
    if cz == 0:
        return pltpu.roll(here, turn, 1) if turn else here
    main = pltpu.roll(here, (turn + cz) % LANES, 1)
    wrapped = pltpu.roll(here, (turn + cz + 64) % LANES, 1)
    return jnp.where(m["first"] if cz == 1 else m["last"], wrapped, main)


def moments(f):
    s = [f[k] + f[k + 1] for k in range(1, 19, 2)]
    d = [f[k] - f[k + 1] for k in range(1, 19, 2)]
    rho = f[0] + ((s[0] + s[1]) + (s[2] + s[3])) + ((s[4] + s[5]) + (s[6] + s[7])) + s[8]
    jx = d[0] + ((d[3] + d[4]) + (d[5] + d[6]))
    jy = d[1] + ((d[3] - d[4]) + (d[7] + d[8]))
    jz = d[2] + ((d[5] - d[6]) + (d[7] - d[8]))
    return rho, jx, jy, jz


def along_odd(k, v):
    total = None
    for c, x in zip(SPEEDS[k], v):
        if c:
            total = x if total is None else (total + x if c == 1 else total - x)
    return total


def relaxed(f, rho, u, om):
    keep = 1.0 - om
    wr = om * rho
    shape = 1.0 - 1.5 * (u[0] * u[0] + u[1] * u[1] + u[2] * u[2])
    out = [None] * 19
    out[0] = keep * f[0] + (wr * (1.0 / 3.0)) * shape
    for first, last, w in ((1, 7, 1.0 / 18.0), (7, 19, 1.0 / 36.0)):
        part = wr * w
        base, lin, quad = part * shape, part * 3.0, part * 4.5
        for k in range(first, last, 2):
            a = along_odd(k, u)
            even, odd = base + quad * (a * a), lin * a
            out[k] = keep * f[k] + (even + odd)
            out[k + 1] = keep * f[k + 1] + (even - odd)
    return out


def adjoint(mu, u, om):
    s = [None] + [mu[k] + mu[k + 1] for k in range(1, 19, 2)]
    d = [None] + [mu[k] - mu[k + 1] for k in range(1, 19, 2)]
    a, b = 1.0 / 18.0, 1.0 / 36.0
    s45, s67, s89 = s[4] + s[5], s[6] + s[7], s[8] + s[9]
    xx = a * s[1] + b * (s45 + s67)
    yy = a * s[2] + b * (s45 + s89)
    zz = a * s[3] + b * (s67 + s89)
    m0 = (1.0 / 3.0) * mu[0] + a * ((s[1] + s[2]) + s[3]) + b * ((s45 + s67) + s89)
    xy, xz, yz = b * (s[4] - s[5]), b * (s[6] - s[7]), b * (s[8] - s[9])
    mx = a * d[1] + b * ((d[4] + d[5]) + (d[6] + d[7]))
    my = a * d[2] + b * ((d[4] - d[5]) + (d[8] + d[9]))
    mz = a * d[3] + b * ((d[6] - d[7]) + (d[8] - d[9]))
    vx = xx * u[0] + xy * u[1] + xz * u[2]
    vy = xy * u[0] + yy * u[1] + yz * u[2]
    vz = xz * u[0] + yz * u[1] + zz * u[2]
    uu = u[0] * u[0] + u[1] * u[1] + u[2] * u[2]
    rho_part = om * (m0 + 1.5 * (m0 * uu) - 4.5 * (u[0] * vx + u[1] * vy + u[2] * vz))
    om3 = 3.0 * om
    flow = [
        om3 * (mx + 3.0 * vx - u[0] * m0),
        om3 * (my + 3.0 * vy - u[1] * m0),
        om3 * (mz + 3.0 * vz - u[2] * m0),
    ]
    keep = 1.0 - om
    out = [None] * 19
    out[0] = keep * mu[0] + rho_part
    for k in range(1, 19, 2):
        g = along_odd(k, flow)
        out[k] = keep * mu[k] + (rho_part + g)
        out[k + 1] = keep * mu[k + 1] + (rho_part - g)
    return out


EDGES, INNER = (0, PLANES - 1), (1, 2)


def plane_of(edge, inner, p):
    return (edge, EDGES.index(p)) if p in EDGES else (inner, INNER.index(p))


def pull_local(edge, inner, p, r, sign, m):
    out = [None] * 19
    for k in range(19):
        cx, cy, cz = (sign * c for c in SPEEDS[k])
        if 0 <= p - cx < PLANES:
            ref, i = plane_of(edge, inner, p - cx)
            out[k] = shifted(ref, (k, i), r, cy, cz, m)
    return out


def crossing(p, sign):
    return (PLUS, MINUS)[(sign == 1) != (p == 0)]


def pull_remote(other, out, p, r, sign, m):
    for i, k in enumerate(crossing(p, sign)):
        out[k] = shifted(other, (i,), r, sign * SPEEDS[k][1], sign * SPEEDS[k][2], m)
    return out


def put_all(ref, values, i, r):
    for k in range(19):
        if values[k] is not None:
            ref[k, i, block(r), :] = values[k]


def get_some(ref, i, r, missing=()):
    return [None if k in missing else ref[k, i, block(r), :] for k in range(19)]


def put_crossing(far_ref, near_ref, values, p, r, sign):
    ref = far_ref if p == 0 else near_ref
    for i, k in enumerate(crossing(p, -sign)):
        ref[i, block(r), :] = values[k]


def put_velocity(u_ref, u, i, r):
    for j in range(3):
        u_ref[j, i, block(r), :] = u[j]


def get_velocity(u_ref, i, r):
    return [u_ref[j, i, block(r), :] for j in range(3)]


def state_of(f):
    rho, jx, jy, jz = moments(f)
    inv = 1.0 / rho
    return rho, [jx * inv, jy * inv, jz * inv]


def native(flip, k, p, r):
    kk = k if MIRROR[k] == k else jnp.where(flip == 1, MIRROR[k], k)
    x = jnp.where(flip == 1, PLANES - 1 - p, p)
    return kk, pl.ds(r * (8 * PLANES) + x, 8, stride=PLANES)


def get_native(ref, flip, p, r):
    out = []
    for k in range(19):
        kk, rows = native(flip, k, p, r)
        out.append(ref[kk, rows, :])
    return out


def put_native(ref, values, flip, p, r):
    for k in range(19):
        kk, rows = native(flip, k, p, r)
        ref[kk, rows, :] = values[k]


def loop(body):
    lax.fori_loop(0, BLOCKS, lambda r, c: (body(r), c)[1], 0)


def chunk(ref, r):
    rows = 8 * PLANES
    return ref.at[:, pl.ds(pl.multiple_of(r * rows, rows), rows), :]


def moved(source, target, sem, r):
    return pltpu.make_async_copy(chunk(source, r), chunk(target, r), sem.at[r])


def flipped():
    return lax.rem(lax.axis_index("gx"), 2)


def first_edges(pops, classes, held, om_ref, post, u_ref, far_out, near_out, cls_ref, sem, cls_sem):
    flip = flipped()
    fetch = pltpu.make_async_copy(classes, cls_ref, cls_sem)
    fetch.start()
    loop(lambda r: moved(pops, held, sem, r).start())
    fetch.wait()

    def body(r):
        moved(pops, held, sem, r).wait()
        for p in range(PLANES):
            cls = cls_ref[native(flip, 0, p, r)[1], :]
            om = jnp.full((8, LANES), RATES[0], F32)
            for entry in range(1, 4):
                om = jnp.where(cls == entry, RATES[entry], om)
            om_ref[p, block(r), :] = om
            if p in EDGES:
                i = EDGES.index(p)
                f = get_native(held, flip, p, r)
                rho, u = state_of(f)
                put_velocity(u_ref, u, i, r)
                out = relaxed(f, rho, u, om)
                put_all(post, out, i, r)
                put_crossing(far_out, near_out, out, p, r, 1)

    loop(body)


def first_inner(held, om_ref, post, u_ref):
    flip = flipped()

    def body(r):
        for i, p in enumerate(INNER):
            f = get_native(held, flip, p, r)
            rho, u = state_of(f)
            put_velocity(u_ref, u, i, r)
            put_all(post, relaxed(f, rho, u, om_ref[p, block(r), :]), i, r)

    loop(body)


def cotangent_planes(cot, edge, inner, far_out, near_out):
    flip = flipped()

    def body(r):
        for p in range(PLANES):
            values = get_native(cot, flip, p, r)
            ref, i = plane_of(edge, inner, p)
            put_all(ref, values, i, r)
            if p in EDGES:
                put_crossing(far_out, near_out, values, p, r, -1)

    loop(body)


def forward_inner(edge, inner, om_ref, post, u_ref, ready):
    m = iotas()

    def body(r):
        for i, p in enumerate(INNER):
            f = pull_local(edge, inner, p, r, 1, m)
            rho, u = state_of(f)
            put_velocity(u_ref, u, i, r)
            put_all(post, relaxed(f, rho, u, om_ref[p, block(r), :]), i, r)
        for i, p in enumerate(EDGES):
            put_all(ready, pull_local(edge, inner, p, r, 1, m), i, r)

    loop(body)


def edge_values(ready, far, near, i, p, r, sign, m):
    values = get_some(ready, i, r, crossing(p, sign))
    return pull_remote(far if p == 0 else near, values, p, r, sign, m)


def forward_edges(ready, far, near, om_ref, post, u_ref, far_out, near_out):
    m = iotas()

    def body(r):
        for i, p in enumerate(EDGES):
            f = edge_values(ready, far, near, i, p, r, 1, m)
            rho, u = state_of(f)
            put_velocity(u_ref, u, i, r)
            out = relaxed(f, rho, u, om_ref[p, block(r), :])
            put_all(post, out, i, r)
            put_crossing(far_out, near_out, out, p, r, 1)

    loop(body)


def adjoint_inner(edge, inner, om_ref, u_ref, lam, ready):
    m = iotas()

    def body(r):
        for i, p in enumerate(INNER):
            mu = pull_local(edge, inner, p, r, -1, m)
            put_all(lam, adjoint(mu, get_velocity(u_ref, i, r), om_ref[p, block(r), :]), i, r)
        for i, p in enumerate(EDGES):
            put_all(ready, pull_local(edge, inner, p, r, -1, m), i, r)

    loop(body)


def adjoint_edges(ready, far, near, om_ref, u_ref, lam, far_out, near_out):
    m = iotas()

    def body(r):
        for i, p in enumerate(EDGES):
            mu = edge_values(ready, far, near, i, p, r, -1, m)
            out = adjoint(mu, get_velocity(u_ref, i, r), om_ref[p, block(r), :])
            put_all(lam, out, i, r)
            put_crossing(far_out, near_out, out, p, r, -1)

    loop(body)


def turn_edges(ready, far, near, om_ref, mus, farc, nearc, post, lam, far_post, near_post, far_out, near_out):
    m = iotas()

    def body(r):
        for i, p in enumerate(EDGES):
            om = om_ref[p, block(r), :]
            f = edge_values(ready, far, near, i, p, r, 1, m)
            rho, u = state_of(f)
            out = relaxed(f, rho, u, om)
            put_all(post, out, i, r)
            put_crossing(far_post, near_post, out, p, r, 1)
            out = adjoint(edge_values(mus, farc, nearc, i, p, r, -1, m), u, om)
            put_all(lam, out, i, r)
            put_crossing(far_out, near_out, out, p, r, -1)

    loop(body)


def stream_last(edge, inner, far, near, final, hold, sem):
    flip, m = flipped(), iotas()

    def body(r):
        for p in range(PLANES):
            f = pull_local(edge, inner, p, r, 1, m)
            if p in EDGES:
                pull_remote(far if p == 0 else near, f, p, r, 1, m)
            put_native(hold, f, flip, p, r)
        moved(hold, final, sem, r).start()

    loop(body)
    loop(lambda r: moved(hold, final, sem, r).wait())


def adjoint_last(ready, far, near, om_ref, u_ref, inner, grad, hold, sem):
    flip, m = flipped(), iotas()

    def body(r):
        for i, p in enumerate(EDGES):
            mu = edge_values(ready, far, near, i, p, r, -1, m)
            out = adjoint(mu, get_velocity(u_ref, i, r), om_ref[p, block(r), :])
            put_native(hold, out, flip, p, r)
        for i, p in enumerate(INNER):
            put_native(hold, get_some(inner, i, r), flip, p, r)
        moved(hold, grad, sem, r).start()

    loop(body)
    loop(lambda r: moved(hold, grad, sem, r).wait())


INSIDE = pl.BlockSpec(memory_space=pltpu.VMEM)
OUTSIDE = pl.BlockSpec(memory_space=pltpu.HBM)
PAIR = (19, 2, ROWS, LANES)
VELOCITY = (3, 2, ROWS, LANES)
RELAX = (PLANES, ROWS, LANES)
CROSS = (5, ROWS, LANES)
NATIVE = (19, PLANES * ROWS, LANES)
SEMS = pltpu.SemaphoreType.DMA((BLOCKS,))
STAGED = [pltpu.VMEM(NATIVE, F32), SEMS]


def kernel(body, outs, scratch=()):
    def call(*args):
        args = [x if isinstance(x, tuple) else (x, 1) for x in args]
        return pl.pallas_call(
            body,
            in_specs=[INSIDE if inside else OUTSIDE for _, inside in args],
            out_specs=[INSIDE if inside else OUTSIDE for _, inside in outs],
            out_shape=[
                pltpu.VMEM(s, F32) if inside else jax.ShapeDtypeStruct(s, F32) for s, inside in outs
            ],
            scratch_shapes=list(scratch),
            compiler_params=pltpu.CompilerParams(vmem_limit_bytes=8 * 2**20),
            name=body.__name__,
        )(
            *[
                pltpu.with_memory_space_constraint(x, pltpu.VMEM if inside else pltpu.HBM)
                for x, inside in args
            ]
        )

    return call


def local(populations, relax_class, cotangent):
    count = lax.axis_size("gx")
    near_pairs = [(i, i ^ 1) for i in range(count)]
    far_pairs = [(i, (i + 1 if i % 2 else i - 1) % count) for i in range(count)]

    def exchange(far, near):
        near = lax.ppermute(near, "gx", near_pairs)
        return lax.ppermute(far, "gx", far_pairs), near

    def to_native(x):
        lead = x.shape[:-2]
        x = x.reshape(lead + (PLANES, ROWS, LANES))
        return jnp.swapaxes(x, -3, -2).reshape(lead + (PLANES * ROWS, LANES))

    def from_native(x):
        return jnp.swapaxes(x.reshape(19, ROWS, PLANES, LANES), 1, 2).reshape(populations.shape)

    pops, classes, cot = to_native(populations), to_native(relax_class), to_native(cotangent)
    pair, speed, cross = (PAIR, 1), (VELOCITY, 1), (CROSS, 1)
    held, om, post_e, u0_e, far, near = kernel(
        first_edges,
        [(NATIVE, 1), (RELAX, 1), pair, speed, cross, cross],
        [pltpu.VMEM(classes.shape, jnp.int32), SEMS, pltpu.SemaphoreType.DMA],
    )((pops, 0), (classes, 0))
    far, near = exchange(far, near)
    post_i, u0_i = kernel(first_inner, [pair, speed])(held, om)
    cot_e, cot_i, farc, nearc = kernel(cotangent_planes, [pair, pair, cross, cross])(cot)
    farc, nearc = exchange(farc, nearc)
    inner = kernel(forward_inner, [pair, speed, pair])
    back_inner = kernel(adjoint_inner, [pair, pair])
    back_edges = kernel(adjoint_edges, [pair, cross, cross])

    post_i, u1_i, ready = inner(post_e, post_i, om)
    post_e, u1_e, far, near = kernel(forward_edges, [pair, speed, cross, cross])(ready, far, near, om)
    far, near = exchange(far, near)
    post_i, u2_i, ready = inner(post_e, post_i, om)
    lam_i, mus = back_inner(cot_e, cot_i, om, u2_i)
    post_e, lam_e, far_post, near_post, far, near = kernel(
        turn_edges, [pair, pair, cross, cross, cross, cross]
    )(ready, far, near, om, mus, farc, nearc)
    far, near = exchange(far, near)
    far_post, near_post = exchange(far_post, near_post)
    lam_i, ready = back_inner(lam_e, lam_i, om, u1_i)
    lam_e, far, near = back_edges(ready, far, near, om, u1_e)
    far, near = exchange(far, near)
    (final,) = kernel(stream_last, [(NATIVE, 0)], STAGED)(post_e, post_i, far_post, near_post)
    lam_i, ready = back_inner(lam_e, lam_i, om, u0_i)
    (grad,) = kernel(adjoint_last, [(NATIVE, 0)], STAGED)(ready, far, near, om, u0_e, lam_i)
    return from_native(final), from_native(grad)


def solution(mesh):
    return jax.shard_map(
        local,
        mesh=mesh,
        in_specs=(
            P(None, ("groups", "gx"), None),
            P(("groups", "gx"), None),
            P(None, ("groups", "gx"), None),
        ),
        out_specs=(P(None, ("groups", "gx"), None), P(None, ("groups", "gx"), None)),
        check_vma=False,
    )
```

time: 47.7 us -> 40.2 us (0.84)
  waiting for transfers between devices: 13.8 us -> 1.8 us
  Pallas kernels: 14.9 us -> 17.7 us
  starting transfers between devices: 17.1 us -> 19.7 us
  local copies, waits for them, and re-layouts: 1.05 us -> 0.01 us
    ppermute x12, waiting for transfers between devices: 13.8 us -> 1.8 us  [the longest x6 1.79 us: exchange(): return (lax.ppermute(far, 'gx', far_pairs), near)]
    pallas_call x8 -> x13, Pallas kernels: 14.9 us -> 17.7 us  [call(): pl.pallas_call(body, in_specs=[INSIDE if inside else OUTSIDE for _, insid...]
    ppermute x12, starting transfers between devices: 17.1 us -> 19.7 us  [the longest x6 19.4 us: exchange(): return (lax.ppermute(far, 'gx', far_pairs), near)]
    unnamed x4 -> x2, local copies, waits for them, and re-layouts: 1.05 us -> 0.01 us
  transfers between devices with their start and end apart: 12 -> 12, of which waited for: 5 -> 2; matrix products, arithmetic and copies ran while one was open for 0% -> 0% of each run, Pallas kernels for 14% -> 31%
where the time goes in v1:
time: 40.2 us; the launch traced here: 40 us
  starting transfers between devices  19.7 us (49%)
  Pallas kernels  17.7 us (44%)
  waiting for transfers between devices  1.8 us (4%)
  between operations  0.8 us (2%)
    ppermute x6, starting transfers between devices, exchange(): return (lax.ppermute(far, 'gx', far_pairs), near)  19.4 us
    pallas_call x13, Pallas kernels, call(): pl.pallas_call(body, in_specs=[INSIDE if inside else OUTSIDE for _, insid...  17.7 us
    ppermute x6, waiting for transfers between devices, exchange(): return (lax.ppermute(far, 'gx', far_pairs), near)  1.79 us
  transfers between devices with their start and end apart: 12, of which 2 were waited for; matrix products, arithmetic and copies ran while one was open for 0% of the time, Pallas kernels for 31%

profile of v1, /device:TPU:0, one launch (start us, length us, event | category | flops | bytes accessed | tf_op | source)
XLA Modules:
  0.0 40.0 jit_solution(8647857056272695404)
XLA Ops:
  0.6 2.0 %first_edges.1 = (f32[19,256,128]{2,1,0:T(8,128)S(1)}, f32[4,64,128]{2,1,0:T(8,128)S(1)}, f32[19,2,64,128]{3,2,1,0:T(8,128)S(1)}, f32[3,2,64,128]{3,2,1,0:T(8,12...) custom-call(f32[19,256,128]{2,1,0:T(8,128)} %bitcast.26, s32[256,128]{1,0:T(8,128)} %bitcast.29), custom_call_target="tpu_custom_call" | custom-call | tf_op jit(solution)/shard_map/first_edges/pallas_call | solution.py:392
  2.6 5.5 %collective-permute-start = (f32[5,64,128]{2,1,0:T(8,128)S(1)}, f32[5,64,128]{2,1,0:T(8,128)S(1)}, u32[]{:S(2)}, u32[]{:S(2)}) collective-permute-start(f32[5,64,128]{2,1,0:T(8,128)S(1)} %get-tuple-element.44), channel_id=1, source_target_pairs={{0,15},{1,2},{2,1},{3,4},{4,3},{5,6},{6,5},{7,8},{8,7},{9,10},{10,... | collective-permute-start | bytes 491528 | tf_op jit(solution)/shard_map/ppermute | solution.py:419
  8.1 0.5 %cotangent_planes.1 = (f32[19,2,64,128]{3,2,1,0:T(8,128)S(1)}, f32[19,2,64,128]{3,2,1,0:T(8,128)S(1)}, f32[5,64,128]{2,1,0:T(8,128)S(1)}, f32[5,64,128]{2,1,0:T(8,128)S(1)}) custom-call(f32[19,256,128]{2,1,0:T(8,128)S(1)} %bitcast.25), custom_call_target="tpu_custom_call" | custom-call | tf_op jit(solution)/shard_map/cotangent_planes/pallas_call | solution.py:392
  8.6 0.8 %collective-permute-start.4 = (f32[5,64,128]{2,1,0:T(8,128)S(1)}, f32[5,64,128]{2,1,0:T(8,128)S(1)}, u32[]{:S(2)}, u32[]{:S(2)}) collective-permute-start(f32[5,64,128]{2,1,0:T(8,128)S(1)} %get-tuple-element.55), channel_id=1, source_target_pairs={{0,15},{1,2},{2,1},{3,4},{4,3},{5,6},{6,5},{7,8},{8,7},{9,10},{10,... | collective-permute-start | bytes 491528 | tf_op jit(solution)/shard_map/ppermute | solution.py:419
  9.4 0.0 collective-permute-start.5
  9.4 0.5 %first_inner.1 = (f32[19,2,64,128]{3,2,1,0:T(8,128)S(1)}, f32[3,2,64,128]{3,2,1,0:T(8,128)S(1)}) custom-call(f32[19,256,128]{2,1,0:T(8,128)S(1)} %get-tuple-element.40.held, f32[4,64,128]{2,1,0:T(8,128)S(1)} %get-tuple-element.41.om_ref), custom_call_target="tpu_custom_call" | custom-call | tf_op jit(solution)/shard_map/first_inner/pallas_call | solution.py:392
  10.0 1.4 %forward_inner.2 = (f32[19,2,64,128]{3,2,1,0:T(8,128)S(1)}, f32[3,2,64,128]{3,2,1,0:T(8,128)S(1)}, f32[19,2,64,128]{3,2,1,0:T(8,128)S(1)}) custom-call(f32[19,2,64,128]{3,2,1,0:T(8,128)S(1)} %get-tuple-element.39.edge, f32[19,2,64,128]{3,2,1,0:T(8,128)S(1)} %get-tuple-element.42.inner, f32[4,64,128]{2,1,0:T(8,128)S(1)} %get-tuple-element.41.om_ref), custom_call_target="tpu_custom_call" | custom-call | tf_op jit(solution)/shard_map/forward_inner/pallas_call | solution.py:392
  11.4 1.0 %forward_edges.1 = (f32[19,2,64,128]{3,2,1,0:T(8,128)S(1)}, f32[3,2,64,128]{3,2,1,0:T(8,128)S(1)}, f32[5,64,128]{2,1,0:T(8,128)S(1)}, f32[5,64,128]{2,1,0:T(8,128)S(1)}) custom-call(f32[19,2,64,128]{3,2,1,0:T(8,128)S(1)} %get-tuple-element.43.ready, f32[5,64,128]{2,1,0:T(8,128)S(1)} %collective-permute-done.far, ...), custom_call_target="tpu_custom_call" | custom-call | tf_op jit(solution)/shard_map/forward_edges/pallas_call | solution.py:392
  12.4 4.4 %collective-permute-start.2 = (f32[5,64,128]{2,1,0:T(8,128)S(1)}, f32[5,64,128]{2,1,0:T(8,128)S(1)}, u32[]{:S(2)}, u32[]{:S(2)}) collective-permute-start(f32[5,64,128]{2,1,0:T(8,128)S(1)} %get-tuple-element.49), channel_id=1, source_target_pairs={{0,15},{1,2},{2,1},{3,4},{4,3},{5,6},{6,5},{7,8},{8,7},{9,10},{10,... | collective-permute-start | bytes 491528 | tf_op jit(solution)/shard_map/ppermute | solution.py:419
  16.8 0.0 collective-permute-start.3
  16.8 1.4 %forward_inner.3 = (f32[19,2,64,128]{3,2,1,0:T(8,128)S(1)}, f32[3,2,64,128]{3,2,1,0:T(8,128)S(1)}, f32[19,2,64,128]{3,2,1,0:T(8,128)S(1)}) custom-call(f32[19,2,64,128]{3,2,1,0:T(8,128)S(1)} %get-tuple-element.46.edge, f32[19,2,64,128]{3,2,1,0:T(8,128)S(1)} %get-tuple-element.47.inner, f32[4,64,128]{2,1,0:T(8,128)S(1)} %get-tuple-element.41.om_ref), custom_call_target="tpu_custom_call" | custom-call | tf_op jit(solution)/shard_map/forward_inner/pallas_call | solution.py:392
  18.2 1.4 %adjoint_inner.3 = (f32[19,2,64,128]{3,2,1,0:T(8,128)S(1)}, f32[19,2,64,128]{3,2,1,0:T(8,128)S(1)}) custom-call(f32[19,2,64,128]{3,2,1,0:T(8,128)S(1)} %get-tuple-element.51.edge, f32[19,2,64,128]{3,2,1,0:T(8,128)S(1)} %get-tuple-element.52.inner, f32[4,64,128]{2,1,0:T(8,128)S(1)} %get-tuple-element.41.om_ref, f32[3,2,64,128]{3,2,1,0:T(8,128)S(1)} %get-tuple-element.53.u_ref), custom_call_target="tpu_custom_call" | custom-call | tf_op jit(solution)/shard_map/adjoint_inner/pallas_call | solution.py:392
  19.6 0.4 %collective-permute-done.2.far = f32[5,64,128]{2,1,0:T(8,128)S(1)} collective-permute-done((f32[5,64,128]{2,1,0:T(8,128)S(1)}, f32[5,64,128]{2,1,0:T(8,128)S(1)}, u32[]{:S(2)}, u32[]{:S(2)}) %collective-permute-start.2) | collective-permute-done | bytes 163872 | tf_op jit(solution)/shard_map/ppermute | solution.py:419
  20.0 1.4 %turn_edges.1 = (f32[19,2,64,128]{3,2,1,0:T(8,128)S(1)}, f32[19,2,64,128]{3,2,1,0:T(8,128)S(1)}, f32[5,64,128]{2,1,0:T(8,128)S(1)}, f32[5,64,128]{2,1,0:T(8,128)...) custom-call(f32[19,2,64,128]{3,2,1,0:T(8,128)S(1)} %get-tuple-element.48.ready, ...), custom_call_target="tpu_custom_call" | custom-call | tf_op jit(solution)/shard_map/turn_edges/pallas_call | solution.py:392
  21.5 4.2 %collective-permute-start.8 = (f32[5,64,128]{2,1,0:T(8,128)S(1)}, f32[5,64,128]{2,1,0:T(8,128)S(1)}, u32[]{:S(2)}, u32[]{:S(2)}) collective-permute-start(f32[5,64,128]{2,1,0:T(8,128)S(1)} %get-tuple-element.65), channel_id=1, source_target_pairs={{0,15},{1,2},{2,1},{3,4},{4,3},{5,6},{6,5},{7,8},{8,7},{9,10},{10,... | collective-permute-start | bytes 491528 | tf_op jit(solution)/shard_map/ppermute | solution.py:419
  25.7 0.3 collective-permute-start.6
  26.0 0.2 collective-permute-start.7
  26.2 1.4 %adjoint_inner.4 = (f32[19,2,64,128]{3,2,1,0:T(8,128)S(1)}, f32[19,2,64,128]{3,2,1,0:T(8,128)S(1)}) custom-call(f32[19,2,64,128]{3,2,1,0:T(8,128)S(1)} %get-tuple-element.61.edge, f32[19,2,64,128]{3,2,1,0:T(8,128)S(1)} %get-tuple-element.62.inner, f32[4,64,128]{2,1,0:T(8,128)S(1)} %get-tuple-element.41.om_ref, f32[3,2,64,128]{3,2,1,0:T(8,128)S(1)} %get-tuple-element.63.u_ref), custom_call_target="tpu_custom_call" | custom-call | tf_op jit(solution)/shard_map/adjoint_inner/pallas_call | solution.py:392
  27.6 1.3 %collective-permute-done.8.far = f32[5,64,128]{2,1,0:T(8,128)S(1)} collective-permute-done((f32[5,64,128]{2,1,0:T(8,128)S(1)}, f32[5,64,128]{2,1,0:T(8,128)S(1)}, u32[]{:S(2)}, u32[]{:S(2)}) %collective-permute-start.8) | collective-permute-done | bytes 163872 | tf_op jit(solution)/shard_map/ppermute | solution.py:419
  29.0 1.0 %adjoint_edges.1 = (f32[19,2,64,128]{3,2,1,0:T(8,128)S(1)}, f32[5,64,128]{2,1,0:T(8,128)S(1)}, f32[5,64,128]{2,1,0:T(8,128)S(1)}) custom-call(f32[19,2,64,128]{3,2,1,0:T(8,128)S(1)} %get-tuple-element.64.ready, f32[5,64,128]{2,1,0:T(8,128)S(1)} %collective-permute-done.8.far, f32[5,64,128]{2,1,0:T(8,128)S(1)} %collective-permute-done.9.near, ...), custom_call_target="tpu_custom_call" | custom-call | tf_op jit(solution)/shard_map/adjoint_edges/pallas_call | solution.py:392
  30.0 4.2 %collective-permute-start.10 = (f32[5,64,128]{2,1,0:T(8,128)S(1)}, f32[5,64,128]{2,1,0:T(8,128)S(1)}, u32[]{:S(2)}, u32[]{:S(2)}) collective-permute-start(f32[5,64,128]{2,1,0:T(8,128)S(1)} %get-tuple-element.72), channel_id=1, source_target_pairs={{0,15},{1,2},{2,1},{3,4},{4,3},{5,6},{6,5},{7,8},{8,7},{9,10},{10,... | collective-permute-start | bytes 491528 | tf_op jit(solution)/shard_map/ppermute | solution.py:419
  34.2 1.4 %adjoint_inner.5 = (f32[19,2,64,128]{3,2,1,0:T(8,128)S(1)}, f32[19,2,64,128]{3,2,1,0:T(8,128)S(1)}) custom-call(f32[19,2,64,128]{3,2,1,0:T(8,128)S(1)} %get-tuple-element.68.edge, f32[19,2,64,128]{3,2,1,0:T(8,128)S(1)} %get-tuple-element.69.inner, f32[4,64,128]{2,1,0:T(8,128)S(1)} %get-tuple-element.41.om_ref, f32[3,2,64,128]{3,2,1,0:T(8,128)S(1)} %get-tuple-element.70.u_ref), custom_call_target="tpu_custom_call" | custom-call | tf_op jit(solution)/shard_map/adjoint_inner/pallas_call | solution.py:392
  35.6 2.3 %stream_last.1 = f32[19,256,128]{2,1,0:T(8,128)} custom-call(f32[19,2,64,128]{3,2,1,0:T(8,128)S(1)} %get-tuple-element.57.edge, f32[19,2,64,128]{3,2,1,0:T(8,128)S(1)} %get-tuple-element.58.inner, f32[5,64,128]{2,1,0:T(8,128)S(1)} %collective-permute-done.6.far, f32[5,64,128]{2,1,0:T(8,128)S(1)} %collective-permute-done.7.near), custom_call_target="tpu_custom_call" | custom-call | tf_op jit(solution)/shard_map/stream_last/pallas_call | solution.py:392
  38.0 2.0 %adjoint_last.1 = f32[19,256,128]{2,1,0:T(8,128)} custom-call(f32[19,2,64,128]{3,2,1,0:T(8,128)S(1)} %get-tuple-element.71.ready, f32[5,64,128]{2,1,0:T(8,128)S(1)} %collective-permute-done.10.far, f32[5,64,128]{2,1,0:T(8,128)S(1)} %collective-permute-done.11.near, f32[4,64,128]{2,1,0:T(8,128)S(1)} %get-tuple-element.41.om_ref, ...), custom_call_target="tpu_custom_call" | custom-call | tf_op jit(solution)/shard_map/adjoint_last/pallas_call | solution.py:392
  (15 shorter events, 0.0 us)
Async XLA Ops:
  0.6 7.5 %copy-start = (f32[19,4,8192]{2,1,0:T(4,128)S(1)}, f32[19,4,8192]{2,1,0:T(4,128)}, u32[]{:S(2)}) copy-start(f32[19,4,8192]{2,1,0:T(4,128)} %param.5) | copy-start | bytes 7471108
  2.6 8.7 %collective-permute-start = (f32[5,64,128]{2,1,0:T(8,128)S(1)}, f32[5,64,128]{2,1,0:T(8,128)S(1)}, u32[]{:S(2)}, u32[]{:S(2)}) collective-permute-start(f32[5,64,128]{2,1,0:T(8,128)S(1)} %get-tuple-element.44), channel_id=1, source_target_pairs={{0,15},{1,2},{2,1},{3,4},{4,3},{5,6},{6,5},{7,8},{8,7},{9,10},{10,... | collective-permute-start | bytes 491528 | tf_op jit(solution)/shard_map/ppermute | solution.py:419
  8.1 3.3 %collective-permute-start.1 = (f32[5,64,128]{2,1,0:T(8,128)S(1)}, f32[5,64,128]{2,1,0:T(8,128)S(1)}, u32[]{:S(2)}, u32[]{:S(2)}) collective-permute-start(f32[5,64,128]{2,1,0:T(8,128)S(1)} %get-tuple-element.45), channel_id=1, source_target_pairs={{0,1},{1,0},{2,3},{3,2},{4,5},{5,4},{6,7},{7,6},{8,9},{9,8},{10,11... | collective-permute-start | bytes 491528 | tf_op jit(solution)/shard_map/ppermute | solution.py:418
  8.6 11.0 %collective-permute-start.4 = (f32[5,64,128]{2,1,0:T(8,128)S(1)}, f32[5,64,128]{2,1,0:T(8,128)S(1)}, u32[]{:S(2)}, u32[]{:S(2)}) collective-permute-start(f32[5,64,128]{2,1,0:T(8,128)S(1)} %get-tuple-element.55), channel_id=1, source_target_pairs={{0,15},{1,2},{2,1},{3,4},{4,3},{5,6},{6,5},{7,8},{8,7},{9,10},{10,... | collective-permute-start | bytes 491528 | tf_op jit(solution)/shard_map/ppermute | solution.py:419
  9.4 10.2 %collective-permute-start.5 = (f32[5,64,128]{2,1,0:T(8,128)S(1)}, f32[5,64,128]{2,1,0:T(8,128)S(1)}, u32[]{:S(2)}, u32[]{:S(2)}) collective-permute-start(f32[5,64,128]{2,1,0:T(8,128)S(1)} %get-tuple-element.56), channel_id=1, source_target_pairs={{0,1},{1,0},{2,3},{3,2},{4,5},{5,4},{6,7},{7,6},{8,9},{9,8},{10,11... | collective-permute-start | bytes 491528 | tf_op jit(solution)/shard_map/ppermute | solution.py:418
  12.4 7.6 %collective-permute-start.2 = (f32[5,64,128]{2,1,0:T(8,128)S(1)}, f32[5,64,128]{2,1,0:T(8,128)S(1)}, u32[]{:S(2)}, u32[]{:S(2)}) collective-permute-start(f32[5,64,128]{2,1,0:T(8,128)S(1)} %get-tuple-element.49), channel_id=1, source_target_pairs={{0,15},{1,2},{2,1},{3,4},{4,3},{5,6},{6,5},{7,8},{8,7},{9,10},{10,... | collective-permute-start | bytes 491528 | tf_op jit(solution)/shard_map/ppermute | solution.py:419
  16.8 3.3 %collective-permute-start.3 = (f32[5,64,128]{2,1,0:T(8,128)S(1)}, f32[5,64,128]{2,1,0:T(8,128)S(1)}, u32[]{:S(2)}, u32[]{:S(2)}) collective-permute-start(f32[5,64,128]{2,1,0:T(8,128)S(1)} %get-tuple-element.50), channel_id=1, source_target_pairs={{0,1},{1,0},{2,3},{3,2},{4,5},{5,4},{6,7},{7,6},{8,9},{9,8},{10,11... | collective-permute-start | bytes 491528 | tf_op jit(solution)/shard_map/ppermute | solution.py:418
  21.5 7.5 %collective-permute-start.8 = (f32[5,64,128]{2,1,0:T(8,128)S(1)}, f32[5,64,128]{2,1,0:T(8,128)S(1)}, u32[]{:S(2)}, u32[]{:S(2)}) collective-permute-start(f32[5,64,128]{2,1,0:T(8,128)S(1)} %get-tuple-element.65), channel_id=1, source_target_pairs={{0,15},{1,2},{2,1},{3,4},{4,3},{5,6},{6,5},{7,8},{8,7},{9,10},{10,... | collective-permute-start | bytes 491528 | tf_op jit(solution)/shard_map/ppermute | solution.py:419
  25.7 3.3 %collective-permute-start.9 = (f32[5,64,128]{2,1,0:T(8,128)S(1)}, f32[5,64,128]{2,1,0:T(8,128)S(1)}, u32[]{:S(2)}, u32[]{:S(2)}) collective-permute-start(f32[5,64,128]{2,1,0:T(8,128)S(1)} %get-tuple-element.66), channel_id=1, source_target_pairs={{0,1},{1,0},{2,3},{3,2},{4,5},{5,4},{6,7},{7,6},{8,9},{9,8},{10,11... | collective-permute-start | bytes 491528 | tf_op jit(solution)/shard_map/ppermute | solution.py:418
  25.7 9.9 %collective-permute-start.6 = (f32[5,64,128]{2,1,0:T(8,128)S(1)}, f32[5,64,128]{2,1,0:T(8,128)S(1)}, u32[]{:S(2)}, u32[]{:S(2)}) collective-permute-start(f32[5,64,128]{2,1,0:T(8,128)S(1)} %get-tuple-element.59), channel_id=1, source_target_pairs={{0,15},{1,2},{2,1},{3,4},{4,3},{5,6},{6,5},{7,8},{8,7},{9,10},{10,... | collective-permute-start | bytes 491528 | tf_op jit(solution)/shard_map/ppermute | solution.py:419
  26.0 9.7 %collective-permute-start.7 = (f32[5,64,128]{2,1,0:T(8,128)S(1)}, f32[5,64,128]{2,1,0:T(8,128)S(1)}, u32[]{:S(2)}, u32[]{:S(2)}) collective-permute-start(f32[5,64,128]{2,1,0:T(8,128)S(1)} %get-tuple-element.60), channel_id=1, source_target_pairs={{0,1},{1,0},{2,3},{3,2},{4,5},{5,4},{6,7},{7,6},{8,9},{9,8},{10,11... | collective-permute-start | bytes 491528 | tf_op jit(solution)/shard_map/ppermute | solution.py:418
  30.0 8.0 %collective-permute-start.10 = (f32[5,64,128]{2,1,0:T(8,128)S(1)}, f32[5,64,128]{2,1,0:T(8,128)S(1)}, u32[]{:S(2)}, u32[]{:S(2)}) collective-permute-start(f32[5,64,128]{2,1,0:T(8,128)S(1)} %get-tuple-element.72), channel_id=1, source_target_pairs={{0,15},{1,2},{2,1},{3,4},{4,3},{5,6},{6,5},{7,8},{8,7},{9,10},{10,... | collective-permute-start | bytes 491528 | tf_op jit(solution)/shard_map/ppermute | solution.py:419
  34.2 3.8 %collective-permute-start.11 = (f32[5,64,128]{2,1,0:T(8,128)S(1)}, f32[5,64,128]{2,1,0:T(8,128)S(1)}, u32[]{:S(2)}, u32[]{:S(2)}) collective-permute-start(f32[5,64,128]{2,1,0:T(8,128)S(1)} %get-tuple-element.73), channel_id=1, source_target_pairs={{0,1},{1,0},{2,3},{3,2},{4,5},{5,4},{6,7},{7,6},{8,9},{9,8},{10,11... | collective-permute-start | bytes 491528 | tf_op jit(solution)/shard_map/ppermute | solution.py:418

commit v2 on v1

--- a/solution.py
+++ b/solution.py
@@ -21,30 +21,31 @@
 def iotas():
     lane = lax.broadcasted_iota(jnp.int32, (8, LANES), 1)
     row = lax.broadcasted_iota(jnp.int32, (8, LANES), 0)
-    return {"high": lane >= 64, "first": lane % 64 == 0, "last": lane % 64 == 63,
-            "top": row == 0, "bottom": row == 7}
+    turns = {}
+    for turn in (0, 64):
+        for cz in (1, -1):
+            turns[turn, cz] = ((lane & 64) ^ turn) | ((lane - cz) & 63)
+    return {"high": lane >= 64, "top": row == 0, "bottom": row == 7, **turns}
 
 
 def block(r):
-    return pl.ds(pl.multiple_of(r * 8, 8), 8)
+    return pl.ds(r * 8 if isinstance(r, int) else pl.multiple_of(r * 8, 8), 8)
 
 
 def shifted(ref, index, r, cy, cz, m):
     here = ref[index + (block(r), slice(None))]
     turn = 0
     if cy == 1:
-        edge = ref[index + (pl.ds(lax.rem(r + 7, 8) * 8 + 7, 1), slice(None))]
+        edge = ref[index + (pl.ds(((r + 7) & 7) * 8 + 7, 1), slice(None))]
         other = jnp.where(m["top"], edge, pltpu.roll(here, 1, 0))
         here, turn = jnp.where(m["high"], other, here), 64
     elif cy == -1:
-        edge = ref[index + (pl.ds(lax.rem(r + 1, 8) * 8, 1), slice(None))]
+        edge = ref[index + (pl.ds(((r + 1) & 7) * 8, 1), slice(None))]
         other = jnp.where(m["bottom"], edge, pltpu.roll(here, 7, 0))
         here, turn = jnp.where(m["high"], here, other), 64
     if cz == 0:
         return pltpu.roll(here, turn, 1) if turn else here
-    main = pltpu.roll(here, (turn + cz) % LANES, 1)
-    wrapped = pltpu.roll(here, (turn + cz + 64) % LANES, 1)
-    return jnp.where(m["first"] if cz == 1 else m["last"], wrapped, main)
+    return jnp.take_along_axis(here, m[turn, cz], axis=1)
 
 
 def moments(f):
@@ -160,8 +161,8 @@
 
 
 def put_velocity(u_ref, u, i, r):
-    for j in range(3):
-        u_ref[j, i, block(r), :] = u[j]
+    for j, value in enumerate(u):
+        u_ref[j, i, block(r), :] = value
 
 
 def get_velocity(u_ref, i, r):
@@ -186,12 +187,6 @@
         kk, rows = native(flip, k, p, r)
         out.append(ref[kk, rows, :])
     return out
-
-
-def put_native(ref, values, flip, p, r):
-    for k in range(19):
-        kk, rows = native(flip, k, p, r)
-        ref[kk, rows, :] = values[k]
 
 
 def loop(body):
@@ -280,17 +275,27 @@
     loop(body)
 
 
-def edge_values(ready, far, near, i, p, r, sign, m):
+def receive(far, near, got, sign, m):
+    for r in range(BLOCKS):
+        for i, p in enumerate(EDGES):
+            for j, k in enumerate(crossing(p, sign)):
+                cy, cz = sign * SPEEDS[k][1], sign * SPEEDS[k][2]
+                got[j, i, block(r), :] = shifted(far if p == 0 else near, (j,), r, cy, cz, m)
+
+
+def edge_values(ready, got, i, p, r, sign):
     values = get_some(ready, i, r, crossing(p, sign))
-    return pull_remote(far if p == 0 else near, values, p, r, sign, m)
-
-
-def forward_edges(ready, far, near, om_ref, post, u_ref, far_out, near_out):
-    m = iotas()
-
-    def body(r):
-        for i, p in enumerate(EDGES):
-            f = edge_values(ready, far, near, i, p, r, 1, m)
+    for j, k in enumerate(crossing(p, sign)):
+        values[k] = got[j, i, block(r), :]
+    return values
+
+
+def forward_edges(ready, far, near, om_ref, post, u_ref, far_out, near_out, got):
+    receive(far, near, got, 1, iotas())
+
+    def body(r):
+        for i, p in enumerate(EDGES):
+            f = edge_values(ready, got, i, p, r, 1)
             rho, u = state_of(f)
             put_velocity(u_ref, u, i, r)
             out = relaxed(f, rho, u, om_ref[p, block(r), :])
@@ -313,12 +318,27 @@
     loop(body)
 
 
-def adjoint_edges(ready, far, near, om_ref, u_ref, lam, far_out, near_out):
+def adjoint_top(edge, inner, om_ref, u_ref, far, near, lam, ready):
     m = iotas()
 
     def body(r):
-        for i, p in enumerate(EDGES):
-            mu = edge_values(ready, far, near, i, p, r, -1, m)
+        for i, p in enumerate(INNER):
+            mu = pull_local(edge, inner, p, r, -1, m)
+            put_all(lam, adjoint(mu, get_velocity(u_ref, i, r), om_ref[p, block(r), :]), i, r)
+        for i, p in enumerate(EDGES):
+            mu = pull_local(edge, inner, p, r, -1, m)
+            pull_remote(far if p == 0 else near, mu, p, r, -1, m)
+            put_all(ready, mu, i, r)
+
+    loop(body)
+
+
+def adjoint_edges(ready, far, near, om_ref, u_ref, lam, far_out, near_out, got):
+    receive(far, near, got, -1, iotas())
+
+    def body(r):
+        for i, p in enumerate(EDGES):
+            mu = edge_values(ready, got, i, p, r, -1)
             out = adjoint(mu, get_velocity(u_ref, i, r), om_ref[p, block(r), :])
             put_all(lam, out, i, r)
             put_crossing(far_out, near_out, out, p, r, -1)
@@ -326,53 +346,107 @@
     loop(body)
 
 
-def turn_edges(ready, far, near, om_ref, mus, farc, nearc, post, lam, far_post, near_post, far_out, near_out):
-    m = iotas()
-
-    def body(r):
-        for i, p in enumerate(EDGES):
-            om = om_ref[p, block(r), :]
-            f = edge_values(ready, far, near, i, p, r, 1, m)
-            rho, u = state_of(f)
-            out = relaxed(f, rho, u, om)
-            put_all(post, out, i, r)
-            put_crossing(far_post, near_post, out, p, r, 1)
-            out = adjoint(edge_values(mus, farc, nearc, i, p, r, -1, m), u, om)
+def turn_edges(ready, far, near, om_ref, mus, lam, far_out, near_out, got, state):
+    receive(far, near, got, 1, iotas())
+
+    def body(r):
+        for i, p in enumerate(EDGES):
+            rho, u = state_of(edge_values(ready, got, i, p, r, 1))
+            put_velocity(state, u + [rho], i, r)
+            out = adjoint(get_some(mus, i, r), u, om_ref[p, block(r), :])
             put_all(lam, out, i, r)
             put_crossing(far_out, near_out, out, p, r, -1)
 
     loop(body)
 
 
-def stream_last(edge, inner, far, near, final, hold, sem):
+def relax_edges(ready, got, state, om_ref, post, far_out, near_out):
+    def body(r):
+        for i, p in enumerate(EDGES):
+            f = edge_values(ready, got, i, p, r, 1)
+            *u, rho = [state[j, i, block(r), :] for j in range(4)]
+            out = relaxed(f, rho, u, om_ref[p, block(r), :])
+            put_all(post, out, i, r)
+            put_crossing(far_out, near_out, out, p, r, 1)
+
+    loop(body)
+
+
+def put_mirrored(hold, values, flip, i, r):
+    for k in range(19):
+        kk = k if MIRROR[k] == k else jnp.where(flip == 1, MIRROR[k], k)
+        hold[kk, i, block(r), :] = values[k]
+
+
+def write_out(hold, result, sem, flip, p, i, r):
+    x = jnp.where(flip == 1, PLANES - 1 - p, p)
+    return pltpu.make_async_copy(
+        hold.at[:, i, block(r), :], result.at[:, block(r), x, :], sem.at[i, r]
+    )
+
+
+def write_all(hold, result, sem, flip, places, each):
+    def body(r):
+        each(r)
+        for i, p in enumerate(places):
+            write_out(hold, result, sem, flip, p, i, r).start()
+
+    def wait(r):
+        for i, p in enumerate(places):
+            write_out(hold, result, sem, flip, p, i, r).wait()
+
+    loop(body)
+    loop(wait)
+
+
+def stream_inner(edge, inner, final, ready, hold, sem):
     flip, m = flipped(), iotas()
 
-    def body(r):
-        for p in range(PLANES):
-            f = pull_local(edge, inner, p, r, 1, m)
-            if p in EDGES:
-                pull_remote(far if p == 0 else near, f, p, r, 1, m)
-            put_native(hold, f, flip, p, r)
-        moved(hold, final, sem, r).start()
-
-    loop(body)
-    loop(lambda r: moved(hold, final, sem, r).wait())
-
-
-def adjoint_last(ready, far, near, om_ref, u_ref, inner, grad, hold, sem):
+    def each(r):
+        for i, p in enumerate(INNER):
+            put_mirrored(hold, pull_local(edge, inner, p, r, 1, m), flip, i, r)
+        for i, p in enumerate(EDGES):
+            put_all(ready, pull_local(edge, inner, p, r, 1, m), i, r)
+
+    write_all(hold, final, sem, flip, INNER, each)
+
+
+def stream_edges(ready, far, near, partial, final, hold, sem, got):
+    flip = flipped()
+    receive(far, near, got, 1, iotas())
+
+    def each(r):
+        for i, p in enumerate(EDGES):
+            put_mirrored(hold, edge_values(ready, got, i, p, r, 1), flip, i, r)
+
+    write_all(hold, final, sem, flip, EDGES, each)
+
+
+def adjoint_inner_last(edge, inner, om_ref, u_ref, grad, ready, hold, sem):
     flip, m = flipped(), iotas()
 
-    def body(r):
-        for i, p in enumerate(EDGES):
-            mu = edge_values(ready, far, near, i, p, r, -1, m)
+    def each(r):
+        for i, p in enumerate(INNER):
+            mu = pull_local(edge, inner, p, r, -1, m)
             out = adjoint(mu, get_velocity(u_ref, i, r), om_ref[p, block(r), :])
-            put_native(hold, out, flip, p, r)
-        for i, p in enumerate(INNER):
-            put_native(hold, get_some(inner, i, r), flip, p, r)
-        moved(hold, grad, sem, r).start()
-
-    loop(body)
-    loop(lambda r: moved(hold, grad, sem, r).wait())
+            put_mirrored(hold, out, flip, i, r)
+        for i, p in enumerate(EDGES):
+            put_all(ready, pull_local(edge, inner, p, r, -1, m), i, r)
+
+    write_all(hold, grad, sem, flip, INNER, each)
+
+
+def adjoint_edges_last(ready, far, near, om_ref, u_ref, partial, grad, hold, sem, got):
+    flip = flipped()
+    receive(far, near, got, -1, iotas())
+
+    def each(r):
+        for i, p in enumerate(EDGES):
+            mu = edge_values(ready, got, i, p, r, -1)
+            out = adjoint(mu, get_velocity(u_ref, i, r), om_ref[p, block(r), :])
+            put_mirrored(hold, out, flip, i, r)
+
+    write_all(hold, grad, sem, flip, EDGES, each)
 
 
 INSIDE = pl.BlockSpec(memory_space=pltpu.VMEM)
@@ -383,10 +457,14 @@
 CROSS = (5, ROWS, LANES)
 NATIVE = (19, PLANES * ROWS, LANES)
 SEMS = pltpu.SemaphoreType.DMA((BLOCKS,))
-STAGED = [pltpu.VMEM(NATIVE, F32), SEMS]
-
-
-def kernel(body, outs, scratch=()):
+STATE = (4, 2, ROWS, LANES)
+CROSSED = (5, 2, ROWS, LANES)
+RESULT = (19, ROWS, PLANES, LANES)
+STAGED = [pltpu.VMEM(PAIR, F32), pltpu.SemaphoreType.DMA((2, BLOCKS))]
+GOT = [pltpu.VMEM(CROSSED, F32)]
+
+
+def kernel(body, outs, scratch=(), aliases=None):
     def call(*args):
         args = [x if isinstance(x, tuple) else (x, 1) for x in args]
         return pl.pallas_call(
@@ -397,6 +475,7 @@
                 pltpu.VMEM(s, F32) if inside else jax.ShapeDtypeStruct(s, F32) for s, inside in outs
             ],
             scratch_shapes=list(scratch),
+            input_output_aliases=aliases or {},
             compiler_params=pltpu.CompilerParams(vmem_limit_bytes=8 * 2**20),
             name=body.__name__,
         )(
@@ -424,7 +503,7 @@
         return jnp.swapaxes(x, -3, -2).reshape(lead + (PLANES * ROWS, LANES))
 
     def from_native(x):
-        return jnp.swapaxes(x.reshape(19, ROWS, PLANES, LANES), 1, 2).reshape(populations.shape)
+        return jnp.swapaxes(x, 1, 2).reshape(populations.shape)
 
     pops, classes, cot = to_native(populations), to_native(relax_class), to_native(cotangent)
     pair, speed, cross = (PAIR, 1), (VELOCITY, 1), (CROSS, 1)
@@ -433,30 +512,38 @@
         [(NATIVE, 1), (RELAX, 1), pair, speed, cross, cross],
         [pltpu.VMEM(classes.shape, jnp.int32), SEMS, pltpu.SemaphoreType.DMA],
     )((pops, 0), (classes, 0))
+    cot, far, near = lax.optimization_barrier((cot, far, near))
     far, near = exchange(far, near)
     post_i, u0_i = kernel(first_inner, [pair, speed])(held, om)
     cot_e, cot_i, farc, nearc = kernel(cotangent_planes, [pair, pair, cross, cross])(cot)
     farc, nearc = exchange(farc, nearc)
     inner = kernel(forward_inner, [pair, speed, pair])
-    back_inner = kernel(adjoint_inner, [pair, pair])
-    back_edges = kernel(adjoint_edges, [pair, cross, cross])
 
     post_i, u1_i, ready = inner(post_e, post_i, om)
-    post_e, u1_e, far, near = kernel(forward_edges, [pair, speed, cross, cross])(ready, far, near, om)
+    post_e, u1_e, far, near = kernel(forward_edges, [pair, speed, cross, cross], GOT)(
+        ready, far, near, om
+    )
     far, near = exchange(far, near)
     post_i, u2_i, ready = inner(post_e, post_i, om)
-    lam_i, mus = back_inner(cot_e, cot_i, om, u2_i)
-    post_e, lam_e, far_post, near_post, far, near = kernel(
-        turn_edges, [pair, pair, cross, cross, cross, cross]
-    )(ready, far, near, om, mus, farc, nearc)
+    lam_i, mus = kernel(adjoint_top, [pair, pair])(cot_e, cot_i, om, u2_i, farc, nearc)
+    lam_e, far, near, got, state = kernel(
+        turn_edges, [pair, cross, cross, (CROSSED, 1), (STATE, 1)]
+    )(ready, far, near, om, mus)
     far, near = exchange(far, near)
+    post_e, far_post, near_post = kernel(relax_edges, [pair, cross, cross])(ready, got, state, om)
     far_post, near_post = exchange(far_post, near_post)
-    lam_i, ready = back_inner(lam_e, lam_i, om, u1_i)
-    lam_e, far, near = back_edges(ready, far, near, om, u1_e)
+    lam_i, ready = kernel(adjoint_inner, [pair, pair])(lam_e, lam_i, om, u1_i)
+    final, ready_f = kernel(stream_inner, [(RESULT, 0), pair], STAGED)(post_e, post_i)
+    ready, ready_f = lax.optimization_barrier((ready, ready_f))
+    lam_e, far, near = kernel(adjoint_edges, [pair, cross, cross], GOT)(ready, far, near, om, u1_e)
     far, near = exchange(far, near)
-    (final,) = kernel(stream_last, [(NATIVE, 0)], STAGED)(post_e, post_i, far_post, near_post)
-    lam_i, ready = back_inner(lam_e, lam_i, om, u0_i)
-    (grad,) = kernel(adjoint_last, [(NATIVE, 0)], STAGED)(ready, far, near, om, u0_e, lam_i)
+    grad, ready = kernel(adjoint_inner_last, [(RESULT, 0), pair], STAGED)(lam_e, lam_i, om, u0_i)
+    (final,) = kernel(stream_edges, [(RESULT, 0)], STAGED + GOT, {3: 0})(
+        ready_f, far_post, near_post, (final, 0)
+    )
+    (grad,) = kernel(adjoint_edges_last, [(RESULT, 0)], STAGED + GOT, {5: 0})(
+        ready, far, near, om, u0_e, (grad, 0)
+    )
     return from_native(final), from_native(grad)
 
 

time: 40.2 us -> 39.8 us (0.990)
  waiting for transfers between devices: 1.8 us -> 0.33 us
  Pallas kernels: 17.7 us -> 19 us
    ppermute x6, waiting for transfers between devices: 1.79 us -> 0.31 us  [exchange(): return (lax.ppermute(far, 'gx', far_pairs), near)]
    pallas_call x13 -> x15, Pallas kernels: 17.7 us -> 19 us  [call(): pl.pallas_call(body, in_specs=[INSIDE if inside else OUTSIDE for _, insid...]
  transfers between devices with their start and end apart: 12 -> 12, of which waited for: 2 -> 1; matrix products, arithmetic and copies ran while one was open for 0% -> 0% of each run, Pallas kernels for 31% -> 37%
where the time goes in v2:
time: 39.8 us; the launch traced here: 39.6 us
  starting transfers between devices  19.4 us (49%)
  Pallas kernels  19 us (48%)
  between operations  0.83 us (2%)
    ppermute x6, starting transfers between devices, exchange(): return (lax.ppermute(far, 'gx', far_pairs), near)  19.1 us
    pallas_call x15, Pallas kernels, call(): pl.pallas_call(body, in_specs=[INSIDE if inside else OUTSIDE for _, insid...  19 us
  transfers between devices with their start and end apart: 12, of which 1 were waited for; matrix products, arithmetic and copies ran while one was open for 0% of the time, Pallas kernels for 37%

profile of v2, /device:TPU:0, one launch (start us, length us, event | category | flops | bytes accessed | tf_op | source)
XLA Modules:
  0.0 39.6 jit_solution(15859185849128285464)
XLA Ops:
  0.6 2.0 %first_edges.1 = (f32[19,256,128]{2,1,0:T(8,128)S(1)}, f32[4,64,128]{2,1,0:T(8,128)S(1)}, f32[19,2,64,128]{3,2,1,0:T(8,128)S(1)}, f32[3,2,64,128]{3,2,1,0:T(8,12...) custom-call(f32[19,256,128]{2,1,0:T(8,128)} %bitcast.22, s32[256,128]{1,0:T(8,128)} %bitcast.25), custom_call_target="tpu_custom_call" | custom-call | tf_op jit(solution)/shard_map/first_edges/pallas_call | solution.py:470
  2.6 5.5 %collective-permute-start = (f32[5,64,128]{2,1,0:T(8,128)S(1)}, f32[5,64,128]{2,1,0:T(8,128)S(1)}, u32[]{:S(2)}, u32[]{:S(2)}) collective-permute-start(f32[5,64,128]{2,1,0:T(8,128)S(1)} %get-tuple-element.55), channel_id=1, source_target_pairs={{0,15},{1,2},{2,1},{3,4},{4,3},{5,6},{6,5},{7,8},{8,7},{9,10},{10,... | collective-permute-start | bytes 491528 | tf_op jit(solution)/shard_map/ppermute | solution.py:498
  8.1 0.0 collective-permute-start.1
  8.1 0.5 %cotangent_planes.1 = (f32[19,2,64,128]{3,2,1,0:T(8,128)S(1)}, f32[19,2,64,128]{3,2,1,0:T(8,128)S(1)}, f32[5,64,128]{2,1,0:T(8,128)S(1)}, f32[5,64,128]{2,1,0:T(8,128)S(1)}) custom-call(f32[19,256,128]{2,1,0:T(8,128)S(1)} %bitcast.21), custom_call_target="tpu_custom_call" | custom-call | tf_op jit(solution)/shard_map/cotangent_planes/pallas_call | solution.py:470
  8.6 0.8 %collective-permute-start.4 = (f32[5,64,128]{2,1,0:T(8,128)S(1)}, f32[5,64,128]{2,1,0:T(8,128)S(1)}, u32[]{:S(2)}, u32[]{:S(2)}) collective-permute-start(f32[5,64,128]{2,1,0:T(8,128)S(1)} %get-tuple-element.66), channel_id=1, source_target_pairs={{0,15},{1,2},{2,1},{3,4},{4,3},{5,6},{6,5},{7,8},{8,7},{9,10},{10,... | collective-permute-start | bytes 491528 | tf_op jit(solution)/shard_map/ppermute | solution.py:498
  9.4 0.5 %first_inner.1 = (f32[19,2,64,128]{3,2,1,0:T(8,128)S(1)}, f32[3,2,64,128]{3,2,1,0:T(8,128)S(1)}) custom-call(f32[19,256,128]{2,1,0:T(8,128)S(1)} %get-tuple-element.49.held, f32[4,64,128]{2,1,0:T(8,128)S(1)} %get-tuple-element.50.om_ref), custom_call_target="tpu_custom_call" | custom-call | tf_op jit(solution)/shard_map/first_inner/pallas_call | solution.py:470
  10.0 1.4 %forward_inner.2 = (f32[19,2,64,128]{3,2,1,0:T(8,128)S(1)}, f32[3,2,64,128]{3,2,1,0:T(8,128)S(1)}, f32[19,2,64,128]{3,2,1,0:T(8,128)S(1)}) custom-call(f32[19,2,64,128]{3,2,1,0:T(8,128)S(1)} %get-tuple-element.48.edge, f32[19,2,64,128]{3,2,1,0:T(8,128)S(1)} %get-tuple-element.51.inner, f32[4,64,128]{2,1,0:T(8,128)S(1)} %get-tuple-element.50.om_ref), custom_call_target="tpu_custom_call" | custom-call | tf_op jit(solution)/shard_map/forward_inner/pallas_call | solution.py:470
  11.4 0.7 %forward_edges.1 = (f32[19,2,64,128]{3,2,1,0:T(8,128)S(1)}, f32[3,2,64,128]{3,2,1,0:T(8,128)S(1)}, f32[5,64,128]{2,1,0:T(8,128)S(1)}, f32[5,64,128]{2,1,0:T(8,128)S(1)}) custom-call(f32[19,2,64,128]{3,2,1,0:T(8,128)S(1)} %get-tuple-element.52.ready, f32[5,64,128]{2,1,0:T(8,128)S(1)} %collective-permute-done.far, ...), custom_call_target="tpu_custom_call" | custom-call | tf_op jit(solution)/shard_map/forward_edges/pallas_call | solution.py:470
  12.1 4.3 %collective-permute-start.2 = (f32[5,64,128]{2,1,0:T(8,128)S(1)}, f32[5,64,128]{2,1,0:T(8,128)S(1)}, u32[]{:S(2)}, u32[]{:S(2)}) collective-permute-start(f32[5,64,128]{2,1,0:T(8,128)S(1)} %get-tuple-element.60), channel_id=1, source_target_pairs={{0,15},{1,2},{2,1},{3,4},{4,3},{5,6},{6,5},{7,8},{8,7},{9,10},{10,... | collective-permute-start | bytes 491528 | tf_op jit(solution)/shard_map/ppermute | solution.py:498
  16.5 1.4 %forward_inner.3 = (f32[19,2,64,128]{3,2,1,0:T(8,128)S(1)}, f32[3,2,64,128]{3,2,1,0:T(8,128)S(1)}, f32[19,2,64,128]{3,2,1,0:T(8,128)S(1)}) custom-call(f32[19,2,64,128]{3,2,1,0:T(8,128)S(1)} %get-tuple-element.57.edge, f32[19,2,64,128]{3,2,1,0:T(8,128)S(1)} %get-tuple-element.58.inner, f32[4,64,128]{2,1,0:T(8,128)S(1)} %get-tuple-element.50.om_ref), custom_call_target="tpu_custom_call" | custom-call | tf_op jit(solution)/shard_map/forward_inner/pallas_call | solution.py:470
  17.9 1.5 %adjoint_top.1 = (f32[19,2,64,128]{3,2,1,0:T(8,128)S(1)}, f32[19,2,64,128]{3,2,1,0:T(8,128)S(1)}) custom-call(f32[19,2,64,128]{3,2,1,0:T(8,128)S(1)} %get-tuple-element.63.edge, f32[19,2,64,128]{3,2,1,0:T(8,128)S(1)} %get-tuple-element.64.inner, f32[4,64,128]{2,1,0:T(8,128)S(1)} %get-tuple-element.50.om_ref, f32[3,2,64,128]{3,2,1,0:T(8,128)S(1)} %get-tuple-element.65.u_ref, ...), custom_call_target="tpu_custom_call" | custom-call | tf_op jit(solution)/shard_map/adjoint_top/pallas_call | solution.py:470
  19.4 0.3 collective-permute-done.2.far
  19.7 0.9 %turn_edges.1 = (f32[19,2,64,128]{3,2,1,0:T(8,128)S(1)}, f32[5,64,128]{2,1,0:T(8,128)S(1)}, f32[5,64,128]{2,1,0:T(8,128)S(1)}, f32[5,2,64,128]{3,2,1,0:T(8,128)S(1)}, f32[4,2,64,128]{3,2,1,0:T(8,128)S(1)}) custom-call(f32[19,2,64,128]{3,2,1,0:T(8,128)S(1)} %get-tuple-element.59.ready, f32[5,64,128]{2,1,0:T(8,128)S(1)} %collective-permute-done.2.far, ...), custom_call_target="tpu_custom_call" | custom-call | tf_op jit(solution)/shard_map/turn_edges/pallas_call | solution.py:470
  20.6 4.2 %collective-permute-start.8 = (f32[5,64,128]{2,1,0:T(8,128)S(1)}, f32[5,64,128]{2,1,0:T(8,128)S(1)}, u32[]{:S(2)}, u32[]{:S(2)}) collective-permute-start(f32[5,64,128]{2,1,0:T(8,128)S(1)} %get-tuple-element.83), channel_id=1, source_target_pairs={{0,15},{1,2},{2,1},{3,4},{4,3},{5,6},{6,5},{7,8},{8,7},{9,10},{10,... | collective-permute-start | bytes 491528 | tf_op jit(solution)/shard_map/ppermute | solution.py:498
  24.9 0.4 relax_edges.1
  25.2 0.4 collective-permute-start.6
  25.6 0.3 collective-permute-start.7
  25.9 2.3 %stream_inner.1 = (f32[19,64,4,128]{3,2,1,0:T(4,128)}, f32[19,2,64,128]{3,2,1,0:T(8,128)S(1)}) custom-call(f32[19,2,64,128]{3,2,1,0:T(8,128)S(1)} %get-tuple-element.75.edge, f32[19,2,64,128]{3,2,1,0:T(8,128)S(1)} %get-tuple-element.76.inner), custom_call_target="tpu_custom_call" | custom-call | tf_op jit(solution)/shard_map/stream_inner/pallas_call | solution.py:470
  28.2 1.5 %adjoint_inner.1 = (f32[19,2,64,128]{3,2,1,0:T(8,128)S(1)}, f32[19,2,64,128]{3,2,1,0:T(8,128)S(1)}) custom-call(f32[19,2,64,128]{3,2,1,0:T(8,128)S(1)} %get-tuple-element.69.edge, f32[19,2,64,128]{3,2,1,0:T(8,128)S(1)} %get-tuple-element.70.inner, f32[4,64,128]{2,1,0:T(8,128)S(1)} %get-tuple-element.50.om_ref, f32[3,2,64,128]{3,2,1,0:T(8,128)S(1)} %get-tuple-element.71.u_ref), custom_call_target="tpu_custom_call" | custom-call | tf_op jit(solution)/shard_map/adjoint_inner/pallas_call | solution.py:470
  29.7 0.7 %adjoint_edges.1 = (f32[19,2,64,128]{3,2,1,0:T(8,128)S(1)}, f32[5,64,128]{2,1,0:T(8,128)S(1)}, f32[5,64,128]{2,1,0:T(8,128)S(1)}) custom-call(f32[19,2,64,128]{3,2,1,0:T(8,128)S(1)} %get-tuple-element.82.ready, f32[5,64,128]{2,1,0:T(8,128)S(1)} %collective-permute-done.8.far, f32[5,64,128]{2,1,0:T(8,128)S(1)} %collective-permute-done.9.near, ...), custom_call_target="tpu_custom_call" | custom-call | tf_op jit(solution)/shard_map/adjoint_edges/pallas_call | solution.py:470
  30.4 3.9 %collective-permute-start.10 = (f32[5,64,128]{2,1,0:T(8,128)S(1)}, f32[5,64,128]{2,1,0:T(8,128)S(1)}, u32[]{:S(2)}, u32[]{:S(2)}) collective-permute-start(f32[5,64,128]{2,1,0:T(8,128)S(1)} %get-tuple-element.90), channel_id=1, source_target_pairs={{0,15},{1,2},{2,1},{3,4},{4,3},{5,6},{6,5},{7,8},{8,7},{9,10},{10,... | collective-permute-start | bytes 491528 | tf_op jit(solution)/shard_map/ppermute | solution.py:498
  34.3 2.2 %adjoint_inner_last.1 = (f32[19,64,4,128]{3,2,1,0:T(4,128)}, f32[19,2,64,128]{3,2,1,0:T(8,128)S(1)}) custom-call(f32[19,2,64,128]{3,2,1,0:T(8,128)S(1)} %get-tuple-element.86.edge, f32[19,2,64,128]{3,2,1,0:T(8,128)S(1)} %get-tuple-element.87.inner, f32[4,64,128]{2,1,0:T(8,128)S(1)} %get-tuple-element.50.om_ref, f32[3,2,64,128]{3,2,1,0:T(8,128)S(1)} %get-tuple-element.88.u_ref), custom_call_target="tpu_custom_call" | custom-call | tf_op jit(solution)/shard_map/adjoint_inner_last/pallas_call | solution.py:470
  36.6 1.4 %stream_edges.1 = f32[19,64,4,128]{3,2,1,0:T(4,128)} custom-call(f32[19,2,64,128]{3,2,1,0:T(8,128)S(1)} %get-tuple-element.78.ready, f32[5,64,128]{2,1,0:T(8,128)S(1)} %collective-permute-done.6.far, f32[5,64,128]{2,1,0:T(8,128)S(1)} %collective-permute-done.7.near, f32[19,64,4,128]{3,2,1,0:T(4,128)} %get-tuple-element.81.partial), custom_call_target="tpu_custom_call", output_to_operand_aliasing={{}: (3, {})} | custom-call | tf_op jit(solution)/shard_map/stream_edges/pallas_call | solution.py:470
  38.0 1.6 %adjoint_edges_last.1 = f32[19,64,4,128]{3,2,1,0:T(4,128)} custom-call(f32[19,2,64,128]{3,2,1,0:T(8,128)S(1)} %get-tuple-element.89.ready, f32[5,64,128]{2,1,0:T(8,128)S(1)} %collective-permute-done.10.far, f32[5,64,128]{2,1,0:T(8,128)S(1)} %collective-permute-done.11.near, ...), custom_call_target="tpu_custom_call", output_to_operand_aliasing={{}: (5, {})} | custom-call | tf_op jit(solution)/shard_map/adjoint_edges_last/pallas_call | solution.py:470
  (17 shorter events, 0.0 us)
Async XLA Ops:
  0.6 7.5 %copy-start = (f32[19,4,8192]{2,1,0:T(4,128)S(1)}, f32[19,4,8192]{2,1,0:T(4,128)}, u32[]{:S(2)}) copy-start(f32[19,4,8192]{2,1,0:T(4,128)} %param.5) | copy-start | bytes 7471108
  2.6 8.8 %collective-permute-start = (f32[5,64,128]{2,1,0:T(8,128)S(1)}, f32[5,64,128]{2,1,0:T(8,128)S(1)}, u32[]{:S(2)}, u32[]{:S(2)}) collective-permute-start(f32[5,64,128]{2,1,0:T(8,128)S(1)} %get-tuple-element.55), channel_id=1, source_target_pairs={{0,15},{1,2},{2,1},{3,4},{4,3},{5,6},{6,5},{7,8},{8,7},{9,10},{10,... | collective-permute-start | bytes 491528 | tf_op jit(solution)/shard_map/ppermute | solution.py:498
  8.1 3.3 %collective-permute-start.1 = (f32[5,64,128]{2,1,0:T(8,128)S(1)}, f32[5,64,128]{2,1,0:T(8,128)S(1)}, u32[]{:S(2)}, u32[]{:S(2)}) collective-permute-start(f32[5,64,128]{2,1,0:T(8,128)S(1)} %get-tuple-element.56), channel_id=1, source_target_pairs={{0,1},{1,0},{2,3},{3,2},{4,5},{5,4},{6,7},{7,6},{8,9},{9,8},{10,11... | collective-permute-start | bytes 491528 | tf_op jit(solution)/shard_map/ppermute | solution.py:497
  8.6 9.3 %collective-permute-start.4 = (f32[5,64,128]{2,1,0:T(8,128)S(1)}, f32[5,64,128]{2,1,0:T(8,128)S(1)}, u32[]{:S(2)}, u32[]{:S(2)}) collective-permute-start(f32[5,64,128]{2,1,0:T(8,128)S(1)} %get-tuple-element.66), channel_id=1, source_target_pairs={{0,15},{1,2},{2,1},{3,4},{4,3},{5,6},{6,5},{7,8},{8,7},{9,10},{10,... | collective-permute-start | bytes 491528 | tf_op jit(solution)/shard_map/ppermute | solution.py:498
  9.4 8.5 %collective-permute-start.5 = (f32[5,64,128]{2,1,0:T(8,128)S(1)}, f32[5,64,128]{2,1,0:T(8,128)S(1)}, u32[]{:S(2)}, u32[]{:S(2)}) collective-permute-start(f32[5,64,128]{2,1,0:T(8,128)S(1)} %get-tuple-element.67), channel_id=1, source_target_pairs={{0,1},{1,0},{2,3},{3,2},{4,5},{5,4},{6,7},{7,6},{8,9},{9,8},{10,11... | collective-permute-start | bytes 491528 | tf_op jit(solution)/shard_map/ppermute | solution.py:497
  12.1 7.6 %collective-permute-start.2 = (f32[5,64,128]{2,1,0:T(8,128)S(1)}, f32[5,64,128]{2,1,0:T(8,128)S(1)}, u32[]{:S(2)}, u32[]{:S(2)}) collective-permute-start(f32[5,64,128]{2,1,0:T(8,128)S(1)} %get-tuple-element.60), channel_id=1, source_target_pairs={{0,15},{1,2},{2,1},{3,4},{4,3},{5,6},{6,5},{7,8},{8,7},{9,10},{10,... | collective-permute-start | bytes 491528 | tf_op jit(solution)/shard_map/ppermute | solution.py:498
  16.5 3.3 %collective-permute-start.3 = (f32[5,64,128]{2,1,0:T(8,128)S(1)}, f32[5,64,128]{2,1,0:T(8,128)S(1)}, u32[]{:S(2)}, u32[]{:S(2)}) collective-permute-start(f32[5,64,128]{2,1,0:T(8,128)S(1)} %get-tuple-element.61), channel_id=1, source_target_pairs={{0,1},{1,0},{2,3},{3,2},{4,5},{5,4},{6,7},{7,6},{8,9},{9,8},{10,11... | collective-permute-start | bytes 491528 | tf_op jit(solution)/shard_map/ppermute | solution.py:497
  20.6 9.0 %collective-permute-start.8 = (f32[5,64,128]{2,1,0:T(8,128)S(1)}, f32[5,64,128]{2,1,0:T(8,128)S(1)}, u32[]{:S(2)}, u32[]{:S(2)}) collective-permute-start(f32[5,64,128]{2,1,0:T(8,128)S(1)} %get-tuple-element.83), channel_id=1, source_target_pairs={{0,15},{1,2},{2,1},{3,4},{4,3},{5,6},{6,5},{7,8},{8,7},{9,10},{10,... | collective-permute-start | bytes 491528 | tf_op jit(solution)/shard_map/ppermute | solution.py:498
  24.9 4.8 %collective-permute-start.9 = (f32[5,64,128]{2,1,0:T(8,128)S(1)}, f32[5,64,128]{2,1,0:T(8,128)S(1)}, u32[]{:S(2)}, u32[]{:S(2)}) collective-permute-start(f32[5,64,128]{2,1,0:T(8,128)S(1)} %get-tuple-element.84), channel_id=1, source_target_pairs={{0,1},{1,0},{2,3},{3,2},{4,5},{5,4},{6,7},{7,6},{8,9},{9,8},{10,11... | collective-permute-start | bytes 491528 | tf_op jit(solution)/shard_map/ppermute | solution.py:497
  25.2 11.3 %collective-permute-start.6 = (f32[5,64,128]{2,1,0:T(8,128)S(1)}, f32[5,64,128]{2,1,0:T(8,128)S(1)}, u32[]{:S(2)}, u32[]{:S(2)}) collective-permute-start(f32[5,64,128]{2,1,0:T(8,128)S(1)} %get-tuple-element.79), channel_id=1, source_target_pairs={{0,15},{1,2},{2,1},{3,4},{4,3},{5,6},{6,5},{7,8},{8,7},{9,10},{10,... | collective-permute-start | bytes 491528 | tf_op jit(solution)/shard_map/ppermute | solution.py:498
  25.6 11.0 %collective-permute-start.7 = (f32[5,64,128]{2,1,0:T(8,128)S(1)}, f32[5,64,128]{2,1,0:T(8,128)S(1)}, u32[]{:S(2)}, u32[]{:S(2)}) collective-permute-start(f32[5,64,128]{2,1,0:T(8,128)S(1)} %get-tuple-element.80), channel_id=1, source_target_pairs={{0,1},{1,0},{2,3},{3,2},{4,5},{5,4},{6,7},{7,6},{8,9},{9,8},{10,11... | collective-permute-start | bytes 491528 | tf_op jit(solution)/shard_map/ppermute | solution.py:497
  30.4 7.6 %collective-permute-start.10 = (f32[5,64,128]{2,1,0:T(8,128)S(1)}, f32[5,64,128]{2,1,0:T(8,128)S(1)}, u32[]{:S(2)}, u32[]{:S(2)}) collective-permute-start(f32[5,64,128]{2,1,0:T(8,128)S(1)} %get-tuple-element.90), channel_id=1, source_target_pairs={{0,15},{1,2},{2,1},{3,4},{4,3},{5,6},{6,5},{7,8},{8,7},{9,10},{10,... | collective-permute-start | bytes 491528 | tf_op jit(solution)/shard_map/ppermute | solution.py:498
  34.3 3.7 %collective-permute-start.11 = (f32[5,64,128]{2,1,0:T(8,128)S(1)}, f32[5,64,128]{2,1,0:T(8,128)S(1)}, u32[]{:S(2)}, u32[]{:S(2)}) collective-permute-start(f32[5,64,128]{2,1,0:T(8,128)S(1)} %get-tuple-element.91), channel_id=1, source_target_pairs={{0,1},{1,0},{2,3},{3,2},{4,5},{5,4},{6,7},{7,6},{8,9},{9,8},{10,11... | collective-permute-start | bytes 491528 | tf_op jit(solution)/shard_map/ppermute | solution.py:497

commit v3 on v1

v3 whole, which is shorter than its diff:
```python
import jax
import jax.numpy as jnp
from jax import lax
from jax.experimental import pallas as pl
from jax.experimental.pallas import tpu as pltpu
from jax.sharding import PartitionSpec as P

PLANES, ROWS, LANES, BLOCKS = 4, 64, 128, 8
SPEEDS = [
    (0, 0, 0), (1, 0, 0), (-1, 0, 0), (0, 1, 0), (0, -1, 0), (0, 0, 1), (0, 0, -1),
    (1, 1, 0), (-1, -1, 0), (1, -1, 0), (-1, 1, 0), (1, 0, 1), (-1, 0, -1),
    (1, 0, -1), (-1, 0, 1), (0, 1, 1), (0, -1, -1), (0, 1, -1), (0, -1, 1),
]
RATES = [1.0 / 1.0, 1.0 / 1.25, 1.0 / 1.6, 1.0 / 2.4]
MIRROR = [SPEEDS.index((-cx, cy, cz)) for cx, cy, cz in SPEEDS]
PLUS = [k for k in range(19) if SPEEDS[k][0] == 1]
MINUS = [MIRROR[k] for k in PLUS]
F32 = jnp.float32


def iotas():
    lane = lax.broadcasted_iota(jnp.int32, (8, LANES), 1)
    row = lax.broadcasted_iota(jnp.int32, (8, LANES), 0)
    turns = {}
    for turn in (0, 64):
        for cz in (1, -1):
            turns[turn, cz] = ((lane & 64) ^ turn) | ((lane - cz) & 63)
    return {"high": lane >= 64, "top": row == 0, "bottom": row == 7, **turns}


def block(r):
    return pl.ds(r * 8 if isinstance(r, int) else pl.multiple_of(r * 8, 8), 8)


def shifted(ref, index, r, cy, cz, m):
    here = ref[index + (block(r), slice(None))]
    turn = 0
    if cy == 1:
        edge = ref[index + (pl.ds(((r + 7) & 7) * 8 + 7, 1), slice(None))]
        other = jnp.where(m["top"], edge, pltpu.roll(here, 1, 0))
        here, turn = jnp.where(m["high"], other, here), 64
    elif cy == -1:
        edge = ref[index + (pl.ds(((r + 1) & 7) * 8, 1), slice(None))]
        other = jnp.where(m["bottom"], edge, pltpu.roll(here, 7, 0))
        here, turn = jnp.where(m["high"], here, other), 64
    if cz == 0:
        return pltpu.roll(here, turn, 1) if turn else here
    return jnp.take_along_axis(here, m[turn, cz], axis=1)


def moments(f):
    s = [f[k] + f[k + 1] for k in range(1, 19, 2)]
    d = [f[k] - f[k + 1] for k in range(1, 19, 2)]
    rho = f[0] + ((s[0] + s[1]) + (s[2] + s[3])) + ((s[4] + s[5]) + (s[6] + s[7])) + s[8]
    jx = d[0] + ((d[3] + d[4]) + (d[5] + d[6]))
    jy = d[1] + ((d[3] - d[4]) + (d[7] + d[8]))
    jz = d[2] + ((d[5] - d[6]) + (d[7] - d[8]))
    return rho, jx, jy, jz


def along_odd(k, v):
    total = None
    for c, x in zip(SPEEDS[k], v):
        if c:
            total = x if total is None else (total + x if c == 1 else total - x)
    return total


def relaxed(f, rho, u, om):
    keep = 1.0 - om
    wr = om * rho
    shape = 1.0 - 1.5 * (u[0] * u[0] + u[1] * u[1] + u[2] * u[2])
    out = [None] * 19
    out[0] = keep * f[0] + (wr * (1.0 / 3.0)) * shape
    for first, last, w in ((1, 7, 1.0 / 18.0), (7, 19, 1.0 / 36.0)):
        part = wr * w
        base, lin, quad = part * shape, part * 3.0, part * 4.5
        for k in range(first, last, 2):
            a = along_odd(k, u)
            even, odd = base + quad * (a * a), lin * a
            out[k] = keep * f[k] + (even + odd)
            out[k + 1] = keep * f[k + 1] + (even - odd)
    return out


def adjoint(mu, u, om):
    s = [None] + [mu[k] + mu[k + 1] for k in range(1, 19, 2)]
    d = [None] + [mu[k] - mu[k + 1] for k in range(1, 19, 2)]
    a, b = 1.0 / 18.0, 1.0 / 36.0
    s45, s67, s89 = s[4] + s[5], s[6] + s[7], s[8] + s[9]
    xx = a * s[1] + b * (s45 + s67)
    yy = a * s[2] + b * (s45 + s89)
    zz = a * s[3] + b * (s67 + s89)
    m0 = (1.0 / 3.0) * mu[0] + a * ((s[1] + s[2]) + s[3]) + b * ((s45 + s67) + s89)
    xy, xz, yz = b * (s[4] - s[5]), b * (s[6] - s[7]), b * (s[8] - s[9])
    mx = a * d[1] + b * ((d[4] + d[5]) + (d[6] + d[7]))
    my = a * d[2] + b * ((d[4] - d[5]) + (d[8] + d[9]))
    mz = a * d[3] + b * ((d[6] - d[7]) + (d[8] - d[9]))
    vx = xx * u[0] + xy * u[1] + xz * u[2]
    vy = xy * u[0] + yy * u[1] + yz * u[2]
    vz = xz * u[0] + yz * u[1] + zz * u[2]
    uu = u[0] * u[0] + u[1] * u[1] + u[2] * u[2]
    rho_part = om * (m0 + 1.5 * (m0 * uu) - 4.5 * (u[0] * vx + u[1] * vy + u[2] * vz))
    om3 = 3.0 * om
    flow = [
        om3 * (mx + 3.0 * vx - u[0] * m0),
        om3 * (my + 3.0 * vy - u[1] * m0),
        om3 * (mz + 3.0 * vz - u[2] * m0),
    ]
    keep = 1.0 - om
    out = [None] * 19
    out[0] = keep * mu[0] + rho_part
    for k in range(1, 19, 2):
        g = along_odd(k, flow)
        out[k] = keep * mu[k] + (rho_part + g)
        out[k + 1] = keep * mu[k + 1] + (rho_part - g)
    return out


FAR, NEAR, INNER = 0, PLANES - 1, (1, 2)


def plane_of(parts, p):
    far, inner, near = parts
    return (far, ()) if p == FAR else (near, ()) if p == NEAR else (inner, (INNER.index(p),))


def pull_local(parts, p, r, sign, m):
    out = [None] * 19
    for k in range(19):
        cx, cy, cz = (sign * c for c in SPEEDS[k])
        if 0 <= p - cx < PLANES:
            ref, i = plane_of(parts, p - cx)
            out[k] = shifted(ref, (k,) + i, r, cy, cz, m)
    return out


def crossing(p, sign):
    return (PLUS, MINUS)[(sign == 1) != (p == FAR)]


def pull_remote(other, out, p, r, sign, m):
    for i, k in enumerate(crossing(p, sign)):
        out[k] = shifted(other, (i,), r, sign * SPEEDS[k][1], sign * SPEEDS[k][2], m)
    return out


def put(ref, values, r, i=()):
    for k, value in enumerate(values):
        if value is not None:
            ref[(k,) + i + (block(r), slice(None))] = value


def get(ref, r, i=(), count=19, missing=()):
    return [
        None if k in missing else ref[(k,) + i + (block(r), slice(None))] for k in range(count)
    ]


def put_crossing(ref, values, p, r, sign):
    put(ref, [values[k] for k in crossing(p, -sign)], r)


def state_of(f):
    rho, jx, jy, jz = moments(f)
    inv = 1.0 / rho
    return rho, [jx * inv, jy * inv, jz * inv]


def native(flip, k, p, r):
    kk = k if MIRROR[k] == k else jnp.where(flip == 1, MIRROR[k], k)
    x = jnp.where(flip == 1, PLANES - 1 - p, p)
    return kk, pl.ds(r * (8 * PLANES) + x, 8, stride=PLANES)


def get_native(ref, flip, p, r):
    out = []
    for k in range(19):
        kk, rows = native(flip, k, p, r)
        out.append(ref[kk, rows, :])
    return out


def put_native(ref, values, flip, p, r):
    for k in range(19):
        kk, rows = native(flip, k, p, r)
        ref[kk, rows, :] = values[k]


def put_mirrored(hold, values, flip, r, i=()):
    for k in range(19):
        kk = k if MIRROR[k] == k else jnp.where(flip == 1, MIRROR[k], k)
        hold[(kk,) + i + (block(r), slice(None))] = values[k]


def loop(body, step=1):
    def steps(r, carry):
        for j in range(step):
            body(r * step + j)
        return carry

    lax.fori_loop(0, BLOCKS // step, steps, 0)


def chunk(ref, r):
    rows = 8 * PLANES
    return ref.at[:, pl.ds(pl.multiple_of(r * rows, rows), rows), :]


def moved(source, target, sem, r):
    return pltpu.make_async_copy(chunk(source, r), chunk(target, r), sem.at[r])


def write_out(hold, result, sem, flip, p, r):
    x = jnp.where(flip == 1, PLANES - 1 - p, p)
    return pltpu.make_async_copy(hold.at[:, block(r), :], result.at[:, block(r), x, :], sem.at[r])


def flipped():
    return lax.rem(lax.axis_index("gx"), 2)


def first_edges(
    pops, classes, held, om_ref, post_f, post_n, u_f, u_n, far_out, near_out, cls_ref, sem, cls_sem
):
    flip = flipped()
    fetch = pltpu.make_async_copy(classes, cls_ref, cls_sem)
    fetch.start()
    loop(lambda r: moved(pops, held, sem, r).start())
    fetch.wait()

    def body(r):
        moved(pops, held, sem, r).wait()
        for p in range(PLANES):
            cls = cls_ref[native(flip, 0, p, r)[1], :]
            om = jnp.full((8, LANES), RATES[0], F32)
            for entry in range(1, 4):
                om = jnp.where(cls == entry, RATES[entry], om)
            om_ref[p, block(r), :] = om
            if p in INNER:
                continue
            f = get_native(held, flip, p, r)
            rho, u = state_of(f)
            put(u_f if p == FAR else u_n, u, r)
            out = relaxed(f, rho, u, om)
            put(post_f if p == FAR else post_n, out, r)
            put_crossing(far_out if p == FAR else near_out, out, p, r, 1)

    loop(body)


def first_inner(held, om_ref, post, u_ref):
    flip = flipped()

    def body(r):
        for i, p in enumerate(INNER):
            f = get_native(held, flip, p, r)
            rho, u = state_of(f)
            put(u_ref, u, r, (i,))
            put(post, relaxed(f, rho, u, om_ref[p, block(r), :]), r, (i,))

    loop(body)


def cotangent_planes(cot, far, inner, near, far_out, near_out):
    flip = flipped()

    def body(r):
        for p in range(PLANES):
            values = get_native(cot, flip, p, r)
            ref, i = plane_of((far, inner, near), p)
            put(ref, values, r, i)
            if p not in INNER:
                put_crossing(far_out if p == FAR else near_out, values, p, r, -1)

    loop(body)


def forward_inner(far, inner, near, om_ref, post, u_ref, ready_f, ready_n):
    parts, m = (far, inner, near), iotas()

    def body(r):
        for i, p in enumerate(INNER):
            f = pull_local(parts, p, r, 1, m)
            rho, u = state_of(f)
            put(u_ref, u, r, (i,))
            put(post, relaxed(f, rho, u, om_ref[p, block(r), :]), r, (i,))
        for p, ready in ((FAR, ready_f), (NEAR, ready_n)):
            put(ready, pull_local(parts, p, r, 1, m), r)

    loop(body, STEP)


def receive(other, got, p, sign):
    m = iotas()
    for r in range(BLOCKS):
        for j, k in enumerate(crossing(p, sign)):
            cy, cz = sign * SPEEDS[k][1], sign * SPEEDS[k][2]
            got[j, block(r), :] = shifted(other, (j,), r, cy, cz, m)


def edge_values(ready, got, p, r, sign):
    values = get(ready, r, missing=crossing(p, sign))
    for j, k in enumerate(crossing(p, sign)):
        values[k] = got[j, block(r), :]
    return values


def forward_edge(p):
    def forward_edge(ready, other, om_ref, post, u_ref, out_ref, got):
        receive(other, got, p, 1)

        def body(r):
            f = edge_values(ready, got, p, r, 1)
            rho, u = state_of(f)
            put(u_ref, u, r)
            out = relaxed(f, rho, u, om_ref[p, block(r), :])
            put(post, out, r)
            put_crossing(out_ref, out, p, r, 1)

        loop(body, 2)

    return forward_edge


def adjoint_planes(parts, om_ref, u_ref, lam, r, m):
    for i, p in enumerate(INNER):
        mu = pull_local(parts, p, r, -1, m)
        out = adjoint(mu, get(u_ref, r, (i,), 3), om_ref[p, block(r), :])
        put(lam, out, r, (i,))


def adjoint_inner(far, inner, near, om_ref, u_ref, lam, ready_f, ready_n):
    parts, m = (far, inner, near), iotas()

    def body(r):
        adjoint_planes(parts, om_ref, u_ref, lam, r, m)
        for p, ready in ((FAR, ready_f), (NEAR, ready_n)):
            put(ready, pull_local(parts, p, r, -1, m), r)

    loop(body, STEP)


def adjoint_top(far, inner, near, om_ref, u_ref, other_f, other_n, lam, mus_f, mus_n):
    parts, m = (far, inner, near), iotas()

    def body(r):
        adjoint_planes(parts, om_ref, u_ref, lam, r, m)
        for p, mus, other in ((FAR, mus_f, other_f), (NEAR, mus_n, other_n)):
            put(mus, pull_remote(other, pull_local(parts, p, r, -1, m), p, r, -1, m), r)

    loop(body, STEP)


def adjoint_edge(p):
    def adjoint_edge(ready, other, om_ref, u_ref, lam, out_ref, got):
        receive(other, got, p, -1)

        def body(r):
            mu = edge_values(ready, got, p, r, -1)
            out = adjoint(mu, get(u_ref, r, count=3), om_ref[p, block(r), :])
            put(lam, out, r)
            put_crossing(out_ref, out, p, r, -1)

        loop(body, 2)

    return adjoint_edge


def turn_edge(p):
    def turn_edge(ready, other, om_ref, mus, lam, out_ref, got, state):
        receive(other, got, p, 1)

        def body(r):
            rho, u = state_of(edge_values(ready, got, p, r, 1))
            put(state, u + [rho], r)
            out = adjoint(get(mus, r), u, om_ref[p, block(r), :])
            put(lam, out, r)
            put_crossing(out_ref, out, p, r, -1)

        loop(body, 2)

    return turn_edge


def relax_edges(ready_f, got_f, state_f, ready_n, got_n, state_n, om_ref, post_f, post_n, out_f, out_n):
    def body(r):
        for p, ready, got, state, post, out_ref in (
            (FAR, ready_f, got_f, state_f, post_f, out_f),
            (NEAR, ready_n, got_n, state_n, post_n, out_n),
        ):
            f = edge_values(ready, got, p, r, 1)
            *u, rho = get(state, r, count=4)
            out = relaxed(f, rho, u, om_ref[p, block(r), :])
            put(post, out, r)
            put_crossing(out_ref, out, p, r, 1)

    loop(body)


def finish(
    far, inner, near, om_ref, u_ref, post_f, post_i, post_n, other_f, other_n,
    grad, ready_f, ready_n, final, hold_1, hold_2, hold, sem_1, sem_2, sem,
):
    flip, parts, m = flipped(), (far, inner, near), iotas()
    posts, places = (post_f, post_i, post_n), ((1, hold_1, sem_1), (2, hold_2, sem_2))

    def body(r):
        for i, (p, keep, done) in enumerate(places):
            mu = pull_local(parts, p, r, -1, m)
            out = adjoint(mu, get(u_ref, r, (i,), 3), om_ref[p, block(r), :])
            put_mirrored(keep, out, flip, r)
            write_out(keep, grad, done, flip, p, r).start()
        for p, ready in ((FAR, ready_f), (NEAR, ready_n)):
            put(ready, pull_local(parts, p, r, -1, m), r)

    def stream(r):
        for p in range(PLANES):
            f = pull_local(posts, p, r, 1, m)
            if p not in INNER:
                pull_remote(other_f if p == FAR else other_n, f, p, r, 1, m)
            put_native(hold, f, flip, p, r)
        moved(hold, final, sem, r).start()

    def wait(r):
        for p, keep, done in places:
            write_out(keep, grad, done, flip, p, r).wait()
        moved(hold, final, sem, r).wait()

    loop(body, STEP)
    loop(stream, STEP)
    loop(wait)


def adjoint_edge_last(p):
    def adjoint_edge_last(ready, other, om_ref, u_ref, partial, grad, hold, sem, got):
        flip = flipped()
        receive(other, got, p, -1)

        def body(r):
            mu = edge_values(ready, got, p, r, -1)
            out = adjoint(mu, get(u_ref, r, count=3), om_ref[p, block(r), :])
            put_mirrored(hold, out, flip, r)

        def both(r):
            for j in range(2):
                body(2 * r + j)
            for j in range(2):
                write_out(hold, grad, sem, flip, p, 2 * r + j).start()

        lax.fori_loop(0, BLOCKS // 2, lambda r, c: (both(r), c)[1], 0)
        loop(lambda r: write_out(hold, grad, sem, flip, p, r).wait())

    return adjoint_edge_last


INSIDE = pl.BlockSpec(memory_space=pltpu.VMEM)
OUTSIDE = pl.BlockSpec(memory_space=pltpu.HBM)
STEP = 2
INNERS = (19, 2, ROWS, LANES)
PLANE = (19, ROWS, LANES)
RELAX = (PLANES, ROWS, LANES)
CROSS = (5, ROWS, LANES)
NATIVE = (19, PLANES * ROWS, LANES)
RESULT = (19, ROWS, PLANES, LANES)
SEMS = pltpu.SemaphoreType.DMA((BLOCKS,))
GOT = [pltpu.VMEM(CROSS, F32)]


def kernel(body, outs, scratch=(), aliases=None):
    def call(*args):
        args = [x if isinstance(x, tuple) else (x, 1) for x in args]
        return pl.pallas_call(
            body,
            in_specs=[INSIDE if inside else OUTSIDE for _, inside in args],
            out_specs=[INSIDE if inside else OUTSIDE for _, inside in outs],
            out_shape=[
                pltpu.VMEM(s, F32) if inside else jax.ShapeDtypeStruct(s, F32) for s, inside in outs
            ],
            scratch_shapes=list(scratch),
            input_output_aliases=aliases or {},
            compiler_params=pltpu.CompilerParams(vmem_limit_bytes=8 * 2**20),
            name=body.__name__,
        )(
            *[
                pltpu.with_memory_space_constraint(x, pltpu.VMEM if inside else pltpu.HBM)
                for x, inside in args
            ]
        )

    return call


def local(populations, relax_class, cotangent):
    count = lax.axis_size("gx")
    near_pairs = [(i, i ^ 1) for i in range(count)]
    far_pairs = [(i, (i + 1 if i % 2 else i - 1) % count) for i in range(count)]

    def exchange(far, near):
        near = lax.ppermute(near, "gx", near_pairs)
        return lax.ppermute(far, "gx", far_pairs), near

    def to_native(x):
        lead = x.shape[:-2]
        x = x.reshape(lead + (PLANES, ROWS, LANES))
        return jnp.swapaxes(x, -3, -2).reshape(lead + (PLANES * ROWS, LANES))

    pops, classes, cot = to_native(populations), to_native(relax_class), to_native(cotangent)
    inners, plane, cross = (INNERS, 1), (PLANE, 1), (CROSS, 1)
    speed, speeds, state = ((3, ROWS, LANES), 1), ((3, 2, ROWS, LANES), 1), ((4, ROWS, LANES), 1)
    held, om, post_f, post_n, u0_f, u0_n, far, near = kernel(
        first_edges,
        [(NATIVE, 1), (RELAX, 1), plane, plane, speed, speed, cross, cross],
        [pltpu.VMEM(classes.shape, jnp.int32), SEMS, pltpu.SemaphoreType.DMA],
    )((pops, 0), (classes, 0))
    far, near = exchange(far, near)
    post_i, u0_i = kernel(first_inner, [inners, speeds])(held, om)
    cot_f, cot_i, cot_n, cfar, cnear = kernel(cotangent_planes, [plane, inners, plane, cross, cross])(
        cot
    )
    cfar, cnear = exchange(cfar, cnear)
    inner = kernel(forward_inner, [inners, speeds, plane, plane])
    edge = [kernel(forward_edge(p), [plane, speed, cross], GOT) for p in (FAR, NEAR)]

    post_i, u1_i, ready_f, ready_n = inner(post_f, post_i, post_n, om)
    post_n, u1_n, near = edge[1](ready_n, near, om)
    post_f, u1_f, far = edge[0](ready_f, far, om)
    far, near = exchange(far, near)
    post_i, u2_i, ready_f, ready_n = inner(post_f, post_i, post_n, om)
    lam_i, mus_f, mus_n = kernel(adjoint_top, [inners, plane, plane])(
        cot_f, cot_i, cot_n, om, u2_i, cfar, cnear
    )
    turn = [kernel(turn_edge(p), [plane, cross, cross, state]) for p in (FAR, NEAR)]
    lam_n, near, got_n, state_n = turn[1](ready_n, near, om, mus_n)
    lam_f, far, got_f, state_f = turn[0](ready_f, far, om, mus_f)
    far, near = exchange(far, near)
    post_f, post_n, pfar, pnear = kernel(relax_edges, [plane, plane, cross, cross])(
        ready_f, got_f, state_f, ready_n, got_n, state_n, om
    )
    lam_i, ready_f, ready_n = kernel(adjoint_inner, [inners, plane, plane])(
        lam_f, lam_i, lam_n, om, u1_i
    )
    pfar, pnear, ready_f = lax.optimization_barrier((pfar, pnear, ready_f))
    pfar, pnear = exchange(pfar, pnear)
    edge = [kernel(adjoint_edge(p), [plane, cross], GOT) for p in (FAR, NEAR)]
    lam_n, near = edge[1](ready_n, near, om, u1_n)
    lam_f, far = edge[0](ready_f, far, om, u1_f)
    far, near = exchange(far, near)
    holds = [pltpu.VMEM(PLANE, F32), pltpu.VMEM(PLANE, F32), pltpu.VMEM(NATIVE, F32), SEMS, SEMS, SEMS]
    grad, ready_f, ready_n, final = kernel(finish, [(RESULT, 0), plane, plane, (NATIVE, 0)], holds)(
        lam_f, lam_i, lam_n, om, u0_i, post_f, post_i, post_n, pfar, pnear
    )
    scratch = [pltpu.VMEM(PLANE, F32), SEMS] + GOT
    last = [kernel(adjoint_edge_last(p), [(RESULT, 0)], scratch, {4: 0}) for p in (FAR, NEAR)]
    (grad,) = last[1](ready_n, near, om, u0_n, (grad, 0))
    (grad,) = last[0](ready_f, far, om, u0_f, (grad, 0))
    final = jnp.swapaxes(final.reshape(19, ROWS, PLANES, LANES), 1, 2)
    return final.reshape(populations.shape), jnp.swapaxes(grad, 1, 2).reshape(populations.shape)


def solution(mesh):
    return jax.shard_map(
        local,
        mesh=mesh,
        in_specs=(
            P(None, ("groups", "gx"), None),
            P(("groups", "gx"), None),
            P(None, ("groups", "gx"), None),
        ),
        out_specs=(P(None, ("groups", "gx"), None), P(None, ("groups", "gx"), None)),
        check_vma=False,
    )
```

time: 40.2 us -> 41.2 us (1.025)
  starting transfers between devices: 19.7 us -> 20.7 us
    ppermute x6, starting transfers between devices: 0.26 us -> 1.78 us  [exchange(): near = lax.ppermute(near, 'gx', near_pairs)]
    ppermute x6, starting transfers between devices: 19.4 us -> 18.9 us  [exchange(): return (lax.ppermute(far, 'gx', far_pairs), near)]
    pallas_call x13 -> x17, Pallas kernels: 17.7 us -> 17.6 us  [call(): pl.pallas_call(body, in_specs=[INSIDE if inside else OUTSIDE for _, insid...]
  transfers between devices with their start and end apart: 12 -> 12, of which waited for: 2 -> 3; matrix products, arithmetic and copies ran while one was open for 0% -> 0% of each run, Pallas kernels for 31% -> 35%
where the time goes in v3:
time: 41.2 us; the launch traced here: 41.1 us
  starting transfers between devices  20.7 us (50%)
  Pallas kernels  17.6 us (43%)
  waiting for transfers between devices  1.93 us (5%)
  between operations  0.83 us (2%)
    ppermute x6, starting transfers between devices, exchange(): return (lax.ppermute(far, 'gx', far_pairs), near)  18.9 us
    pallas_call x17, Pallas kernels, call(): pl.pallas_call(body, in_specs=[INSIDE if inside else OUTSIDE for _, insid...  17.6 us
    ppermute x6, waiting for transfers between devices, exchange(): return (lax.ppermute(far, 'gx', far_pairs), near)  1.92 us
    ppermute x6, starting transfers between devices, exchange(): near = lax.ppermute(near, 'gx', near_pairs)  1.78 us
  transfers between devices with their start and end apart: 12, of which 3 were waited for; matrix products, arithmetic and copies ran while one was open for 0% of the time, Pallas kernels for 35%

profile of v3, /device:TPU:0, one launch (start us, length us, event | category | flops | bytes accessed | tf_op | source)
XLA Modules:
  0.0 41.1 jit_solution(5262485958807715449)
XLA Ops:
  0.6 2.0 %first_edges.1 = (f32[19,256,128]{2,1,0:T(8,128)S(1)}, f32[4,64,128]{2,1,0:T(8,128)S(1)}, f32[19,64,128]{2,1,0:T(8,128)S(1)}, f32[19,64,128]{2,1,0:T(8,128)S(1)}...) custom-call(f32[19,256,128]{2,1,0:T(8,128)} %bitcast.25, ...), custom_call_target="tpu_custom_call" | custom-call | tf_op jit(solution)/shard_map/first_edges/pallas_call | solution.py:473
  2.6 0.5 %collective-permute-start.1 = (f32[5,64,128]{2,1,0:T(8,128)S(1)}, f32[5,64,128]{2,1,0:T(8,128)S(1)}, u32[]{:S(2)}, u32[]{:S(2)}) collective-permute-start(f32[5,64,128]{2,1,0:T(8,128)S(1)} %get-tuple-element.70), channel_id=1, source_target_pairs={{0,1},{1,0},{2,3},{3,2},{4,5},{5,4},{6,7},{7,6},{8,9},{9,8},{10,11... | collective-permute-start | bytes 491528 | tf_op jit(solution)/shard_map/ppermute | solution.py:500
  3.2 5.6 %collective-permute-start = (f32[5,64,128]{2,1,0:T(8,128)S(1)}, f32[5,64,128]{2,1,0:T(8,128)S(1)}, u32[]{:S(2)}, u32[]{:S(2)}) collective-permute-start(f32[5,64,128]{2,1,0:T(8,128)S(1)} %get-tuple-element.66), channel_id=1, source_target_pairs={{0,15},{1,2},{2,1},{3,4},{4,3},{5,6},{6,5},{7,8},{8,7},{9,10},{10,... | collective-permute-start | bytes 491528 | tf_op jit(solution)/shard_map/ppermute | solution.py:501
  8.8 0.5 %cotangent_planes.1 = (f32[19,64,128]{2,1,0:T(8,128)S(1)}, f32[19,2,64,128]{3,2,1,0:T(8,128)S(1)}, f32[19,64,128]{2,1,0:T(8,128)S(1)}, f32[5,64,128]{2,1,0:T(8,128)S(1)}, f32[5,64,128]{2,1,0:T(8,128)S(1)}) custom-call(f32[19,256,128]{2,1,0:T(8,128)S(1)} %bitcast.23), custom_call_target="tpu_custom_call" | custom-call | tf_op jit(solution)/shard_map/cotangent_planes/pallas_call | solution.py:473
  9.4 0.5 %first_inner.1 = (f32[19,2,64,128]{3,2,1,0:T(8,128)S(1)}, f32[3,2,64,128]{3,2,1,0:T(8,128)S(1)}) custom-call(f32[19,256,128]{2,1,0:T(8,128)S(1)} %get-tuple-element.61.held, f32[4,64,128]{2,1,0:T(8,128)S(1)} %get-tuple-element.62.om_ref), custom_call_target="tpu_custom_call" | custom-call | tf_op jit(solution)/shard_map/first_inner/pallas_call | solution.py:473
  10.0 1.2 %forward_inner.2 = (f32[19,2,64,128]{3,2,1,0:T(8,128)S(1)}, f32[3,2,64,128]{3,2,1,0:T(8,128)S(1)}, f32[19,64,128]{2,1,0:T(8,128)S(1)}, f32[19,64,128]{2,1,0:T(8,128)S(1)}) custom-call(f32[19,64,128]{2,1,0:T(8,128)S(1)} %get-tuple-element.60.far, f32[19,2,64,128]{3,2,1,0:T(8,128)S(1)} %get-tuple-element.63.inner, f32[19,64,128]{2,1,0:T(8,128)S(1)} %get-tuple-element.64.near, ...), custom_call_target="tpu_custom_call" | custom-call | tf_op jit(solution)/shard_map/forward_inner/pallas_call | solution.py:473
  11.6 0.5 %collective-permute-start.5 = (f32[5,64,128]{2,1,0:T(8,128)S(1)}, f32[5,64,128]{2,1,0:T(8,128)S(1)}, u32[]{:S(2)}, u32[]{:S(2)}) collective-permute-start(f32[5,64,128]{2,1,0:T(8,128)S(1)} %get-tuple-element.84), channel_id=1, source_target_pairs={{0,1},{1,0},{2,3},{3,2},{4,5},{5,4},{6,7},{7,6},{8,9},{9,8},{10,11... | collective-permute-start | bytes 491528 | tf_op jit(solution)/shard_map/ppermute | solution.py:500
  12.5 4.4 %collective-permute-start.2 = (f32[5,64,128]{2,1,0:T(8,128)S(1)}, f32[5,64,128]{2,1,0:T(8,128)S(1)}, u32[]{:S(2)}, u32[]{:S(2)}) collective-permute-start(f32[5,64,128]{2,1,0:T(8,128)S(1)} %get-tuple-element.73), channel_id=1, source_target_pairs={{0,15},{1,2},{2,1},{3,4},{4,3},{5,6},{6,5},{7,8},{8,7},{9,10},{10,... | collective-permute-start | bytes 491528 | tf_op jit(solution)/shard_map/ppermute | solution.py:501
  16.9 1.2 %forward_inner.3 = (f32[19,2,64,128]{3,2,1,0:T(8,128)S(1)}, f32[3,2,64,128]{3,2,1,0:T(8,128)S(1)}, f32[19,64,128]{2,1,0:T(8,128)S(1)}, f32[19,64,128]{2,1,0:T(8,128)S(1)}) custom-call(f32[19,64,128]{2,1,0:T(8,128)S(1)} %get-tuple-element.67.far, f32[19,2,64,128]{3,2,1,0:T(8,128)S(1)} %get-tuple-element.68.inner, f32[19,64,128]{2,1,0:T(8,128)S(1)} %get-tuple-element.71.near, ...), custom_call_target="tpu_custom_call" | custom-call | tf_op jit(solution)/shard_map/forward_inner/pallas_call | solution.py:473
  18.1 1.3 %adjoint_top.1 = (f32[19,2,64,128]{3,2,1,0:T(8,128)S(1)}, f32[19,64,128]{2,1,0:T(8,128)S(1)}, f32[19,64,128]{2,1,0:T(8,128)S(1)}) custom-call(f32[19,64,128]{2,1,0:T(8,128)S(1)} %get-tuple-element.74.far, f32[19,2,64,128]{3,2,1,0:T(8,128)S(1)} %get-tuple-element.75.inner, f32[19,64,128]{2,1,0:T(8,128)S(1)} %get-tuple-element.76.near, ...), custom_call_target="tpu_custom_call" | custom-call | tf_op jit(solution)/shard_map/adjoint_top/pallas_call | solution.py:473
  19.4 0.5 %turn_edge.3 = (f32[19,64,128]{2,1,0:T(8,128)S(1)}, f32[5,64,128]{2,1,0:T(8,128)S(1)}, f32[5,64,128]{2,1,0:T(8,128)S(1)}, f32[4,64,128]{2,1,0:T(8,128)S(1)}) custom-call(f32[19,64,128]{2,1,0:T(8,128)S(1)} %get-tuple-element.83.ready.ready_n, f32[5,64,128]{2,1,0:T(8,128)S(1)} %collective-permute-done.5.other, f32[4,64,128]{2,1,0:T(8,128)S(1)} %get-tuple-element.62.om_ref, ...), custom_call_target="tpu_custom_call" | custom-call | tf_op jit(solution)/shard_map/turn_edge/pallas_call | solution.py:473
  20.1 0.5 %turn_edge.2 = (f32[19,64,128]{2,1,0:T(8,128)S(1)}, f32[5,64,128]{2,1,0:T(8,128)S(1)}, f32[5,64,128]{2,1,0:T(8,128)S(1)}, f32[4,64,128]{2,1,0:T(8,128)S(1)}) custom-call(f32[19,64,128]{2,1,0:T(8,128)S(1)} %get-tuple-element.72.ready.ready_f, f32[5,64,128]{2,1,0:T(8,128)S(1)} %collective-permute-done.2.other, f32[4,64,128]{2,1,0:T(8,128)S(1)} %get-tuple-element.62.om_ref, ...), custom_call_target="tpu_custom_call" | custom-call | tf_op jit(solution)/shard_map/turn_edge/pallas_call | solution.py:473
  20.6 4.3 %collective-permute-start.6 = (f32[5,64,128]{2,1,0:T(8,128)S(1)}, f32[5,64,128]{2,1,0:T(8,128)S(1)}, u32[]{:S(2)}, u32[]{:S(2)}) collective-permute-start(f32[5,64,128]{2,1,0:T(8,128)S(1)} %get-tuple-element.96), channel_id=1, source_target_pairs={{0,15},{1,2},{2,1},{3,4},{4,3},{5,6},{6,5},{7,8},{8,7},{9,10},{10,... | collective-permute-start | bytes 491528 | tf_op jit(solution)/shard_map/ppermute | solution.py:501
  24.9 0.4 relax_edges.1
  25.3 1.2 %adjoint_inner.1 = (f32[19,2,64,128]{3,2,1,0:T(8,128)S(1)}, f32[19,64,128]{2,1,0:T(8,128)S(1)}, f32[19,64,128]{2,1,0:T(8,128)S(1)}) custom-call(f32[19,64,128]{2,1,0:T(8,128)S(1)} %get-tuple-element.90.far, f32[19,2,64,128]{3,2,1,0:T(8,128)S(1)} %get-tuple-element.91.inner, f32[19,64,128]{2,1,0:T(8,128)S(1)} %get-tuple-element.92.near, ...), custom_call_target="tpu_custom_call" | custom-call | tf_op jit(solution)/shard_map/adjoint_inner/pallas_call | solution.py:473
  26.7 0.4 adjoint_edge.3
  27.1 0.6 %collective-permute-start.11 = (f32[5,64,128]{2,1,0:T(8,128)S(1)}, f32[5,64,128]{2,1,0:T(8,128)S(1)}, u32[]{:S(2)}, u32[]{:S(2)}) collective-permute-start(f32[5,64,128]{2,1,0:T(8,128)S(1)} %get-tuple-element.115), channel_id=1, source_target_pairs={{0,1},{1,0},{2,3},{3,2},{4,5},{5,4},{6,7},{7,6},{8,9},{9,8},{10,11... | collective-permute-start | bytes 491528 | tf_op jit(solution)/shard_map/ppermute | solution.py:500
  27.7 0.5 %collective-permute-done.6.other = f32[5,64,128]{2,1,0:T(8,128)S(1)} collective-permute-done((f32[5,64,128]{2,1,0:T(8,128)S(1)}, f32[5,64,128]{2,1,0:T(8,128)S(1)}, u32[]{:S(2)}, u32[]{:S(2)}) %collective-permute-start.6) | collective-permute-done | bytes 163872 | tf_op jit(solution)/shard_map/ppermute | solution.py:501
  28.2 0.4 adjoint_edge.2
  28.6 4.2 %collective-permute-start.10 = (f32[5,64,128]{2,1,0:T(8,128)S(1)}, f32[5,64,128]{2,1,0:T(8,128)S(1)}, u32[]{:S(2)}, u32[]{:S(2)}) collective-permute-start(f32[5,64,128]{2,1,0:T(8,128)S(1)} %get-tuple-element.112), channel_id=1, source_target_pairs={{0,15},{1,2},{2,1},{3,4},{4,3},{5,6},{6,5},{7,8},{8,7},{9,10},{10,... | collective-permute-start | bytes 491528 | tf_op jit(solution)/shard_map/ppermute | solution.py:501
  32.8 1.3 %collective-permute-done.8.other_f = f32[5,64,128]{2,1,0:T(8,128)S(1)} collective-permute-done((f32[5,64,128]{2,1,0:T(8,128)S(1)}, f32[5,64,128]{2,1,0:T(8,128)S(1)}, u32[]{:S(2)}, u32[]{:S(2)}) %collective-permute-start.8) | collective-permute-done | bytes 163872 | tf_op jit(solution)/shard_map/ppermute | solution.py:501
  34.1 4.7 %finish.1 = (f32[19,64,4,128]{3,2,1,0:T(4,128)}, f32[19,64,128]{2,1,0:T(8,128)S(1)}, f32[19,64,128]{2,1,0:T(8,128)S(1)}, f32[19,256,128]{2,1,0:T(8,128)}) custom-call(f32[19,64,128]{2,1,0:T(8,128)S(1)} %get-tuple-element.98.far, f32[19,2,64,128]{3,2,1,0:T(8,128)S(1)} %get-tuple-element.99.inner, f32[19,64,128]{2,1,0:T(8,128)S(1)} %get-tuple-element.103.near, ...), custom_call_target="tpu_custom_call" | custom-call | tf_op jit(solution)/shard_map/finish/pallas_call | solution.py:473
  38.8 1.1 %adjoint_edge_last.2.partial = f32[19,64,4,128]{3,2,1,0:T(4,128)} custom-call(f32[19,64,128]{2,1,0:T(8,128)S(1)} %get-tuple-element.114.ready, f32[5,64,128]{2,1,0:T(8,128)S(1)} %collective-permute-done.11.other, f32[4,64,128]{2,1,0:T(8,128)S(1)} %get-tuple-element.62.om_ref, ...), custom_call_target="tpu_custom_call", output_to_operand_aliasing={{}: (4, {})} | custom-call | tf_op jit(solution)/shard_map/adjoint_edge_last/pallas_call | solution.py:473
  40.0 1.1 %adjoint_edge_last.3 = f32[19,64,4,128]{3,2,1,0:T(4,128)} custom-call(f32[19,64,128]{2,1,0:T(8,128)S(1)} %get-tuple-element.111.ready, f32[5,64,128]{2,1,0:T(8,128)S(1)} %collective-permute-done.10.other, f32[4,64,128]{2,1,0:T(8,128)S(1)} %get-tuple-element.62.om_ref, f32[3,64,128]{2,1,0:T(8,128)S(1)} %get-tuple-element.113.u_ref, ...), custom_call_target="tpu_custom_call", output_to_operand_aliasing={{}: (4, {})} | custom-call | tf_op jit(solution)/shard_map/adjoint_edge_last/pallas_call | solution.py:473
  (19 shorter events, 1.4 us)
Async XLA Ops:
  0.6 8.2 %copy-start = (f32[19,4,8192]{2,1,0:T(4,128)S(1)}, f32[19,4,8192]{2,1,0:T(4,128)}, u32[]{:S(2)}) copy-start(f32[19,4,8192]{2,1,0:T(4,128)} %param.5) | copy-start | bytes 7471108
  2.6 8.5 %collective-permute-start.1 = (f32[5,64,128]{2,1,0:T(8,128)S(1)}, f32[5,64,128]{2,1,0:T(8,128)S(1)}, u32[]{:S(2)}, u32[]{:S(2)}) collective-permute-start(f32[5,64,128]{2,1,0:T(8,128)S(1)} %get-tuple-element.70), channel_id=1, source_target_pairs={{0,1},{1,0},{2,3},{3,2},{4,5},{5,4},{6,7},{7,6},{8,9},{9,8},{10,11... | collective-permute-start | bytes 491528 | tf_op jit(solution)/shard_map/ppermute | solution.py:500
  3.2 8.9 %collective-permute-start = (f32[5,64,128]{2,1,0:T(8,128)S(1)}, f32[5,64,128]{2,1,0:T(8,128)S(1)}, u32[]{:S(2)}, u32[]{:S(2)}) collective-permute-start(f32[5,64,128]{2,1,0:T(8,128)S(1)} %get-tuple-element.66), channel_id=1, source_target_pairs={{0,15},{1,2},{2,1},{3,4},{4,3},{5,6},{6,5},{7,8},{8,7},{9,10},{10,... | collective-permute-start | bytes 491528 | tf_op jit(solution)/shard_map/ppermute | solution.py:501
  9.3 8.8 %collective-permute-start.3 = (f32[5,64,128]{2,1,0:T(8,128)S(1)}, f32[5,64,128]{2,1,0:T(8,128)S(1)}, u32[]{:S(2)}, u32[]{:S(2)}) collective-permute-start(f32[5,64,128]{2,1,0:T(8,128)S(1)} %get-tuple-element.78), channel_id=1, source_target_pairs={{0,15},{1,2},{2,1},{3,4},{4,3},{5,6},{6,5},{7,8},{8,7},{9,10},{10,... | collective-permute-start | bytes 491528 | tf_op jit(solution)/shard_map/ppermute | solution.py:501
  9.4 8.8 %collective-permute-start.4 = (f32[5,64,128]{2,1,0:T(8,128)S(1)}, f32[5,64,128]{2,1,0:T(8,128)S(1)}, u32[]{:S(2)}, u32[]{:S(2)}) collective-permute-start(f32[5,64,128]{2,1,0:T(8,128)S(1)} %get-tuple-element.79), channel_id=1, source_target_pairs={{0,1},{1,0},{2,3},{3,2},{4,5},{5,4},{6,7},{7,6},{8,9},{9,8},{10,11... | collective-permute-start | bytes 491528 | tf_op jit(solution)/shard_map/ppermute | solution.py:500
  11.6 7.9 %collective-permute-start.5 = (f32[5,64,128]{2,1,0:T(8,128)S(1)}, f32[5,64,128]{2,1,0:T(8,128)S(1)}, u32[]{:S(2)}, u32[]{:S(2)}) collective-permute-start(f32[5,64,128]{2,1,0:T(8,128)S(1)} %get-tuple-element.84), channel_id=1, source_target_pairs={{0,1},{1,0},{2,3},{3,2},{4,5},{5,4},{6,7},{7,6},{8,9},{9,8},{10,11... | collective-permute-start | bytes 491528 | tf_op jit(solution)/shard_map/ppermute | solution.py:500
  12.5 7.6 %collective-permute-start.2 = (f32[5,64,128]{2,1,0:T(8,128)S(1)}, f32[5,64,128]{2,1,0:T(8,128)S(1)}, u32[]{:S(2)}, u32[]{:S(2)}) collective-permute-start(f32[5,64,128]{2,1,0:T(8,128)S(1)} %get-tuple-element.73), channel_id=1, source_target_pairs={{0,15},{1,2},{2,1},{3,4},{4,3},{5,6},{6,5},{7,8},{8,7},{9,10},{10,... | collective-permute-start | bytes 491528 | tf_op jit(solution)/shard_map/ppermute | solution.py:501
  19.9 6.8 %collective-permute-start.7 = (f32[5,64,128]{2,1,0:T(8,128)S(1)}, f32[5,64,128]{2,1,0:T(8,128)S(1)}, u32[]{:S(2)}, u32[]{:S(2)}) collective-permute-start(f32[5,64,128]{2,1,0:T(8,128)S(1)} %get-tuple-element.101), channel_id=1, source_target_pairs={{0,1},{1,0},{2,3},{3,2},{4,5},{5,4},{6,7},{7,6},{8,9},{9,8},{10,11... | collective-permute-start | bytes 491528 | tf_op jit(solution)/shard_map/ppermute | solution.py:500
  20.6 7.6 %collective-permute-start.6 = (f32[5,64,128]{2,1,0:T(8,128)S(1)}, f32[5,64,128]{2,1,0:T(8,128)S(1)}, u32[]{:S(2)}, u32[]{:S(2)}) collective-permute-start(f32[5,64,128]{2,1,0:T(8,128)S(1)} %get-tuple-element.96), channel_id=1, source_target_pairs={{0,15},{1,2},{2,1},{3,4},{4,3},{5,6},{6,5},{7,8},{8,7},{9,10},{10,... | collective-permute-start | bytes 491528 | tf_op jit(solution)/shard_map/ppermute | solution.py:501
  26.5 7.6 %collective-permute-start.8 = (f32[5,64,128]{2,1,0:T(8,128)S(1)}, f32[5,64,128]{2,1,0:T(8,128)S(1)}, u32[]{:S(2)}, u32[]{:S(2)}) collective-permute-start(f32[5,64,128]{2,1,0:T(8,128)S(1)} %get-tuple-element.108), channel_id=1, source_target_pairs={{0,15},{1,2},{2,1},{3,4},{4,3},{5,6},{6,5},{7,8},{8,7},{9,10},{10,... | collective-permute-start | bytes 491528 | tf_op jit(solution)/shard_map/ppermute | solution.py:501
  26.7 7.4 %collective-permute-start.9 = (f32[5,64,128]{2,1,0:T(8,128)S(1)}, f32[5,64,128]{2,1,0:T(8,128)S(1)}, u32[]{:S(2)}, u32[]{:S(2)}) collective-permute-start(f32[5,64,128]{2,1,0:T(8,128)S(1)} %get-tuple-element.109), channel_id=1, source_target_pairs={{0,1},{1,0},{2,3},{3,2},{4,5},{5,4},{6,7},{7,6},{8,9},{9,8},{10,11... | collective-permute-start | bytes 491528 | tf_op jit(solution)/shard_map/ppermute | solution.py:500
  27.1 11.7 %collective-permute-start.11 = (f32[5,64,128]{2,1,0:T(8,128)S(1)}, f32[5,64,128]{2,1,0:T(8,128)S(1)}, u32[]{:S(2)}, u32[]{:S(2)}) collective-permute-start(f32[5,64,128]{2,1,0:T(8,128)S(1)} %get-tuple-element.115), channel_id=1, source_target_pairs={{0,1},{1,0},{2,3},{3,2},{4,5},{5,4},{6,7},{7,6},{8,9},{9,8},{10,11... | collective-permute-start | bytes 491528 | tf_op jit(solution)/shard_map/ppermute | solution.py:500
  28.6 11.4 %collective-permute-start.10 = (f32[5,64,128]{2,1,0:T(8,128)S(1)}, f32[5,64,128]{2,1,0:T(8,128)S(1)}, u32[]{:S(2)}, u32[]{:S(2)}) collective-permute-start(f32[5,64,128]{2,1,0:T(8,128)S(1)} %get-tuple-element.112), channel_id=1, source_target_pairs={{0,15},{1,2},{2,1},{3,4},{4,3},{5,6},{6,5},{7,8},{8,7},{9,10},{10,... | collective-permute-start | bytes 491528 | tf_op jit(solution)/shard_map/ppermute | solution.py:501

commit v4 on v3

--- a/solution.py
+++ b/solution.py
@@ -167,10 +167,22 @@
     return rho, [jx * inv, jy * inv, jz * inv]
 
 
+def by_side(run):
+    side = lax.rem(lax.axis_index("gx"), 2)
+    for flip in (0, 1):
+        pl.when(side == flip)(lambda flip=flip: run(flip))
+
+
 def native(flip, k, p, r):
-    kk = k if MIRROR[k] == k else jnp.where(flip == 1, MIRROR[k], k)
-    x = jnp.where(flip == 1, PLANES - 1 - p, p)
-    return kk, pl.ds(r * (8 * PLANES) + x, 8, stride=PLANES)
+    return mirrored(flip, k), pl.ds(r * (8 * PLANES) + place(flip, p), 8, stride=PLANES)
+
+
+def mirrored(flip, k):
+    return MIRROR[k] if flip else k
+
+
+def place(flip, p):
+    return PLANES - 1 - p if flip else p
 
 
 def get_native(ref, flip, p, r):
@@ -189,8 +201,7 @@
 
 def put_mirrored(hold, values, flip, r, i=()):
     for k in range(19):
-        kk = k if MIRROR[k] == k else jnp.where(flip == 1, MIRROR[k], k)
-        hold[(kk,) + i + (block(r), slice(None))] = values[k]
+        hold[(mirrored(flip, k),) + i + (block(r), slice(None))] = values[k]
 
 
 def loop(body, step=1):
@@ -211,69 +222,64 @@
     return pltpu.make_async_copy(chunk(source, r), chunk(target, r), sem.at[r])
 
 
-def write_out(hold, result, sem, flip, p, r):
-    x = jnp.where(flip == 1, PLANES - 1 - p, p)
-    return pltpu.make_async_copy(hold.at[:, block(r), :], result.at[:, block(r), x, :], sem.at[r])
-
-
-def flipped():
-    return lax.rem(lax.axis_index("gx"), 2)
-
-
 def first_edges(
     pops, classes, held, om_ref, post_f, post_n, u_f, u_n, far_out, near_out, cls_ref, sem, cls_sem
 ):
-    flip = flipped()
     fetch = pltpu.make_async_copy(classes, cls_ref, cls_sem)
     fetch.start()
     loop(lambda r: moved(pops, held, sem, r).start())
     fetch.wait()
 
-    def body(r):
-        moved(pops, held, sem, r).wait()
-        for p in range(PLANES):
-            cls = cls_ref[native(flip, 0, p, r)[1], :]
-            om = jnp.full((8, LANES), RATES[0], F32)
-            for entry in range(1, 4):
-                om = jnp.where(cls == entry, RATES[entry], om)
-            om_ref[p, block(r), :] = om
-            if p in INNER:
-                continue
-            f = get_native(held, flip, p, r)
-            rho, u = state_of(f)
-            put(u_f if p == FAR else u_n, u, r)
-            out = relaxed(f, rho, u, om)
-            put(post_f if p == FAR else post_n, out, r)
-            put_crossing(far_out if p == FAR else near_out, out, p, r, 1)
-
-    loop(body)
+    def run(flip):
+        def body(r):
+            moved(pops, held, sem, r).wait()
+            for p in range(PLANES):
+                cls = cls_ref[native(flip, 0, p, r)[1], :]
+                om = jnp.full((8, LANES), RATES[0], F32)
+                for entry in range(1, 4):
+                    om = jnp.where(cls == entry, RATES[entry], om)
+                om_ref[p, block(r), :] = om
+                if p in INNER:
+                    continue
+                f = get_native(held, flip, p, r)
+                rho, u = state_of(f)
+                put(u_f if p == FAR else u_n, u, r)
+                out = relaxed(f, rho, u, om)
+                put(post_f if p == FAR else post_n, out, r)
+                put_crossing(far_out if p == FAR else near_out, out, p, r, 1)
+
+        loop(body)
+
+    by_side(run)
 
 
 def first_inner(held, om_ref, post, u_ref):
-    flip = flipped()
-
-    def body(r):
-        for i, p in enumerate(INNER):
-            f = get_native(held, flip, p, r)
-            rho, u = state_of(f)
-            put(u_ref, u, r, (i,))
-            put(post, relaxed(f, rho, u, om_ref[p, block(r), :]), r, (i,))
-
-    loop(body)
+    def run(flip):
+        def body(r):
+            for i, p in enumerate(INNER):
+                f = get_native(held, flip, p, r)
+                rho, u = state_of(f)
+                put(u_ref, u, r, (i,))
+                put(post, relaxed(f, rho, u, om_ref[p, block(r), :]), r, (i,))
+
+        loop(body)
+
+    by_side(run)
 
 
 def cotangent_planes(cot, far, inner, near, far_out, near_out):
-    flip = flipped()
-
-    def body(r):
-        for p in range(PLANES):
-            values = get_native(cot, flip, p, r)
-            ref, i = plane_of((far, inner, near), p)
-            put(ref, values, r, i)
-            if p not in INNER:
-                put_crossing(far_out if p == FAR else near_out, values, p, r, -1)
-
-    loop(body)
+    def run(flip):
+        def body(r):
+            for p in range(PLANES):
+                values = get_native(cot, flip, p, r)
+                ref, i = plane_of((far, inner, near), p)
+                put(ref, values, r, i)
+                if p not in INNER:
+                    put_crossing(far_out if p == FAR else near_out, values, p, r, -1)
+
+        loop(body)
+
+    by_side(run)
 
 
 def forward_inner(far, inner, near, om_ref, post, u_ref, ready_f, ready_n):
@@ -306,11 +312,19 @@
     return values
 
 
-def forward_edge(p):
-    def forward_edge(ready, other, om_ref, post, u_ref, out_ref, got):
+def forward_edges(
+    ready_f, ready_n, far, near, om_ref,
+    post_f, post_n, u_f, u_n, out_f, out_n, got_f, got_n,
+):
+    sides = (
+        (FAR, ready_f, far, post_f, u_f, out_f, got_f),
+        (NEAR, ready_n, near, post_n, u_n, out_n, got_n),
+    )
+    for p, _, other, _, _, _, got in sides:
         receive(other, got, p, 1)
 
-        def body(r):
+    def body(r):
+        for p, ready, _, post, u_ref, out_ref, got in sides:
             f = edge_values(ready, got, p, r, 1)
             rho, u = state_of(f)
             put(u_ref, u, r)
@@ -318,9 +332,7 @@
             put(post, out, r)
             put_crossing(out_ref, out, p, r, 1)
 
-        loop(body, 2)
-
-    return forward_edge
+    loop(body)
 
 
 def adjoint_planes(parts, om_ref, u_ref, lam, r, m):
@@ -399,59 +411,85 @@
 
 
 def finish(
-    far, inner, near, om_ref, u_ref, post_f, post_i, post_n, other_f, other_n,
-    grad, ready_f, ready_n, final, hold_1, hold_2, hold, sem_1, sem_2, sem,
+    far, inner, near, om_ref, u_ref, un_ref, other, post_f, post_i, post_n, other_f, other_n,
+    grad, ready_f, final, flat, hold, sem, hold_sem, near_sem, lam, ready_n, got,
 ):
-    flip, parts, m = flipped(), (far, inner, near), iotas()
-    posts, places = (post_f, post_i, post_n), ((1, hold_1, sem_1), (2, hold_2, sem_2))
+    parts, posts, m = (far, inner, near), (post_f, post_i, post_n), iotas()
+
+    def run(flip):
+        def copy(i, p):
+            return pltpu.make_async_copy(
+                lam.at[:, i], grad.at[:, :, place(flip, p), :], hold_sem.at[i]
+            )
+
+        def stream(r):
+            for p in range(PLANES):
+                f = pull_local(posts, p, r, 1, m)
+                if p not in INNER:
+                    pull_remote(other_f if p == FAR else other_n, f, p, r, 1, m)
+                put_native(flat, f, flip, p, r)
+
+        def streams(r, carry):
+            for j in range(STEP):
+                stream(STEP * r + j)
+            for j in range(STEP):
+                moved(flat, final, sem, STEP * r + j).start()
+            return carry
+
+        def body(r):
+            for i, p in enumerate(INNER):
+                mu = pull_local(parts, p, r, -1, m)
+                out = adjoint(mu, get(u_ref, r, (i,), 3), om_ref[p, block(r), :])
+                put_mirrored(lam, out, flip, r, (i,))
+            for p, ready in ((FAR, ready_f), (NEAR, ready_n)):
+                put(ready, pull_local(parts, p, r, -1, m), r)
+
+        lax.fori_loop(0, BLOCKS // STEP, streams, 0)
+        loop(body, STEP)
+        for i, p in enumerate(INNER):
+            copy(i, p).start()
+        receive(other, got, NEAR, -1)
+        edge_last(ready_n, got, om_ref, un_ref, grad, hold, near_sem, NEAR, flip)
+        for i, p in enumerate(INNER):
+            copy(i, p).wait()
+        loop(lambda r: moved(flat, final, sem, r).wait())
+
+    by_side(run)
+
+
+def edge_last(ready, got, om_ref, u_ref, grad, hold, sem, p, flip):
+    half = ROWS // 2
+
+    def copy(i):
+        rows = pl.ds(i * half, half)
+        return pltpu.make_async_copy(
+            hold.at[:, rows, :], grad.at[:, rows, place(flip, p), :], sem.at[i]
+        )
 
     def body(r):
-        for i, (p, keep, done) in enumerate(places):
-            mu = pull_local(parts, p, r, -1, m)
-            out = adjoint(mu, get(u_ref, r, (i,), 3), om_ref[p, block(r), :])
-            put_mirrored(keep, out, flip, r)
-            write_out(keep, grad, done, flip, p, r).start()
-        for p, ready in ((FAR, ready_f), (NEAR, ready_n)):
-            put(ready, pull_local(parts, p, r, -1, m), r)
-
-    def stream(r):
-        for p in range(PLANES):
-            f = pull_local(posts, p, r, 1, m)
-            if p not in INNER:
-                pull_remote(other_f if p == FAR else other_n, f, p, r, 1, m)
-            put_native(hold, f, flip, p, r)
-        moved(hold, final, sem, r).start()
-
-    def wait(r):
-        for p, keep, done in places:
-            write_out(keep, grad, done, flip, p, r).wait()
-        moved(hold, final, sem, r).wait()
-
-    loop(body, STEP)
-    loop(stream, STEP)
-    loop(wait)
-
-
-def adjoint_edge_last(p):
-    def adjoint_edge_last(ready, other, om_ref, u_ref, partial, grad, hold, sem, got):
-        flip = flipped()
-        receive(other, got, p, -1)
-
-        def body(r):
-            mu = edge_values(ready, got, p, r, -1)
-            out = adjoint(mu, get(u_ref, r, count=3), om_ref[p, block(r), :])
-            put_mirrored(hold, out, flip, r)
-
-        def both(r):
-            for j in range(2):
-                body(2 * r + j)
-            for j in range(2):
-                write_out(hold, grad, sem, flip, p, 2 * r + j).start()
-
-        lax.fori_loop(0, BLOCKS // 2, lambda r, c: (both(r), c)[1], 0)
-        loop(lambda r: write_out(hold, grad, sem, flip, p, r).wait())
-
-    return adjoint_edge_last
+        mu = edge_values(ready, got, p, r, -1)
+        out = adjoint(mu, get(u_ref, r, count=3), om_ref[p, block(r), :])
+        put_mirrored(hold, out, flip, r)
+
+    def pairs(first):
+        def pair(r, carry):
+            body(first + 2 * r)
+            body(first + 2 * r + 1)
+            return carry
+
+        lax.fori_loop(0, BLOCKS // 4, pair, 0)
+
+    pairs(0)
+    copy(0).start()
+    pairs(BLOCKS // 2)
+    copy(1).start()
+    copy(0).wait()
+    copy(1).wait()
+
+
+def far_last(ready, other, om_ref, u_ref, partial, grad, hold, sem, got):
+    receive(other, got, FAR, -1)
+    by_side(lambda flip: edge_last(ready, got, om_ref, u_ref, grad, hold, sem, FAR, flip))
 
 
 INSIDE = pl.BlockSpec(memory_space=pltpu.VMEM)
@@ -479,7 +517,7 @@
             ],
             scratch_shapes=list(scratch),
             input_output_aliases=aliases or {},
-            compiler_params=pltpu.CompilerParams(vmem_limit_bytes=8 * 2**20),
+            compiler_params=pltpu.CompilerParams(vmem_limit_bytes=12 * 2**20),
             name=body.__name__,
         )(
             *[
@@ -513,18 +551,19 @@
         [(NATIVE, 1), (RELAX, 1), plane, plane, speed, speed, cross, cross],
         [pltpu.VMEM(classes.shape, jnp.int32), SEMS, pltpu.SemaphoreType.DMA],
     )((pops, 0), (classes, 0))
+    cot, far, near = lax.optimization_barrier((cot, far, near))
     far, near = exchange(far, near)
-    post_i, u0_i = kernel(first_inner, [inners, speeds])(held, om)
     cot_f, cot_i, cot_n, cfar, cnear = kernel(cotangent_planes, [plane, inners, plane, cross, cross])(
         cot
     )
     cfar, cnear = exchange(cfar, cnear)
+    post_i, u0_i = kernel(first_inner, [inners, speeds])(held, om)
     inner = kernel(forward_inner, [inners, speeds, plane, plane])
-    edge = [kernel(forward_edge(p), [plane, speed, cross], GOT) for p in (FAR, NEAR)]
 
     post_i, u1_i, ready_f, ready_n = inner(post_f, post_i, post_n, om)
-    post_n, u1_n, near = edge[1](ready_n, near, om)
-    post_f, u1_f, far = edge[0](ready_f, far, om)
+    post_f, post_n, u1_f, u1_n, far, near = kernel(
+        forward_edges, [plane, plane, speed, speed, cross, cross], GOT + GOT
+    )(ready_f, ready_n, far, near, om)
     far, near = exchange(far, near)
     post_i, u2_i, ready_f, ready_n = inner(post_f, post_i, post_n, om)
     lam_i, mus_f, mus_n = kernel(adjoint_top, [inners, plane, plane])(
@@ -540,20 +579,22 @@
     lam_i, ready_f, ready_n = kernel(adjoint_inner, [inners, plane, plane])(
         lam_f, lam_i, lam_n, om, u1_i
     )
-    pfar, pnear, ready_f = lax.optimization_barrier((pfar, pnear, ready_f))
     pfar, pnear = exchange(pfar, pnear)
     edge = [kernel(adjoint_edge(p), [plane, cross], GOT) for p in (FAR, NEAR)]
     lam_n, near = edge[1](ready_n, near, om, u1_n)
     lam_f, far = edge[0](ready_f, far, om, u1_f)
     far, near = exchange(far, near)
-    holds = [pltpu.VMEM(PLANE, F32), pltpu.VMEM(PLANE, F32), pltpu.VMEM(NATIVE, F32), SEMS, SEMS, SEMS]
-    grad, ready_f, ready_n, final = kernel(finish, [(RESULT, 0), plane, plane, (NATIVE, 0)], holds)(
-        lam_f, lam_i, lam_n, om, u0_i, post_f, post_i, post_n, pfar, pnear
+    pair_sem = pltpu.SemaphoreType.DMA((2,))
+    grad, ready_f, final = kernel(
+        finish,
+        [(RESULT, 0), plane, (NATIVE, 0)],
+        [pltpu.VMEM(NATIVE, F32), pltpu.VMEM(PLANE, F32), SEMS, pair_sem, pair_sem]
+        + [pltpu.VMEM(INNERS, F32), pltpu.VMEM(PLANE, F32)]
+        + GOT,
+    )(lam_f, lam_i, lam_n, om, u0_i, u0_n, near, post_f, post_i, post_n, pfar, pnear)
+    (grad,) = kernel(far_last, [(RESULT, 0)], [pltpu.VMEM(PLANE, F32), pair_sem] + GOT, {4: 0})(
+        ready_f, far, om, u0_f, (grad, 0)
     )
-    scratch = [pltpu.VMEM(PLANE, F32), SEMS] + GOT
-    last = [kernel(adjoint_edge_last(p), [(RESULT, 0)], scratch, {4: 0}) for p in (FAR, NEAR)]
-    (grad,) = last[1](ready_n, near, om, u0_n, (grad, 0))
-    (grad,) = last[0](ready_f, far, om, u0_f, (grad, 0))
     final = jnp.swapaxes(final.reshape(19, ROWS, PLANES, LANES), 1, 2)
     return final.reshape(populations.shape), jnp.swapaxes(grad, 1, 2).reshape(populations.shape)
 

time: 41.2 us -> 37.5 us (0.910)
  Pallas kernels: 17.6 us -> 15.4 us
  waiting for transfers between devices: 1.93 us -> 0.88 us
    pallas_call x17 -> x15, Pallas kernels: 17.6 us -> 15.4 us  [call(): pl.pallas_call(body, in_specs=[INSIDE if inside else OUTSIDE for _, insid...]
    ppermute x6, waiting for transfers between devices: 1.92 us -> 0.86 us  [exchange(): return (lax.ppermute(far, 'gx', far_pairs), near)]
    ppermute x6, starting transfers between devices: 1.78 us -> 1.12 us  [exchange(): near = lax.ppermute(near, 'gx', near_pairs)]
  transfers between devices with their start and end apart: 12 -> 12, of which waited for: 3 -> 3; matrix products, arithmetic and copies ran while one was open for 0% -> 0% of each run, Pallas kernels for 35% -> 33%
where the time goes in v4:
time: 37.5 us; the launch traced here: 37.4 us
  starting transfers between devices  20.3 us (54%)
  Pallas kernels  15.4 us (41%)
  waiting for transfers between devices  0.88 us (2%)
  between operations  0.79 us (2%)
    ppermute x6, starting transfers between devices, exchange(): return (lax.ppermute(far, 'gx', far_pairs), near)  19.2 us
    pallas_call x15, Pallas kernels, call(): pl.pallas_call(body, in_specs=[INSIDE if inside else OUTSIDE for _, insid...  15.4 us
    ppermute x6, starting transfers between devices, exchange(): near = lax.ppermute(near, 'gx', near_pairs)  1.12 us
    ppermute x6, waiting for transfers between devices, exchange(): return (lax.ppermute(far, 'gx', far_pairs), near)  0.86 us
  transfers between devices with their start and end apart: 12, of which 3 were waited for; matrix products, arithmetic and copies ran while one was open for 0% of the time, Pallas kernels for 33%

profile of v4, /device:TPU:0, one launch (start us, length us, event | category | flops | bytes accessed | tf_op | source)
XLA Modules:
  0.0 37.4 jit_solution(11699967156344889408)
XLA Ops:
  0.6 2.0 %first_edges.1 = (f32[19,256,128]{2,1,0:T(8,128)S(1)}, f32[4,64,128]{2,1,0:T(8,128)S(1)}, f32[19,64,128]{2,1,0:T(8,128)S(1)}, f32[19,64,128]{2,1,0:T(8,128)S(1)}...) custom-call(f32[19,256,128]{2,1,0:T(8,128)} %bitcast.24, ...), custom_call_target="tpu_custom_call" | custom-call | tf_op jit(solution)/shard_map/first_edges/pallas_call | solution.py:511
  2.6 5.5 %collective-permute-start = (f32[5,64,128]{2,1,0:T(8,128)S(1)}, f32[5,64,128]{2,1,0:T(8,128)S(1)}, u32[]{:S(2)}, u32[]{:S(2)}) collective-permute-start(f32[5,64,128]{2,1,0:T(8,128)S(1)} %get-tuple-element.68), channel_id=1, source_target_pairs={{0,15},{1,2},{2,1},{3,4},{4,3},{5,6},{6,5},{7,8},{8,7},{9,10},{10,... | collective-permute-start | bytes 491528 | tf_op jit(solution)/shard_map/ppermute | solution.py:539
  8.1 0.4 %cotangent_planes.1 = (f32[19,64,128]{2,1,0:T(8,128)S(1)}, f32[19,2,64,128]{3,2,1,0:T(8,128)S(1)}, f32[19,64,128]{2,1,0:T(8,128)S(1)}, f32[5,64,128]{2,1,0:T(8,128)S(1)}, f32[5,64,128]{2,1,0:T(8,128)S(1)}) custom-call(f32[19,256,128]{2,1,0:T(8,128)S(1)} %bitcast.23), custom_call_target="tpu_custom_call" | custom-call | tf_op jit(solution)/shard_map/cotangent_planes/pallas_call | solution.py:511
  8.5 0.8 %collective-permute-start.3 = (f32[5,64,128]{2,1,0:T(8,128)S(1)}, f32[5,64,128]{2,1,0:T(8,128)S(1)}, u32[]{:S(2)}, u32[]{:S(2)}) collective-permute-start(f32[5,64,128]{2,1,0:T(8,128)S(1)} %get-tuple-element.80), channel_id=1, source_target_pairs={{0,15},{1,2},{2,1},{3,4},{4,3},{5,6},{6,5},{7,8},{8,7},{9,10},{10,... | collective-permute-start | bytes 491528 | tf_op jit(solution)/shard_map/ppermute | solution.py:539
  9.3 0.5 %first_inner.1 = (f32[19,2,64,128]{3,2,1,0:T(8,128)S(1)}, f32[3,2,64,128]{3,2,1,0:T(8,128)S(1)}) custom-call(f32[19,256,128]{2,1,0:T(8,128)S(1)} %get-tuple-element.60.held, f32[4,64,128]{2,1,0:T(8,128)S(1)} %get-tuple-element.61.om_ref), custom_call_target="tpu_custom_call" | custom-call | tf_op jit(solution)/shard_map/first_inner/pallas_call | solution.py:511
  9.8 1.2 %forward_inner.2 = (f32[19,2,64,128]{3,2,1,0:T(8,128)S(1)}, f32[3,2,64,128]{3,2,1,0:T(8,128)S(1)}, f32[19,64,128]{2,1,0:T(8,128)S(1)}, f32[19,64,128]{2,1,0:T(8,128)S(1)}) custom-call(f32[19,64,128]{2,1,0:T(8,128)S(1)} %get-tuple-element.59.far, f32[19,2,64,128]{3,2,1,0:T(8,128)S(1)} %get-tuple-element.62.inner, f32[19,64,128]{2,1,0:T(8,128)S(1)} %get-tuple-element.63.near, ...), custom_call_target="tpu_custom_call" | custom-call | tf_op jit(solution)/shard_map/forward_inner/pallas_call | solution.py:511
  11.1 0.7 %forward_edges.1 = (f32[19,64,128]{2,1,0:T(8,128)S(1)}, f32[19,64,128]{2,1,0:T(8,128)S(1)}, f32[3,64,128]{2,1,0:T(8,128)S(1)}, f32[3,64,128]{2,1,0:T(8,128)S(1)}...) custom-call(f32[19,64,128]{2,1,0:T(8,128)S(1)} %get-tuple-element.64.ready_f, ...), custom_call_target="tpu_custom_call" | custom-call | tf_op jit(solution)/shard_map/forward_edges/pallas_call | solution.py:511
  11.8 0.5 %collective-permute-start.5 = (f32[5,64,128]{2,1,0:T(8,128)S(1)}, f32[5,64,128]{2,1,0:T(8,128)S(1)}, u32[]{:S(2)}, u32[]{:S(2)}) collective-permute-start(f32[5,64,128]{2,1,0:T(8,128)S(1)} %get-tuple-element.86), channel_id=1, source_target_pairs={{0,1},{1,0},{2,3},{3,2},{4,5},{5,4},{6,7},{7,6},{8,9},{9,8},{10,11... | collective-permute-start | bytes 491528 | tf_op jit(solution)/shard_map/ppermute | solution.py:538
  12.3 4.2 %collective-permute-start.2 = (f32[5,64,128]{2,1,0:T(8,128)S(1)}, f32[5,64,128]{2,1,0:T(8,128)S(1)}, u32[]{:S(2)}, u32[]{:S(2)}) collective-permute-start(f32[5,64,128]{2,1,0:T(8,128)S(1)} %get-tuple-element.74), channel_id=1, source_target_pairs={{0,15},{1,2},{2,1},{3,4},{4,3},{5,6},{6,5},{7,8},{8,7},{9,10},{10,... | collective-permute-start | bytes 491528 | tf_op jit(solution)/shard_map/ppermute | solution.py:539
  16.5 1.2 %forward_inner.3 = (f32[19,2,64,128]{3,2,1,0:T(8,128)S(1)}, f32[3,2,64,128]{3,2,1,0:T(8,128)S(1)}, f32[19,64,128]{2,1,0:T(8,128)S(1)}, f32[19,64,128]{2,1,0:T(8,128)S(1)}) custom-call(f32[19,64,128]{2,1,0:T(8,128)S(1)} %get-tuple-element.70.far, f32[19,2,64,128]{3,2,1,0:T(8,128)S(1)} %get-tuple-element.71.inner, f32[19,64,128]{2,1,0:T(8,128)S(1)} %get-tuple-element.72.near, ...), custom_call_target="tpu_custom_call" | custom-call | tf_op jit(solution)/shard_map/forward_inner/pallas_call | solution.py:511
  17.7 1.3 %adjoint_top.1 = (f32[19,2,64,128]{3,2,1,0:T(8,128)S(1)}, f32[19,64,128]{2,1,0:T(8,128)S(1)}, f32[19,64,128]{2,1,0:T(8,128)S(1)}) custom-call(f32[19,64,128]{2,1,0:T(8,128)S(1)} %get-tuple-element.76.far, f32[19,2,64,128]{3,2,1,0:T(8,128)S(1)} %get-tuple-element.77.inner, f32[19,64,128]{2,1,0:T(8,128)S(1)} %get-tuple-element.78.near, ...), custom_call_target="tpu_custom_call" | custom-call | tf_op jit(solution)/shard_map/adjoint_top/pallas_call | solution.py:511
  19.0 0.5 %turn_edge.3 = (f32[19,64,128]{2,1,0:T(8,128)S(1)}, f32[5,64,128]{2,1,0:T(8,128)S(1)}, f32[5,64,128]{2,1,0:T(8,128)S(1)}, f32[4,64,128]{2,1,0:T(8,128)S(1)}) custom-call(f32[19,64,128]{2,1,0:T(8,128)S(1)} %get-tuple-element.85.ready.ready_n, f32[5,64,128]{2,1,0:T(8,128)S(1)} %collective-permute-done.5.other, f32[4,64,128]{2,1,0:T(8,128)S(1)} %get-tuple-element.61.om_ref, ...), custom_call_target="tpu_custom_call" | custom-call | tf_op jit(solution)/shard_map/turn_edge/pallas_call | solution.py:511
  19.8 0.5 %turn_edge.2 = (f32[19,64,128]{2,1,0:T(8,128)S(1)}, f32[5,64,128]{2,1,0:T(8,128)S(1)}, f32[5,64,128]{2,1,0:T(8,128)S(1)}, f32[4,64,128]{2,1,0:T(8,128)S(1)}) custom-call(f32[19,64,128]{2,1,0:T(8,128)S(1)} %get-tuple-element.73.ready.ready_f, f32[5,64,128]{2,1,0:T(8,128)S(1)} %collective-permute-done.2.other, f32[4,64,128]{2,1,0:T(8,128)S(1)} %get-tuple-element.61.om_ref, ...), custom_call_target="tpu_custom_call" | custom-call | tf_op jit(solution)/shard_map/turn_edge/pallas_call | solution.py:511
  20.3 4.2 %collective-permute-start.6 = (f32[5,64,128]{2,1,0:T(8,128)S(1)}, f32[5,64,128]{2,1,0:T(8,128)S(1)}, u32[]{:S(2)}, u32[]{:S(2)}) collective-permute-start(f32[5,64,128]{2,1,0:T(8,128)S(1)} %get-tuple-element.91), channel_id=1, source_target_pairs={{0,15},{1,2},{2,1},{3,4},{4,3},{5,6},{6,5},{7,8},{8,7},{9,10},{10,... | collective-permute-start | bytes 491528 | tf_op jit(solution)/shard_map/ppermute | solution.py:539
  24.5 0.4 %relax_edges.1 = (f32[19,64,128]{2,1,0:T(8,128)S(1)}, f32[19,64,128]{2,1,0:T(8,128)S(1)}, f32[5,64,128]{2,1,0:T(8,128)S(1)}, f32[5,64,128]{2,1,0:T(8,128)S(1)}) custom-call(f32[19,64,128]{2,1,0:T(8,128)S(1)} %get-tuple-element.73.ready.ready_f, f32[5,64,128]{2,1,0:T(8,128)S(1)} %get-tuple-element.102.got_f, f32[4,64,128]{2,1,0:T(8,128)S(1)} %get-tuple-element.103.state_f, ...), custom_call_target="tpu_custom_call" | custom-call | tf_op jit(solution)/shard_map/relax_edges/pallas_call | solution.py:511
  24.9 0.4 collective-permute-start.9
  25.2 1.2 %adjoint_inner.1 = (f32[19,2,64,128]{3,2,1,0:T(8,128)S(1)}, f32[19,64,128]{2,1,0:T(8,128)S(1)}, f32[19,64,128]{2,1,0:T(8,128)S(1)}) custom-call(f32[19,64,128]{2,1,0:T(8,128)S(1)} %get-tuple-element.83.far, f32[19,2,64,128]{3,2,1,0:T(8,128)S(1)} %get-tuple-element.84.inner, f32[19,64,128]{2,1,0:T(8,128)S(1)} %get-tuple-element.88.near, ...), custom_call_target="tpu_custom_call" | custom-call | tf_op jit(solution)/shard_map/adjoint_inner/pallas_call | solution.py:511
  26.4 0.4 %adjoint_edge.3 = (f32[19,64,128]{2,1,0:T(8,128)S(1)}, f32[5,64,128]{2,1,0:T(8,128)S(1)}) custom-call(f32[19,64,128]{2,1,0:T(8,128)S(1)} %get-tuple-element.95.ready, f32[5,64,128]{2,1,0:T(8,128)S(1)} %collective-permute-done.7.other, f32[4,64,128]{2,1,0:T(8,128)S(1)} %get-tuple-element.61.om_ref, f32[3,64,128]{2,1,0:T(8,128)S(1)} %get-tuple-element.97.u_ref), custom_call_target="tpu_custom_call" | custom-call | tf_op jit(solution)/shard_map/adjoint_edge/pallas_call | solution.py:511
  26.8 0.6 %collective-permute-start.8 = (f32[5,64,128]{2,1,0:T(8,128)S(1)}, f32[5,64,128]{2,1,0:T(8,128)S(1)}, u32[]{:S(2)}, u32[]{:S(2)}) collective-permute-start(f32[5,64,128]{2,1,0:T(8,128)S(1)} %get-tuple-element.101), channel_id=1, source_target_pairs={{0,1},{1,0},{2,3},{3,2},{4,5},{5,4},{6,7},{7,6},{8,9},{9,8},{10,11... | collective-permute-start | bytes 491528 | tf_op jit(solution)/shard_map/ppermute | solution.py:538
  27.4 0.5 %collective-permute-done.6.other = f32[5,64,128]{2,1,0:T(8,128)S(1)} collective-permute-done((f32[5,64,128]{2,1,0:T(8,128)S(1)}, f32[5,64,128]{2,1,0:T(8,128)S(1)}, u32[]{:S(2)}, u32[]{:S(2)}) %collective-permute-start.6) | collective-permute-done | bytes 163872 | tf_op jit(solution)/shard_map/ppermute | solution.py:539
  27.9 0.4 %adjoint_edge.2 = (f32[19,64,128]{2,1,0:T(8,128)S(1)}, f32[5,64,128]{2,1,0:T(8,128)S(1)}) custom-call(f32[19,64,128]{2,1,0:T(8,128)S(1)} %get-tuple-element.90.ready, f32[5,64,128]{2,1,0:T(8,128)S(1)} %collective-permute-done.6.other, f32[4,64,128]{2,1,0:T(8,128)S(1)} %get-tuple-element.61.om_ref, f32[3,64,128]{2,1,0:T(8,128)S(1)} %get-tuple-element.92.u_ref), custom_call_target="tpu_custom_call" | custom-call | tf_op jit(solution)/shard_map/adjoint_edge/pallas_call | solution.py:511
  28.3 4.1 %collective-permute-start.11 = (f32[5,64,128]{2,1,0:T(8,128)S(1)}, f32[5,64,128]{2,1,0:T(8,128)S(1)}, u32[]{:S(2)}, u32[]{:S(2)}) collective-permute-start(f32[5,64,128]{2,1,0:T(8,128)S(1)} %get-tuple-element.113), channel_id=1, source_target_pairs={{0,15},{1,2},{2,1},{3,4},{4,3},{5,6},{6,5},{7,8},{8,7},{9,10},{10,... | collective-permute-start | bytes 491528 | tf_op jit(solution)/shard_map/ppermute | solution.py:539
  32.4 3.8 %finish.1 = (f32[19,64,4,128]{3,2,1,0:T(4,128)}, f32[19,64,128]{2,1,0:T(8,128)S(1)}, f32[19,256,128]{2,1,0:T(8,128)}) custom-call(f32[19,64,128]{2,1,0:T(8,128)S(1)} %get-tuple-element.93.far, f32[19,2,64,128]{3,2,1,0:T(8,128)S(1)} %get-tuple-element.94.inner, f32[19,64,128]{2,1,0:T(8,128)S(1)} %get-tuple-element.98.near, ...), custom_call_target="tpu_custom_call" | custom-call | tf_op jit(solution)/shard_map/finish/pallas_call | solution.py:511
  36.3 1.1 %far_last.1 = f32[19,64,4,128]{3,2,1,0:T(4,128)} custom-call(f32[19,64,128]{2,1,0:T(8,128)S(1)} %get-tuple-element.112.ready, f32[5,64,128]{2,1,0:T(8,128)S(1)} %collective-permute-done.11.other, f32[4,64,128]{2,1,0:T(8,128)S(1)} %get-tuple-element.61.om_ref, f32[3,64,128]{2,1,0:T(8,128)S(1)} %get-tuple-element.114.u_ref, ...), custom_call_target="tpu_custom_call", output_to_operand_aliasing={{}: (4, {})} | custom-call | tf_op jit(solution)/shard_map/far_last/pallas_call | solution.py:511
  (17 shorter events, 0.5 us)
Async XLA Ops:
  0.6 7.5 %copy-start = (f32[19,4,8192]{2,1,0:T(4,128)S(1)}, f32[19,4,8192]{2,1,0:T(4,128)}, u32[]{:S(2)}) copy-start(f32[19,4,8192]{2,1,0:T(4,128)} %param.5) | copy-start | bytes 7471108
  2.6 8.5 %collective-permute-start = (f32[5,64,128]{2,1,0:T(8,128)S(1)}, f32[5,64,128]{2,1,0:T(8,128)S(1)}, u32[]{:S(2)}, u32[]{:S(2)}) collective-permute-start(f32[5,64,128]{2,1,0:T(8,128)S(1)} %get-tuple-element.68), channel_id=1, source_target_pairs={{0,15},{1,2},{2,1},{3,4},{4,3},{5,6},{6,5},{7,8},{8,7},{9,10},{10,... | collective-permute-start | bytes 491528 | tf_op jit(solution)/shard_map/ppermute | solution.py:539
  8.1 3.0 %collective-permute-start.1 = (f32[5,64,128]{2,1,0:T(8,128)S(1)}, f32[5,64,128]{2,1,0:T(8,128)S(1)}, u32[]{:S(2)}, u32[]{:S(2)}) collective-permute-start(f32[5,64,128]{2,1,0:T(8,128)S(1)} %get-tuple-element.69), channel_id=1, source_target_pairs={{0,1},{1,0},{2,3},{3,2},{4,5},{5,4},{6,7},{7,6},{8,9},{9,8},{10,11... | collective-permute-start | bytes 491528 | tf_op jit(solution)/shard_map/ppermute | solution.py:538
  8.5 9.2 %collective-permute-start.3 = (f32[5,64,128]{2,1,0:T(8,128)S(1)}, f32[5,64,128]{2,1,0:T(8,128)S(1)}, u32[]{:S(2)}, u32[]{:S(2)}) collective-permute-start(f32[5,64,128]{2,1,0:T(8,128)S(1)} %get-tuple-element.80), channel_id=1, source_target_pairs={{0,15},{1,2},{2,1},{3,4},{4,3},{5,6},{6,5},{7,8},{8,7},{9,10},{10,... | collective-permute-start | bytes 491528 | tf_op jit(solution)/shard_map/ppermute | solution.py:539
  9.3 8.4 %collective-permute-start.4 = (f32[5,64,128]{2,1,0:T(8,128)S(1)}, f32[5,64,128]{2,1,0:T(8,128)S(1)}, u32[]{:S(2)}, u32[]{:S(2)}) collective-permute-start(f32[5,64,128]{2,1,0:T(8,128)S(1)} %get-tuple-element.81), channel_id=1, source_target_pairs={{0,1},{1,0},{2,3},{3,2},{4,5},{5,4},{6,7},{7,6},{8,9},{9,8},{10,11... | collective-permute-start | bytes 491528 | tf_op jit(solution)/shard_map/ppermute | solution.py:538
  11.8 7.2 %collective-permute-start.5 = (f32[5,64,128]{2,1,0:T(8,128)S(1)}, f32[5,64,128]{2,1,0:T(8,128)S(1)}, u32[]{:S(2)}, u32[]{:S(2)}) collective-permute-start(f32[5,64,128]{2,1,0:T(8,128)S(1)} %get-tuple-element.86), channel_id=1, source_target_pairs={{0,1},{1,0},{2,3},{3,2},{4,5},{5,4},{6,7},{7,6},{8,9},{9,8},{10,11... | collective-permute-start | bytes 491528 | tf_op jit(solution)/shard_map/ppermute | solution.py:538
  12.3 7.5 %collective-permute-start.2 = (f32[5,64,128]{2,1,0:T(8,128)S(1)}, f32[5,64,128]{2,1,0:T(8,128)S(1)}, u32[]{:S(2)}, u32[]{:S(2)}) collective-permute-start(f32[5,64,128]{2,1,0:T(8,128)S(1)} %get-tuple-element.74), channel_id=1, source_target_pairs={{0,15},{1,2},{2,1},{3,4},{4,3},{5,6},{6,5},{7,8},{8,7},{9,10},{10,... | collective-permute-start | bytes 491528 | tf_op jit(solution)/shard_map/ppermute | solution.py:539
  19.5 6.9 %collective-permute-start.7 = (f32[5,64,128]{2,1,0:T(8,128)S(1)}, f32[5,64,128]{2,1,0:T(8,128)S(1)}, u32[]{:S(2)}, u32[]{:S(2)}) collective-permute-start(f32[5,64,128]{2,1,0:T(8,128)S(1)} %get-tuple-element.96), channel_id=1, source_target_pairs={{0,1},{1,0},{2,3},{3,2},{4,5},{5,4},{6,7},{7,6},{8,9},{9,8},{10,11... | collective-permute-start | bytes 491528 | tf_op jit(solution)/shard_map/ppermute | solution.py:538
  20.3 7.6 %collective-permute-start.6 = (f32[5,64,128]{2,1,0:T(8,128)S(1)}, f32[5,64,128]{2,1,0:T(8,128)S(1)}, u32[]{:S(2)}, u32[]{:S(2)}) collective-permute-start(f32[5,64,128]{2,1,0:T(8,128)S(1)} %get-tuple-element.91), channel_id=1, source_target_pairs={{0,15},{1,2},{2,1},{3,4},{4,3},{5,6},{6,5},{7,8},{8,7},{9,10},{10,... | collective-permute-start | bytes 491528 | tf_op jit(solution)/shard_map/ppermute | solution.py:539
  24.9 7.5 %collective-permute-start.9 = (f32[5,64,128]{2,1,0:T(8,128)S(1)}, f32[5,64,128]{2,1,0:T(8,128)S(1)}, u32[]{:S(2)}, u32[]{:S(2)}) collective-permute-start(f32[5,64,128]{2,1,0:T(8,128)S(1)} %get-tuple-element.109), channel_id=1, source_target_pairs={{0,15},{1,2},{2,1},{3,4},{4,3},{5,6},{6,5},{7,8},{8,7},{9,10},{10,... | collective-permute-start | bytes 491528 | tf_op jit(solution)/shard_map/ppermute | solution.py:539
  25.2 7.2 %collective-permute-start.10 = (f32[5,64,128]{2,1,0:T(8,128)S(1)}, f32[5,64,128]{2,1,0:T(8,128)S(1)}, u32[]{:S(2)}, u32[]{:S(2)}) collective-permute-start(f32[5,64,128]{2,1,0:T(8,128)S(1)} %get-tuple-element.110), channel_id=1, source_target_pairs={{0,1},{1,0},{2,3},{3,2},{4,5},{5,4},{6,7},{7,6},{8,9},{9,8},{10,11... | collective-permute-start | bytes 491528 | tf_op jit(solution)/shard_map/ppermute | solution.py:538
  26.8 5.6 %collective-permute-start.8 = (f32[5,64,128]{2,1,0:T(8,128)S(1)}, f32[5,64,128]{2,1,0:T(8,128)S(1)}, u32[]{:S(2)}, u32[]{:S(2)}) collective-permute-start(f32[5,64,128]{2,1,0:T(8,128)S(1)} %get-tuple-element.101), channel_id=1, source_target_pairs={{0,1},{1,0},{2,3},{3,2},{4,5},{5,4},{6,7},{7,6},{8,9},{9,8},{10,11... | collective-permute-start | bytes 491528 | tf_op jit(solution)/shard_map/ppermute | solution.py:538
  28.3 8.0 %collective-permute-start.11 = (f32[5,64,128]{2,1,0:T(8,128)S(1)}, f32[5,64,128]{2,1,0:T(8,128)S(1)}, u32[]{:S(2)}, u32[]{:S(2)}) collective-permute-start(f32[5,64,128]{2,1,0:T(8,128)S(1)} %get-tuple-element.113), channel_id=1, source_target_pairs={{0,15},{1,2},{2,1},{3,4},{4,3},{5,6},{6,5},{7,8},{8,7},{9,10},{10,... | collective-permute-start | bytes 491528 | tf_op jit(solution)/shard_map/ppermute | solution.py:539

commit v5 on v4

--- a/solution.py
+++ b/solution.py
@@ -342,8 +342,54 @@
         put(lam, out, r, (i,))
 
 
-def adjoint_inner(far, inner, near, om_ref, u_ref, lam, ready_f, ready_n):
+def write_half(hold, result, sem, flip, p, i):
+    rows = pl.ds(i * (ROWS // 2), ROWS // 2)
+    return pltpu.make_async_copy(
+        hold.at[:, rows, :], result.at[:, rows, place(flip, p), :], sem.at[i]
+    )
+
+
+def by_halves(body, after):
+    for i in range(2):
+        first = i * (BLOCKS // 2)
+
+        def pair(r, carry, first=first):
+            body(first + 2 * r)
+            body(first + 2 * r + 1)
+            return carry
+
+        lax.fori_loop(0, BLOCKS // 4, pair, 0)
+        after(i)
+
+
+def stream_planes(places, posts, others, result, flip, m):
+    def body(r):
+        for p, hold, _ in places:
+            f = pull_local(posts, p, r, 1, m)
+            if p not in INNER:
+                pull_remote(others[p == NEAR], f, p, r, 1, m)
+            put_mirrored(hold, f, flip, r)
+
+    def after(i):
+        for p, hold, sem in places:
+            write_half(hold, result, sem, flip, p, i).start()
+
+    by_halves(body, after)
+
+
+def wait_planes(places, result, flip):
+    for p, hold, sem in places:
+        for i in range(2):
+            write_half(hold, result, sem, flip, p, i).wait()
+
+
+def adjoint_inner(
+    far, inner, near, om_ref, u_ref, post_f, post_i, post_n,
+    lam, ready_f, ready_n, final, hold_1, hold_2, sem_1, sem_2,
+):
     parts, m = (far, inner, near), iotas()
+    places = ((1, hold_1, sem_1), (2, hold_2, sem_2))
+    by_side(lambda flip: stream_planes(places, (post_f, post_i, post_n), None, final, flip, m))
 
     def body(r):
         adjoint_planes(parts, om_ref, u_ref, lam, r, m)
@@ -351,6 +397,7 @@
             put(ready, pull_local(parts, p, r, -1, m), r)
 
     loop(body, STEP)
+    by_side(lambda flip: wait_planes(places, final, flip))
 
 
 def adjoint_top(far, inner, near, om_ref, u_ref, other_f, other_n, lam, mus_f, mus_n):
@@ -411,30 +458,17 @@
 
 
 def finish(
-    far, inner, near, om_ref, u_ref, un_ref, other, post_f, post_i, post_n, other_f, other_n,
-    grad, ready_f, final, flat, hold, sem, hold_sem, near_sem, lam, ready_n, got,
+    far, inner, near, om_ref, u_ref, un_ref, other, post_f, post_i, post_n, other_f, other_n, partial,
+    grad, ready_f, final, hold_1, hold_2, sem_1, sem_2, hold, hold_sem, near_sem, lam, ready_n, got,
 ):
     parts, posts, m = (far, inner, near), (post_f, post_i, post_n), iotas()
+    places = ((FAR, hold_1, sem_1), (NEAR, hold_2, sem_2))
 
     def run(flip):
         def copy(i, p):
             return pltpu.make_async_copy(
                 lam.at[:, i], grad.at[:, :, place(flip, p), :], hold_sem.at[i]
             )
-
-        def stream(r):
-            for p in range(PLANES):
-                f = pull_local(posts, p, r, 1, m)
-                if p not in INNER:
-                    pull_remote(other_f if p == FAR else other_n, f, p, r, 1, m)
-                put_native(flat, f, flip, p, r)
-
-        def streams(r, carry):
-            for j in range(STEP):
-                stream(STEP * r + j)
-            for j in range(STEP):
-                moved(flat, final, sem, STEP * r + j).start()
-            return carry
 
         def body(r):
             for i, p in enumerate(INNER):
@@ -444,52 +478,35 @@
             for p, ready in ((FAR, ready_f), (NEAR, ready_n)):
                 put(ready, pull_local(parts, p, r, -1, m), r)
 
-        lax.fori_loop(0, BLOCKS // STEP, streams, 0)
+        stream_planes(places, posts, (other_f, other_n), final, flip, m)
         loop(body, STEP)
         for i, p in enumerate(INNER):
             copy(i, p).start()
-        receive(other, got, NEAR, -1)
-        edge_last(ready_n, got, om_ref, un_ref, grad, hold, near_sem, NEAR, flip)
+        edge_last(ready_n, other, got, om_ref, un_ref, grad, hold, near_sem, NEAR, flip)
         for i, p in enumerate(INNER):
             copy(i, p).wait()
-        loop(lambda r: moved(flat, final, sem, r).wait())
+        wait_planes(places, final, flip)
 
     by_side(run)
 
 
-def edge_last(ready, got, om_ref, u_ref, grad, hold, sem, p, flip):
-    half = ROWS // 2
-
-    def copy(i):
-        rows = pl.ds(i * half, half)
-        return pltpu.make_async_copy(
-            hold.at[:, rows, :], grad.at[:, rows, place(flip, p), :], sem.at[i]
-        )
+def edge_last(ready, other, got, om_ref, u_ref, grad, hold, sem, p, flip):
+    receive(other, got, p, -1)
 
     def body(r):
         mu = edge_values(ready, got, p, r, -1)
         out = adjoint(mu, get(u_ref, r, count=3), om_ref[p, block(r), :])
         put_mirrored(hold, out, flip, r)
 
-    def pairs(first):
-        def pair(r, carry):
-            body(first + 2 * r)
-            body(first + 2 * r + 1)
-            return carry
-
-        lax.fori_loop(0, BLOCKS // 4, pair, 0)
-
-    pairs(0)
-    copy(0).start()
-    pairs(BLOCKS // 2)
-    copy(1).start()
-    copy(0).wait()
-    copy(1).wait()
+    by_halves(body, lambda i: write_half(hold, grad, sem, flip, p, i).start())
+    for i in range(2):
+        write_half(hold, grad, sem, flip, p, i).wait()
 
 
 def far_last(ready, other, om_ref, u_ref, partial, grad, hold, sem, got):
-    receive(other, got, FAR, -1)
-    by_side(lambda flip: edge_last(ready, got, om_ref, u_ref, grad, hold, sem, FAR, flip))
+    by_side(
+        lambda flip: edge_last(ready, other, got, om_ref, u_ref, grad, hold, sem, FAR, flip)
+    )
 
 
 INSIDE = pl.BlockSpec(memory_space=pltpu.VMEM)
@@ -576,27 +593,29 @@
     post_f, post_n, pfar, pnear = kernel(relax_edges, [plane, plane, cross, cross])(
         ready_f, got_f, state_f, ready_n, got_n, state_n, om
     )
-    lam_i, ready_f, ready_n = kernel(adjoint_inner, [inners, plane, plane])(
-        lam_f, lam_i, lam_n, om, u1_i
-    )
+    pair_sem = pltpu.SemaphoreType.DMA((2,))
+    halves = [pltpu.VMEM(PLANE, F32), pltpu.VMEM(PLANE, F32), pair_sem, pair_sem]
+    lam_i, ready_f, ready_n, final = kernel(
+        adjoint_inner, [inners, plane, plane, (RESULT, 0)], halves
+    )(lam_f, lam_i, lam_n, om, u1_i, post_f, post_i, post_n)
+    pfar, pnear, ready_f = lax.optimization_barrier((pfar, pnear, ready_f))
     pfar, pnear = exchange(pfar, pnear)
     edge = [kernel(adjoint_edge(p), [plane, cross], GOT) for p in (FAR, NEAR)]
     lam_n, near = edge[1](ready_n, near, om, u1_n)
     lam_f, far = edge[0](ready_f, far, om, u1_f)
     far, near = exchange(far, near)
-    pair_sem = pltpu.SemaphoreType.DMA((2,))
     grad, ready_f, final = kernel(
         finish,
-        [(RESULT, 0), plane, (NATIVE, 0)],
-        [pltpu.VMEM(NATIVE, F32), pltpu.VMEM(PLANE, F32), SEMS, pair_sem, pair_sem]
-        + [pltpu.VMEM(INNERS, F32), pltpu.VMEM(PLANE, F32)]
+        [(RESULT, 0), plane, (RESULT, 0)],
+        halves
+        + [pltpu.VMEM(PLANE, F32), pair_sem, pair_sem, pltpu.VMEM(INNERS, F32), pltpu.VMEM(PLANE, F32)]
         + GOT,
-    )(lam_f, lam_i, lam_n, om, u0_i, u0_n, near, post_f, post_i, post_n, pfar, pnear)
+        {12: 2},
+    )(lam_f, lam_i, lam_n, om, u0_i, u0_n, near, post_f, post_i, post_n, pfar, pnear, (final, 0))
     (grad,) = kernel(far_last, [(RESULT, 0)], [pltpu.VMEM(PLANE, F32), pair_sem] + GOT, {4: 0})(
         ready_f, far, om, u0_f, (grad, 0)
     )
-    final = jnp.swapaxes(final.reshape(19, ROWS, PLANES, LANES), 1, 2)
-    return final.reshape(populations.shape), jnp.swapaxes(grad, 1, 2).reshape(populations.shape)
+    return tuple(jnp.swapaxes(x, 1, 2).reshape(populations.shape) for x in (final, grad))
 
 
 def solution(mesh):

time: 37.5 us -> 39.1 us (1.043)
  waiting for transfers between devices: 0.88 us -> 2.04 us
    ppermute x6, waiting for transfers between devices: 0.86 us -> 2.02 us  [exchange(): return (lax.ppermute(far, 'gx', far_pairs), near)]
  transfers between devices with their start and end apart: 12 -> 12, of which waited for: 3 -> 3; matrix products, arithmetic and copies ran while one was open for 0% -> 0% of each run, Pallas kernels for 33% -> 32%
where the time goes in v5:
time: 39.1 us; the launch traced here: 38.9 us
  starting transfers between devices  20.4 us (52%)
  Pallas kernels  15.7 us (40%)
  waiting for transfers between devices  2.04 us (5%)
  between operations  0.79 us (2%)
    ppermute x6, starting transfers between devices, exchange(): return (lax.ppermute(far, 'gx', far_pairs), near)  19.3 us
    pallas_call x15, Pallas kernels, call(): pl.pallas_call(body, in_specs=[INSIDE if inside else OUTSIDE for _, insid...  15.7 us
    ppermute x6, waiting for transfers between devices, exchange(): return (lax.ppermute(far, 'gx', far_pairs), near)  2.02 us
    ppermute x6, starting transfers between devices, exchange(): near = lax.ppermute(near, 'gx', near_pairs)  1.12 us
  transfers between devices with their start and end apart: 12, of which 3 were waited for; matrix products, arithmetic and copies ran while one was open for 0% of the time, Pallas kernels for 32%

profile of v5, /device:TPU:0, one launch (start us, length us, event | category | flops | bytes accessed | tf_op | source)
XLA Modules:
  0.0 38.9 jit_solution(9086405400388411370)
XLA Ops:
  0.6 2.0 %first_edges.1 = (f32[19,256,128]{2,1,0:T(8,128)S(1)}, f32[4,64,128]{2,1,0:T(8,128)S(1)}, f32[19,64,128]{2,1,0:T(8,128)S(1)}, f32[19,64,128]{2,1,0:T(8,128)S(1)}...) custom-call(f32[19,256,128]{2,1,0:T(8,128)} %bitcast.22, ...), custom_call_target="tpu_custom_call" | custom-call | tf_op jit(solution)/shard_map/first_edges/pallas_call | solution.py:528
  2.6 5.5 %collective-permute-start = (f32[5,64,128]{2,1,0:T(8,128)S(1)}, f32[5,64,128]{2,1,0:T(8,128)S(1)}, u32[]{:S(2)}, u32[]{:S(2)}) collective-permute-start(f32[5,64,128]{2,1,0:T(8,128)S(1)} %get-tuple-element.72), channel_id=1, source_target_pairs={{0,15},{1,2},{2,1},{3,4},{4,3},{5,6},{6,5},{7,8},{8,7},{9,10},{10,... | collective-permute-start | bytes 491528 | tf_op jit(solution)/shard_map/ppermute | solution.py:556
  8.1 0.4 %cotangent_planes.1 = (f32[19,64,128]{2,1,0:T(8,128)S(1)}, f32[19,2,64,128]{3,2,1,0:T(8,128)S(1)}, f32[19,64,128]{2,1,0:T(8,128)S(1)}, f32[5,64,128]{2,1,0:T(8,128)S(1)}, f32[5,64,128]{2,1,0:T(8,128)S(1)}) custom-call(f32[19,256,128]{2,1,0:T(8,128)S(1)} %bitcast.21), custom_call_target="tpu_custom_call" | custom-call | tf_op jit(solution)/shard_map/cotangent_planes/pallas_call | solution.py:528
  8.5 0.8 %collective-permute-start.3 = (f32[5,64,128]{2,1,0:T(8,128)S(1)}, f32[5,64,128]{2,1,0:T(8,128)S(1)}, u32[]{:S(2)}, u32[]{:S(2)}) collective-permute-start(f32[5,64,128]{2,1,0:T(8,128)S(1)} %get-tuple-element.84), channel_id=1, source_target_pairs={{0,15},{1,2},{2,1},{3,4},{4,3},{5,6},{6,5},{7,8},{8,7},{9,10},{10,... | collective-permute-start | bytes 491528 | tf_op jit(solution)/shard_map/ppermute | solution.py:556
  9.3 0.5 %first_inner.1 = (f32[19,2,64,128]{3,2,1,0:T(8,128)S(1)}, f32[3,2,64,128]{3,2,1,0:T(8,128)S(1)}) custom-call(f32[19,256,128]{2,1,0:T(8,128)S(1)} %get-tuple-element.64.held, f32[4,64,128]{2,1,0:T(8,128)S(1)} %get-tuple-element.65.om_ref), custom_call_target="tpu_custom_call" | custom-call | tf_op jit(solution)/shard_map/first_inner/pallas_call | solution.py:528
  9.8 1.2 %forward_inner.2 = (f32[19,2,64,128]{3,2,1,0:T(8,128)S(1)}, f32[3,2,64,128]{3,2,1,0:T(8,128)S(1)}, f32[19,64,128]{2,1,0:T(8,128)S(1)}, f32[19,64,128]{2,1,0:T(8,128)S(1)}) custom-call(f32[19,64,128]{2,1,0:T(8,128)S(1)} %get-tuple-element.63.far, f32[19,2,64,128]{3,2,1,0:T(8,128)S(1)} %get-tuple-element.66.inner, f32[19,64,128]{2,1,0:T(8,128)S(1)} %get-tuple-element.67.near, ...), custom_call_target="tpu_custom_call" | custom-call | tf_op jit(solution)/shard_map/forward_inner/pallas_call | solution.py:528
  11.1 0.7 %forward_edges.1 = (f32[19,64,128]{2,1,0:T(8,128)S(1)}, f32[19,64,128]{2,1,0:T(8,128)S(1)}, f32[3,64,128]{2,1,0:T(8,128)S(1)}, f32[3,64,128]{2,1,0:T(8,128)S(1)}...) custom-call(f32[19,64,128]{2,1,0:T(8,128)S(1)} %get-tuple-element.68.ready_f, ...), custom_call_target="tpu_custom_call" | custom-call | tf_op jit(solution)/shard_map/forward_edges/pallas_call | solution.py:528
  11.8 0.5 %collective-permute-start.5 = (f32[5,64,128]{2,1,0:T(8,128)S(1)}, f32[5,64,128]{2,1,0:T(8,128)S(1)}, u32[]{:S(2)}, u32[]{:S(2)}) collective-permute-start(f32[5,64,128]{2,1,0:T(8,128)S(1)} %get-tuple-element.90), channel_id=1, source_target_pairs={{0,1},{1,0},{2,3},{3,2},{4,5},{5,4},{6,7},{7,6},{8,9},{9,8},{10,11... | collective-permute-start | bytes 491528 | tf_op jit(solution)/shard_map/ppermute | solution.py:555
  12.3 4.2 %collective-permute-start.2 = (f32[5,64,128]{2,1,0:T(8,128)S(1)}, f32[5,64,128]{2,1,0:T(8,128)S(1)}, u32[]{:S(2)}, u32[]{:S(2)}) collective-permute-start(f32[5,64,128]{2,1,0:T(8,128)S(1)} %get-tuple-element.78), channel_id=1, source_target_pairs={{0,15},{1,2},{2,1},{3,4},{4,3},{5,6},{6,5},{7,8},{8,7},{9,10},{10,... | collective-permute-start | bytes 491528 | tf_op jit(solution)/shard_map/ppermute | solution.py:556
  16.5 1.2 %forward_inner.3 = (f32[19,2,64,128]{3,2,1,0:T(8,128)S(1)}, f32[3,2,64,128]{3,2,1,0:T(8,128)S(1)}, f32[19,64,128]{2,1,0:T(8,128)S(1)}, f32[19,64,128]{2,1,0:T(8,128)S(1)}) custom-call(f32[19,64,128]{2,1,0:T(8,128)S(1)} %get-tuple-element.74.far, f32[19,2,64,128]{3,2,1,0:T(8,128)S(1)} %get-tuple-element.75.inner, f32[19,64,128]{2,1,0:T(8,128)S(1)} %get-tuple-element.76.near, ...), custom_call_target="tpu_custom_call" | custom-call | tf_op jit(solution)/shard_map/forward_inner/pallas_call | solution.py:528
  17.7 1.3 %adjoint_top.1 = (f32[19,2,64,128]{3,2,1,0:T(8,128)S(1)}, f32[19,64,128]{2,1,0:T(8,128)S(1)}, f32[19,64,128]{2,1,0:T(8,128)S(1)}) custom-call(f32[19,64,128]{2,1,0:T(8,128)S(1)} %get-tuple-element.80.far, f32[19,2,64,128]{3,2,1,0:T(8,128)S(1)} %get-tuple-element.81.inner, f32[19,64,128]{2,1,0:T(8,128)S(1)} %get-tuple-element.82.near, ...), custom_call_target="tpu_custom_call" | custom-call | tf_op jit(solution)/shard_map/adjoint_top/pallas_call | solution.py:528
  19.0 0.5 %turn_edge.3 = (f32[19,64,128]{2,1,0:T(8,128)S(1)}, f32[5,64,128]{2,1,0:T(8,128)S(1)}, f32[5,64,128]{2,1,0:T(8,128)S(1)}, f32[4,64,128]{2,1,0:T(8,128)S(1)}) custom-call(f32[19,64,128]{2,1,0:T(8,128)S(1)} %get-tuple-element.89.ready.ready_n, f32[5,64,128]{2,1,0:T(8,128)S(1)} %collective-permute-done.5.other, f32[4,64,128]{2,1,0:T(8,128)S(1)} %get-tuple-element.65.om_ref, ...), custom_call_target="tpu_custom_call" | custom-call | tf_op jit(solution)/shard_map/turn_edge/pallas_call | solution.py:528
  19.8 0.5 %turn_edge.2 = (f32[19,64,128]{2,1,0:T(8,128)S(1)}, f32[5,64,128]{2,1,0:T(8,128)S(1)}, f32[5,64,128]{2,1,0:T(8,128)S(1)}, f32[4,64,128]{2,1,0:T(8,128)S(1)}) custom-call(f32[19,64,128]{2,1,0:T(8,128)S(1)} %get-tuple-element.77.ready.ready_f, f32[5,64,128]{2,1,0:T(8,128)S(1)} %collective-permute-done.2.other, f32[4,64,128]{2,1,0:T(8,128)S(1)} %get-tuple-element.65.om_ref, ...), custom_call_target="tpu_custom_call" | custom-call | tf_op jit(solution)/shard_map/turn_edge/pallas_call | solution.py:528
  20.3 4.2 %collective-permute-start.6 = (f32[5,64,128]{2,1,0:T(8,128)S(1)}, f32[5,64,128]{2,1,0:T(8,128)S(1)}, u32[]{:S(2)}, u32[]{:S(2)}) collective-permute-start(f32[5,64,128]{2,1,0:T(8,128)S(1)} %get-tuple-element.105), channel_id=1, source_target_pairs={{0,15},{1,2},{2,1},{3,4},{4,3},{5,6},{6,5},{7,8},{8,7},{9,10},{10,... | collective-permute-start | bytes 491528 | tf_op jit(solution)/shard_map/ppermute | solution.py:556
  24.5 0.4 relax_edges.1
  24.9 2.0 %adjoint_inner.1 = (f32[19,2,64,128]{3,2,1,0:T(8,128)S(1)}, f32[19,64,128]{2,1,0:T(8,128)S(1)}, f32[19,64,128]{2,1,0:T(8,128)S(1)}, f32[19,64,4,128]{3,2,1,0:T(4,128)}) custom-call(f32[19,64,128]{2,1,0:T(8,128)S(1)} %get-tuple-element.96.far, f32[19,2,64,128]{3,2,1,0:T(8,128)S(1)} %get-tuple-element.97.inner, f32[19,64,128]{2,1,0:T(8,128)S(1)} %get-tuple-element.98.near, ...), custom_call_target="tpu_custom_call" | custom-call | tf_op jit(solution)/shard_map/adjoint_inner/pallas_call | solution.py:528
  26.9 0.4 collective-permute-start.9
  27.2 0.4 adjoint_edge.3
  27.6 0.6 %collective-permute-start.8 = (f32[5,64,128]{2,1,0:T(8,128)S(1)}, f32[5,64,128]{2,1,0:T(8,128)S(1)}, u32[]{:S(2)}, u32[]{:S(2)}) collective-permute-start(f32[5,64,128]{2,1,0:T(8,128)S(1)} %get-tuple-element.115), channel_id=1, source_target_pairs={{0,1},{1,0},{2,3},{3,2},{4,5},{5,4},{6,7},{7,6},{8,9},{9,8},{10,11... | collective-permute-start | bytes 491528 | tf_op jit(solution)/shard_map/ppermute | solution.py:555
  28.2 0.4 adjoint_edge.2
  28.6 4.2 %collective-permute-start.11 = (f32[5,64,128]{2,1,0:T(8,128)S(1)}, f32[5,64,128]{2,1,0:T(8,128)S(1)}, u32[]{:S(2)}, u32[]{:S(2)}) collective-permute-start(f32[5,64,128]{2,1,0:T(8,128)S(1)} %get-tuple-element.121), channel_id=1, source_target_pairs={{0,15},{1,2},{2,1},{3,4},{4,3},{5,6},{6,5},{7,8},{8,7},{9,10},{10,... | collective-permute-start | bytes 491528 | tf_op jit(solution)/shard_map/ppermute | solution.py:556
  32.8 1.7 %collective-permute-done.9.other_f = f32[5,64,128]{2,1,0:T(8,128)S(1)} collective-permute-done((f32[5,64,128]{2,1,0:T(8,128)S(1)}, f32[5,64,128]{2,1,0:T(8,128)S(1)}, u32[]{:S(2)}, u32[]{:S(2)}) %collective-permute-start.9) | collective-permute-done | bytes 163872 | tf_op jit(solution)/shard_map/ppermute | solution.py:556
  34.5 3.3 %finish.1 = (f32[19,64,4,128]{3,2,1,0:T(4,128)}, f32[19,64,128]{2,1,0:T(8,128)S(1)}, f32[19,64,4,128]{3,2,1,0:T(4,128)}) custom-call(f32[19,64,128]{2,1,0:T(8,128)S(1)} %get-tuple-element.107.far, f32[19,2,64,128]{3,2,1,0:T(8,128)S(1)} %get-tuple-element.108.inner, f32[19,64,128]{2,1,0:T(8,128)S(1)} %get-tuple-element.112.near, ...), custom_call_target="tpu_custom_call", output_to_operand_aliasing={{2}: (12, {})} | custom-call | tf_op jit(solution)/shard_map/finish/pallas_call | solution.py:528
  37.8 1.1 %far_last.1 = f32[19,64,4,128]{3,2,1,0:T(4,128)} custom-call(f32[19,64,128]{2,1,0:T(8,128)S(1)} %get-tuple-element.120.ready, f32[5,64,128]{2,1,0:T(8,128)S(1)} %collective-permute-done.11.other, f32[4,64,128]{2,1,0:T(8,128)S(1)} %get-tuple-element.65.om_ref, f32[3,64,128]{2,1,0:T(8,128)S(1)} %get-tuple-element.122.u_ref, ...), custom_call_target="tpu_custom_call", output_to_operand_aliasing={{}: (4, {})} | custom-call | tf_op jit(solution)/shard_map/far_last/pallas_call | solution.py:528
  (17 shorter events, 0.5 us)
Async XLA Ops:
  0.6 7.5 %copy-start = (f32[19,4,8192]{2,1,0:T(4,128)S(1)}, f32[19,4,8192]{2,1,0:T(4,128)}, u32[]{:S(2)}) copy-start(f32[19,4,8192]{2,1,0:T(4,128)} %param.5) | copy-start | bytes 7471108
  2.6 8.5 %collective-permute-start = (f32[5,64,128]{2,1,0:T(8,128)S(1)}, f32[5,64,128]{2,1,0:T(8,128)S(1)}, u32[]{:S(2)}, u32[]{:S(2)}) collective-permute-start(f32[5,64,128]{2,1,0:T(8,128)S(1)} %get-tuple-element.72), channel_id=1, source_target_pairs={{0,15},{1,2},{2,1},{3,4},{4,3},{5,6},{6,5},{7,8},{8,7},{9,10},{10,... | collective-permute-start | bytes 491528 | tf_op jit(solution)/shard_map/ppermute | solution.py:556
  8.1 3.0 %collective-permute-start.1 = (f32[5,64,128]{2,1,0:T(8,128)S(1)}, f32[5,64,128]{2,1,0:T(8,128)S(1)}, u32[]{:S(2)}, u32[]{:S(2)}) collective-permute-start(f32[5,64,128]{2,1,0:T(8,128)S(1)} %get-tuple-element.73), channel_id=1, source_target_pairs={{0,1},{1,0},{2,3},{3,2},{4,5},{5,4},{6,7},{7,6},{8,9},{9,8},{10,11... | collective-permute-start | bytes 491528 | tf_op jit(solution)/shard_map/ppermute | solution.py:555
  8.5 9.2 %collective-permute-start.3 = (f32[5,64,128]{2,1,0:T(8,128)S(1)}, f32[5,64,128]{2,1,0:T(8,128)S(1)}, u32[]{:S(2)}, u32[]{:S(2)}) collective-permute-start(f32[5,64,128]{2,1,0:T(8,128)S(1)} %get-tuple-element.84), channel_id=1, source_target_pairs={{0,15},{1,2},{2,1},{3,4},{4,3},{5,6},{6,5},{7,8},{8,7},{9,10},{10,... | collective-permute-start | bytes 491528 | tf_op jit(solution)/shard_map/ppermute | solution.py:556
  9.3 8.4 %collective-permute-start.4 = (f32[5,64,128]{2,1,0:T(8,128)S(1)}, f32[5,64,128]{2,1,0:T(8,128)S(1)}, u32[]{:S(2)}, u32[]{:S(2)}) collective-permute-start(f32[5,64,128]{2,1,0:T(8,128)S(1)} %get-tuple-element.85), channel_id=1, source_target_pairs={{0,1},{1,0},{2,3},{3,2},{4,5},{5,4},{6,7},{7,6},{8,9},{9,8},{10,11... | collective-permute-start | bytes 491528 | tf_op jit(solution)/shard_map/ppermute | solution.py:555
  11.8 7.2 %collective-permute-start.5 = (f32[5,64,128]{2,1,0:T(8,128)S(1)}, f32[5,64,128]{2,1,0:T(8,128)S(1)}, u32[]{:S(2)}, u32[]{:S(2)}) collective-permute-start(f32[5,64,128]{2,1,0:T(8,128)S(1)} %get-tuple-element.90), channel_id=1, source_target_pairs={{0,1},{1,0},{2,3},{3,2},{4,5},{5,4},{6,7},{7,6},{8,9},{9,8},{10,11... | collective-permute-start | bytes 491528 | tf_op jit(solution)/shard_map/ppermute | solution.py:555
  12.3 7.5 %collective-permute-start.2 = (f32[5,64,128]{2,1,0:T(8,128)S(1)}, f32[5,64,128]{2,1,0:T(8,128)S(1)}, u32[]{:S(2)}, u32[]{:S(2)}) collective-permute-start(f32[5,64,128]{2,1,0:T(8,128)S(1)} %get-tuple-element.78), channel_id=1, source_target_pairs={{0,15},{1,2},{2,1},{3,4},{4,3},{5,6},{6,5},{7,8},{8,7},{9,10},{10,... | collective-permute-start | bytes 491528 | tf_op jit(solution)/shard_map/ppermute | solution.py:556
  19.5 7.7 %collective-permute-start.7 = (f32[5,64,128]{2,1,0:T(8,128)S(1)}, f32[5,64,128]{2,1,0:T(8,128)S(1)}, u32[]{:S(2)}, u32[]{:S(2)}) collective-permute-start(f32[5,64,128]{2,1,0:T(8,128)S(1)} %get-tuple-element.110), channel_id=1, source_target_pairs={{0,1},{1,0},{2,3},{3,2},{4,5},{5,4},{6,7},{7,6},{8,9},{9,8},{10,11... | collective-permute-start | bytes 491528 | tf_op jit(solution)/shard_map/ppermute | solution.py:555
  20.3 7.9 %collective-permute-start.6 = (f32[5,64,128]{2,1,0:T(8,128)S(1)}, f32[5,64,128]{2,1,0:T(8,128)S(1)}, u32[]{:S(2)}, u32[]{:S(2)}) collective-permute-start(f32[5,64,128]{2,1,0:T(8,128)S(1)} %get-tuple-element.105), channel_id=1, source_target_pairs={{0,15},{1,2},{2,1},{3,4},{4,3},{5,6},{6,5},{7,8},{8,7},{9,10},{10,... | collective-permute-start | bytes 491528 | tf_op jit(solution)/shard_map/ppermute | solution.py:556
  26.9 7.6 %collective-permute-start.9 = (f32[5,64,128]{2,1,0:T(8,128)S(1)}, f32[5,64,128]{2,1,0:T(8,128)S(1)}, u32[]{:S(2)}, u32[]{:S(2)}) collective-permute-start(f32[5,64,128]{2,1,0:T(8,128)S(1)} %get-tuple-element.116), channel_id=1, source_target_pairs={{0,15},{1,2},{2,1},{3,4},{4,3},{5,6},{6,5},{7,8},{8,7},{9,10},{10,... | collective-permute-start | bytes 491528 | tf_op jit(solution)/shard_map/ppermute | solution.py:556
  27.2 7.2 %collective-permute-start.10 = (f32[5,64,128]{2,1,0:T(8,128)S(1)}, f32[5,64,128]{2,1,0:T(8,128)S(1)}, u32[]{:S(2)}, u32[]{:S(2)}) collective-permute-start(f32[5,64,128]{2,1,0:T(8,128)S(1)} %get-tuple-element.117), channel_id=1, source_target_pairs={{0,1},{1,0},{2,3},{3,2},{4,5},{5,4},{6,7},{7,6},{8,9},{9,8},{10,11... | collective-permute-start | bytes 491528 | tf_op jit(solution)/shard_map/ppermute | solution.py:555
  27.6 6.8 %collective-permute-start.8 = (f32[5,64,128]{2,1,0:T(8,128)S(1)}, f32[5,64,128]{2,1,0:T(8,128)S(1)}, u32[]{:S(2)}, u32[]{:S(2)}) collective-permute-start(f32[5,64,128]{2,1,0:T(8,128)S(1)} %get-tuple-element.115), channel_id=1, source_target_pairs={{0,1},{1,0},{2,3},{3,2},{4,5},{5,4},{6,7},{7,6},{8,9},{9,8},{10,11... | collective-permute-start | bytes 491528 | tf_op jit(solution)/shard_map/ppermute | solution.py:555
  28.6 9.2 %collective-permute-start.11 = (f32[5,64,128]{2,1,0:T(8,128)S(1)}, f32[5,64,128]{2,1,0:T(8,128)S(1)}, u32[]{:S(2)}, u32[]{:S(2)}) collective-permute-start(f32[5,64,128]{2,1,0:T(8,128)S(1)} %get-tuple-element.121), channel_id=1, source_target_pairs={{0,15},{1,2},{2,1},{3,4},{4,3},{5,6},{6,5},{7,8},{8,7},{9,10},{10,... | collective-permute-start | bytes 491528 | tf_op jit(solution)/shard_map/ppermute | solution.py:556

commit v6 on v4

--- a/solution.py
+++ b/solution.py
@@ -223,33 +223,46 @@
 
 
 def first_edges(
-    pops, classes, held, om_ref, post_f, post_n, u_f, u_n, far_out, near_out, cls_ref, sem, cls_sem
+    pops, classes, om_ref, post_f, post_n, u_f, u_n, far_out, near_out, held_f, held_n, cls_ref, sem_f, sem_n, cls_sem
 ):
     fetch = pltpu.make_async_copy(classes, cls_ref, cls_sem)
-    fetch.start()
-    loop(lambda r: moved(pops, held, sem, r).start())
-    fetch.wait()
+    sides = (
+        (FAR, held_f, sem_f, post_f, u_f, far_out),
+        (NEAR, held_n, sem_n, post_n, u_n, near_out),
+    )
 
     def run(flip):
+        def copy(p, held, sem, r):
+            return pltpu.make_async_copy(
+                pops.at[:, block(r), place(flip, p), :], held.at[:, block(r), :], sem.at[r]
+            )
+
+        def start(r):
+            for p, held, sem, *_ in sides:
+                copy(p, held, sem, r).start()
+
         def body(r):
-            moved(pops, held, sem, r).wait()
             for p in range(PLANES):
                 cls = cls_ref[native(flip, 0, p, r)[1], :]
                 om = jnp.full((8, LANES), RATES[0], F32)
                 for entry in range(1, 4):
                     om = jnp.where(cls == entry, RATES[entry], om)
                 om_ref[p, block(r), :] = om
-                if p in INNER:
-                    continue
-                f = get_native(held, flip, p, r)
+            for p, held, sem, *_ in sides:
+                copy(p, held, sem, r).wait()
+            for p, held, sem, post, u_ref, out_ref in sides:
+                f = [held[mirrored(flip, k), block(r), :] for k in range(19)]
                 rho, u = state_of(f)
-                put(u_f if p == FAR else u_n, u, r)
-                out = relaxed(f, rho, u, om)
-                put(post_f if p == FAR else post_n, out, r)
-                put_crossing(far_out if p == FAR else near_out, out, p, r, 1)
-
+                put(u_ref, u, r)
+                out = relaxed(f, rho, u, om_ref[p, block(r), :])
+                put(post, out, r)
+                put_crossing(out_ref, out, p, r, 1)
+
+        loop(start)
+        fetch.wait()
         loop(body)
 
+    fetch.start()
     by_side(run)
 
 
@@ -412,14 +425,15 @@
 
 def finish(
     far, inner, near, om_ref, u_ref, un_ref, other, post_f, post_i, post_n, other_f, other_n,
-    grad, ready_f, final, flat, hold, sem, hold_sem, near_sem, lam, ready_n, got,
+    grad, ready_f, final, flat, hold, sem, hold_sem, near_sem, lam, ready_n, even, odd, got,
 ):
     parts, posts, m = (far, inner, near), (post_f, post_i, post_n), iotas()
 
     def run(flip):
-        def copy(i, p):
+        def copy(i, p, h):
+            rows = pl.ds(h * (ROWS // 2), ROWS // 2)
             return pltpu.make_async_copy(
-                lam.at[:, i], grad.at[:, :, place(flip, p), :], hold_sem.at[i]
+                lam.at[:, i, rows, :], grad.at[:, rows, place(flip, p), :], hold_sem.at[2 * i + h]
             )
 
         def stream(r):
@@ -429,72 +443,74 @@
                     pull_remote(other_f if p == FAR else other_n, f, p, r, 1, m)
                 put_native(flat, f, flip, p, r)
 
-        def streams(r, carry):
-            for j in range(STEP):
-                stream(STEP * r + j)
-            for j in range(STEP):
-                moved(flat, final, sem, STEP * r + j).start()
-            return carry
-
-        def body(r):
+        def pull(r, keep):
             for i, p in enumerate(INNER):
-                mu = pull_local(parts, p, r, -1, m)
+                for k, value in enumerate(pull_local(parts, p, r, -1, m)):
+                    keep[19 * i + k] = value
+            for p, ready in ((FAR, ready_f), (NEAR, ready_n)):
+                put(ready, pull_local(parts, p, r, -1, m), r)
+
+        def turn(r, keep):
+            for i, p in enumerate(INNER):
+                mu = [keep[19 * i + k] for k in range(19)]
                 out = adjoint(mu, get(u_ref, r, (i,), 3), om_ref[p, block(r), :])
                 put_mirrored(lam, out, flip, r, (i,))
-            for p, ready in ((FAR, ready_f), (NEAR, ready_n)):
-                put(ready, pull_local(parts, p, r, -1, m), r)
-
-        lax.fori_loop(0, BLOCKS // STEP, streams, 0)
-        loop(body, STEP)
-        for i, p in enumerate(INNER):
-            copy(i, p).start()
-        receive(other, got, NEAR, -1)
-        edge_last(ready_n, got, om_ref, un_ref, grad, hold, near_sem, NEAR, flip)
-        for i, p in enumerate(INNER):
-            copy(i, p).wait()
+
+        pull(0, even)
+        for h in range(2):
+            base = h * (BLOCKS // 2)
+
+            def pair(i, carry, base=base):
+                r = base + 2 * i
+                pull(r + 1, odd)
+                stream(r)
+                turn(r, even)
+                pull(jnp.minimum(r + 2, BLOCKS - 1), even)
+                stream(r + 1)
+                turn(r + 1, odd)
+                moved(flat, final, sem, r).start()
+                moved(flat, final, sem, r + 1).start()
+                return carry
+
+            lax.fori_loop(0, BLOCKS // 4, pair, 0)
+            for i, p in enumerate(INNER):
+                copy(i, p, h).start()
+        edge_last(ready_n, other, got, om_ref, un_ref, grad, hold, near_sem, NEAR, flip)
+        for h in range(2):
+            for i, p in enumerate(INNER):
+                copy(i, p, h).wait()
         loop(lambda r: moved(flat, final, sem, r).wait())
 
     by_side(run)
 
 
-def edge_last(ready, got, om_ref, u_ref, grad, hold, sem, p, flip):
-    half = ROWS // 2
-
+def edge_last(ready, other, got, om_ref, u_ref, grad, hold, sem, p, flip):
     def copy(i):
-        rows = pl.ds(i * half, half)
+        rows = pl.ds(i * PIECE * 8, PIECE * 8)
         return pltpu.make_async_copy(
             hold.at[:, rows, :], grad.at[:, rows, place(flip, p), :], sem.at[i]
         )
 
-    def body(r):
-        mu = edge_values(ready, got, p, r, -1)
-        out = adjoint(mu, get(u_ref, r, count=3), om_ref[p, block(r), :])
-        put_mirrored(hold, out, flip, r)
-
-    def pairs(first):
-        def pair(r, carry):
-            body(first + 2 * r)
-            body(first + 2 * r + 1)
-            return carry
-
-        lax.fori_loop(0, BLOCKS // 4, pair, 0)
-
-    pairs(0)
-    copy(0).start()
-    pairs(BLOCKS // 2)
-    copy(1).start()
-    copy(0).wait()
-    copy(1).wait()
+    receive(other, got, p, -1)
+    for i in range(BLOCKS // PIECE):
+        for r in range(i * PIECE, (i + 1) * PIECE):
+            mu = edge_values(ready, got, p, r, -1)
+            out = adjoint(mu, get(u_ref, r, count=3), om_ref[p, block(r), :])
+            put_mirrored(hold, out, flip, r)
+        copy(i).start()
+    for i in range(BLOCKS // PIECE):
+        copy(i).wait()
 
 
 def far_last(ready, other, om_ref, u_ref, partial, grad, hold, sem, got):
-    receive(other, got, FAR, -1)
-    by_side(lambda flip: edge_last(ready, got, om_ref, u_ref, grad, hold, sem, FAR, flip))
+    by_side(
+        lambda flip: edge_last(ready, other, got, om_ref, u_ref, grad, hold, sem, FAR, flip)
+    )
 
 
 INSIDE = pl.BlockSpec(memory_space=pltpu.VMEM)
 OUTSIDE = pl.BlockSpec(memory_space=pltpu.HBM)
-STEP = 2
+STEP, PIECE = 2, 2
 INNERS = (19, 2, ROWS, LANES)
 PLANE = (19, ROWS, LANES)
 RELAX = (PLANES, ROWS, LANES)
@@ -546,18 +562,19 @@
     pops, classes, cot = to_native(populations), to_native(relax_class), to_native(cotangent)
     inners, plane, cross = (INNERS, 1), (PLANE, 1), (CROSS, 1)
     speed, speeds, state = ((3, ROWS, LANES), 1), ((3, 2, ROWS, LANES), 1), ((4, ROWS, LANES), 1)
-    held, om, post_f, post_n, u0_f, u0_n, far, near = kernel(
+    om, post_f, post_n, u0_f, u0_n, far, near = kernel(
         first_edges,
-        [(NATIVE, 1), (RELAX, 1), plane, plane, speed, speed, cross, cross],
-        [pltpu.VMEM(classes.shape, jnp.int32), SEMS, pltpu.SemaphoreType.DMA],
-    )((pops, 0), (classes, 0))
+        [(RELAX, 1), plane, plane, speed, speed, cross, cross],
+        [pltpu.VMEM(PLANE, F32), pltpu.VMEM(PLANE, F32), pltpu.VMEM(classes.shape, jnp.int32)]
+        + [SEMS, SEMS, pltpu.SemaphoreType.DMA],
+    )((pops.reshape(RESULT), 0), (classes, 0))
     cot, far, near = lax.optimization_barrier((cot, far, near))
     far, near = exchange(far, near)
     cot_f, cot_i, cot_n, cfar, cnear = kernel(cotangent_planes, [plane, inners, plane, cross, cross])(
         cot
     )
     cfar, cnear = exchange(cfar, cnear)
-    post_i, u0_i = kernel(first_inner, [inners, speeds])(held, om)
+    post_i, u0_i = kernel(first_inner, [inners, speeds])(pops, om)
     inner = kernel(forward_inner, [inners, speeds, plane, plane])
 
     post_i, u1_i, ready_f, ready_n = inner(post_f, post_i, post_n, om)
@@ -584,15 +601,16 @@
     lam_n, near = edge[1](ready_n, near, om, u1_n)
     lam_f, far = edge[0](ready_f, far, om, u1_f)
     far, near = exchange(far, near)
-    pair_sem = pltpu.SemaphoreType.DMA((2,))
+    quad_sem = pltpu.SemaphoreType.DMA((4,))
     grad, ready_f, final = kernel(
         finish,
         [(RESULT, 0), plane, (NATIVE, 0)],
-        [pltpu.VMEM(NATIVE, F32), pltpu.VMEM(PLANE, F32), SEMS, pair_sem, pair_sem]
+        [pltpu.VMEM(NATIVE, F32), pltpu.VMEM(PLANE, F32), SEMS, quad_sem, quad_sem]
         + [pltpu.VMEM(INNERS, F32), pltpu.VMEM(PLANE, F32)]
+        + [pltpu.VMEM((38, 8, LANES), F32), pltpu.VMEM((38, 8, LANES), F32)]
         + GOT,
     )(lam_f, lam_i, lam_n, om, u0_i, u0_n, near, post_f, post_i, post_n, pfar, pnear)
-    (grad,) = kernel(far_last, [(RESULT, 0)], [pltpu.VMEM(PLANE, F32), pair_sem] + GOT, {4: 0})(
+    (grad,) = kernel(far_last, [(RESULT, 0)], [pltpu.VMEM(PLANE, F32), quad_sem] + GOT, {4: 0})(
         ready_f, far, om, u0_f, (grad, 0)
     )
     final = jnp.swapaxes(final.reshape(19, ROWS, PLANES, LANES), 1, 2)

time: 37.5 us -> 37.4 us (level)
  no operation moved by 1% of the time
where the time goes in v6:
time: 37.4 us; the launch traced here: 37.2 us
  starting transfers between devices  20.3 us (54%)
  Pallas kernels  15.2 us (41%)
  waiting for transfers between devices  0.87 us (2%)
  between operations  0.8 us (2%)
    ppermute x6, starting transfers between devices, exchange(): return (lax.ppermute(far, 'gx', far_pairs), near)  19.2 us
    pallas_call x15, Pallas kernels, call(): pl.pallas_call(body, in_specs=[INSIDE if inside else OUTSIDE for _, insid...  15.2 us
    ppermute x6, starting transfers between devices, exchange(): near = lax.ppermute(near, 'gx', near_pairs)  1.13 us
    ppermute x6, waiting for transfers between devices, exchange(): return (lax.ppermute(far, 'gx', far_pairs), near)  0.86 us
  transfers between devices with their start and end apart: 12, of which 3 were waited for; matrix products, arithmetic and copies ran while one was open for 0% of the time, Pallas kernels for 33%

profile of v6, /device:TPU:0, one launch (start us, length us, event | category | flops | bytes accessed | tf_op | source)
XLA Modules:
  0.0 37.2 jit_solution(12683405144086947731)
XLA Ops:
  0.6 1.9 %first_edges.1 = (f32[4,64,128]{2,1,0:T(8,128)S(1)}, f32[19,64,128]{2,1,0:T(8,128)S(1)}, f32[19,64,128]{2,1,0:T(8,128)S(1)}, f32[3,64,128]{2,1,0:T(8,128)S(1)}, ...) custom-call(f32[19,64,4,128]{3,2,1,0:T(4,128)} %bitcast.23, s32[256,128]{1,0:T(8,128)} %bitcast.27), custom_call_target="tpu_custom_call" | custom-call | tf_op jit(solution)/shard_map/first_edges/pallas_call | solution.py:527
  2.5 5.5 %collective-permute-start = (f32[5,64,128]{2,1,0:T(8,128)S(1)}, f32[5,64,128]{2,1,0:T(8,128)S(1)}, u32[]{:S(2)}, u32[]{:S(2)}) collective-permute-start(f32[5,64,128]{2,1,0:T(8,128)S(1)} %get-tuple-element.66), channel_id=1, source_target_pairs={{0,15},{1,2},{2,1},{3,4},{4,3},{5,6},{6,5},{7,8},{8,7},{9,10},{10,... | collective-permute-start | bytes 491528 | tf_op jit(solution)/shard_map/ppermute | solution.py:555
  8.0 0.4 %cotangent_planes.1 = (f32[19,64,128]{2,1,0:T(8,128)S(1)}, f32[19,2,64,128]{3,2,1,0:T(8,128)S(1)}, f32[19,64,128]{2,1,0:T(8,128)S(1)}, f32[5,64,128]{2,1,0:T(8,128)S(1)}, f32[5,64,128]{2,1,0:T(8,128)S(1)}) custom-call(f32[19,256,128]{2,1,0:T(8,128)S(1)} %bitcast.25), custom_call_target="tpu_custom_call" | custom-call | tf_op jit(solution)/shard_map/cotangent_planes/pallas_call | solution.py:527
  8.4 0.8 %collective-permute-start.3 = (f32[5,64,128]{2,1,0:T(8,128)S(1)}, f32[5,64,128]{2,1,0:T(8,128)S(1)}, u32[]{:S(2)}, u32[]{:S(2)}) collective-permute-start(f32[5,64,128]{2,1,0:T(8,128)S(1)} %get-tuple-element.78), channel_id=1, source_target_pairs={{0,15},{1,2},{2,1},{3,4},{4,3},{5,6},{6,5},{7,8},{8,7},{9,10},{10,... | collective-permute-start | bytes 491528 | tf_op jit(solution)/shard_map/ppermute | solution.py:555
  9.3 0.5 %first_inner.1 = (f32[19,2,64,128]{3,2,1,0:T(8,128)S(1)}, f32[3,2,64,128]{3,2,1,0:T(8,128)S(1)}) custom-call(f32[19,256,128]{2,1,0:T(8,128)S(1)} %bitcast.24, f32[4,64,128]{2,1,0:T(8,128)S(1)} %get-tuple-element.59.om_ref), custom_call_target="tpu_custom_call" | custom-call | tf_op jit(solution)/shard_map/first_inner/pallas_call | solution.py:527
  9.7 1.2 %forward_inner.2 = (f32[19,2,64,128]{3,2,1,0:T(8,128)S(1)}, f32[3,2,64,128]{3,2,1,0:T(8,128)S(1)}, f32[19,64,128]{2,1,0:T(8,128)S(1)}, f32[19,64,128]{2,1,0:T(8,128)S(1)}) custom-call(f32[19,64,128]{2,1,0:T(8,128)S(1)} %get-tuple-element.58.far, f32[19,2,64,128]{3,2,1,0:T(8,128)S(1)} %get-tuple-element.60.inner, f32[19,64,128]{2,1,0:T(8,128)S(1)} %get-tuple-element.61.near, ...), custom_call_target="tpu_custom_call" | custom-call | tf_op jit(solution)/shard_map/forward_inner/pallas_call | solution.py:527
  11.0 0.7 %forward_edges.1 = (f32[19,64,128]{2,1,0:T(8,128)S(1)}, f32[19,64,128]{2,1,0:T(8,128)S(1)}, f32[3,64,128]{2,1,0:T(8,128)S(1)}, f32[3,64,128]{2,1,0:T(8,128)S(1)}...) custom-call(f32[19,64,128]{2,1,0:T(8,128)S(1)} %get-tuple-element.62.ready_f, ...), custom_call_target="tpu_custom_call" | custom-call | tf_op jit(solution)/shard_map/forward_edges/pallas_call | solution.py:527
  11.7 0.5 %collective-permute-start.5 = (f32[5,64,128]{2,1,0:T(8,128)S(1)}, f32[5,64,128]{2,1,0:T(8,128)S(1)}, u32[]{:S(2)}, u32[]{:S(2)}) collective-permute-start(f32[5,64,128]{2,1,0:T(8,128)S(1)} %get-tuple-element.84), channel_id=1, source_target_pairs={{0,1},{1,0},{2,3},{3,2},{4,5},{5,4},{6,7},{7,6},{8,9},{9,8},{10,11... | collective-permute-start | bytes 491528 | tf_op jit(solution)/shard_map/ppermute | solution.py:554
  12.2 4.2 %collective-permute-start.2 = (f32[5,64,128]{2,1,0:T(8,128)S(1)}, f32[5,64,128]{2,1,0:T(8,128)S(1)}, u32[]{:S(2)}, u32[]{:S(2)}) collective-permute-start(f32[5,64,128]{2,1,0:T(8,128)S(1)} %get-tuple-element.72), channel_id=1, source_target_pairs={{0,15},{1,2},{2,1},{3,4},{4,3},{5,6},{6,5},{7,8},{8,7},{9,10},{10,... | collective-permute-start | bytes 491528 | tf_op jit(solution)/shard_map/ppermute | solution.py:555
  16.4 1.2 %forward_inner.3 = (f32[19,2,64,128]{3,2,1,0:T(8,128)S(1)}, f32[3,2,64,128]{3,2,1,0:T(8,128)S(1)}, f32[19,64,128]{2,1,0:T(8,128)S(1)}, f32[19,64,128]{2,1,0:T(8,128)S(1)}) custom-call(f32[19,64,128]{2,1,0:T(8,128)S(1)} %get-tuple-element.68.far, f32[19,2,64,128]{3,2,1,0:T(8,128)S(1)} %get-tuple-element.69.inner, f32[19,64,128]{2,1,0:T(8,128)S(1)} %get-tuple-element.70.near, ...), custom_call_target="tpu_custom_call" | custom-call | tf_op jit(solution)/shard_map/forward_inner/pallas_call | solution.py:527
  17.6 1.3 %adjoint_top.1 = (f32[19,2,64,128]{3,2,1,0:T(8,128)S(1)}, f32[19,64,128]{2,1,0:T(8,128)S(1)}, f32[19,64,128]{2,1,0:T(8,128)S(1)}) custom-call(f32[19,64,128]{2,1,0:T(8,128)S(1)} %get-tuple-element.74.far, f32[19,2,64,128]{3,2,1,0:T(8,128)S(1)} %get-tuple-element.75.inner, f32[19,64,128]{2,1,0:T(8,128)S(1)} %get-tuple-element.76.near, ...), custom_call_target="tpu_custom_call" | custom-call | tf_op jit(solution)/shard_map/adjoint_top/pallas_call | solution.py:527
  18.9 0.5 %turn_edge.3 = (f32[19,64,128]{2,1,0:T(8,128)S(1)}, f32[5,64,128]{2,1,0:T(8,128)S(1)}, f32[5,64,128]{2,1,0:T(8,128)S(1)}, f32[4,64,128]{2,1,0:T(8,128)S(1)}) custom-call(f32[19,64,128]{2,1,0:T(8,128)S(1)} %get-tuple-element.83.ready.ready_n, f32[5,64,128]{2,1,0:T(8,128)S(1)} %collective-permute-done.5.other, f32[4,64,128]{2,1,0:T(8,128)S(1)} %get-tuple-element.59.om_ref, ...), custom_call_target="tpu_custom_call" | custom-call | tf_op jit(solution)/shard_map/turn_edge/pallas_call | solution.py:527
  19.7 0.5 %turn_edge.2 = (f32[19,64,128]{2,1,0:T(8,128)S(1)}, f32[5,64,128]{2,1,0:T(8,128)S(1)}, f32[5,64,128]{2,1,0:T(8,128)S(1)}, f32[4,64,128]{2,1,0:T(8,128)S(1)}) custom-call(f32[19,64,128]{2,1,0:T(8,128)S(1)} %get-tuple-element.71.ready.ready_f, f32[5,64,128]{2,1,0:T(8,128)S(1)} %collective-permute-done.2.other, f32[4,64,128]{2,1,0:T(8,128)S(1)} %get-tuple-element.59.om_ref, ...), custom_call_target="tpu_custom_call" | custom-call | tf_op jit(solution)/shard_map/turn_edge/pallas_call | solution.py:527
  20.2 4.2 %collective-permute-start.6 = (f32[5,64,128]{2,1,0:T(8,128)S(1)}, f32[5,64,128]{2,1,0:T(8,128)S(1)}, u32[]{:S(2)}, u32[]{:S(2)}) collective-permute-start(f32[5,64,128]{2,1,0:T(8,128)S(1)} %get-tuple-element.89), channel_id=1, source_target_pairs={{0,15},{1,2},{2,1},{3,4},{4,3},{5,6},{6,5},{7,8},{8,7},{9,10},{10,... | collective-permute-start | bytes 491528 | tf_op jit(solution)/shard_map/ppermute | solution.py:555
  24.4 0.4 %relax_edges.1 = (f32[19,64,128]{2,1,0:T(8,128)S(1)}, f32[19,64,128]{2,1,0:T(8,128)S(1)}, f32[5,64,128]{2,1,0:T(8,128)S(1)}, f32[5,64,128]{2,1,0:T(8,128)S(1)}) custom-call(f32[19,64,128]{2,1,0:T(8,128)S(1)} %get-tuple-element.71.ready.ready_f, f32[5,64,128]{2,1,0:T(8,128)S(1)} %get-tuple-element.100.got_f, f32[4,64,128]{2,1,0:T(8,128)S(1)} %get-tuple-element.101.state_f, ...), custom_call_target="tpu_custom_call" | custom-call | tf_op jit(solution)/shard_map/relax_edges/pallas_call | solution.py:527
  24.8 0.4 collective-permute-start.9
  25.1 1.2 %adjoint_inner.1 = (f32[19,2,64,128]{3,2,1,0:T(8,128)S(1)}, f32[19,64,128]{2,1,0:T(8,128)S(1)}, f32[19,64,128]{2,1,0:T(8,128)S(1)}) custom-call(f32[19,64,128]{2,1,0:T(8,128)S(1)} %get-tuple-element.81.far, f32[19,2,64,128]{3,2,1,0:T(8,128)S(1)} %get-tuple-element.82.inner, f32[19,64,128]{2,1,0:T(8,128)S(1)} %get-tuple-element.86.near, ...), custom_call_target="tpu_custom_call" | custom-call | tf_op jit(solution)/shard_map/adjoint_inner/pallas_call | solution.py:527
  26.3 0.4 %adjoint_edge.3 = (f32[19,64,128]{2,1,0:T(8,128)S(1)}, f32[5,64,128]{2,1,0:T(8,128)S(1)}) custom-call(f32[19,64,128]{2,1,0:T(8,128)S(1)} %get-tuple-element.93.ready, f32[5,64,128]{2,1,0:T(8,128)S(1)} %collective-permute-done.7.other, f32[4,64,128]{2,1,0:T(8,128)S(1)} %get-tuple-element.59.om_ref, f32[3,64,128]{2,1,0:T(8,128)S(1)} %get-tuple-element.95.u_ref), custom_call_target="tpu_custom_call" | custom-call | tf_op jit(solution)/shard_map/adjoint_edge/pallas_call | solution.py:527
  26.7 0.6 %collective-permute-start.8 = (f32[5,64,128]{2,1,0:T(8,128)S(1)}, f32[5,64,128]{2,1,0:T(8,128)S(1)}, u32[]{:S(2)}, u32[]{:S(2)}) collective-permute-start(f32[5,64,128]{2,1,0:T(8,128)S(1)} %get-tuple-element.99), channel_id=1, source_target_pairs={{0,1},{1,0},{2,3},{3,2},{4,5},{5,4},{6,7},{7,6},{8,9},{9,8},{10,11... | collective-permute-start | bytes 491528 | tf_op jit(solution)/shard_map/ppermute | solution.py:554
  27.3 0.5 %collective-permute-done.6.other = f32[5,64,128]{2,1,0:T(8,128)S(1)} collective-permute-done((f32[5,64,128]{2,1,0:T(8,128)S(1)}, f32[5,64,128]{2,1,0:T(8,128)S(1)}, u32[]{:S(2)}, u32[]{:S(2)}) %collective-permute-start.6) | collective-permute-done | bytes 163872 | tf_op jit(solution)/shard_map/ppermute | solution.py:555
  27.8 0.4 %adjoint_edge.2 = (f32[19,64,128]{2,1,0:T(8,128)S(1)}, f32[5,64,128]{2,1,0:T(8,128)S(1)}) custom-call(f32[19,64,128]{2,1,0:T(8,128)S(1)} %get-tuple-element.88.ready, f32[5,64,128]{2,1,0:T(8,128)S(1)} %collective-permute-done.6.other, f32[4,64,128]{2,1,0:T(8,128)S(1)} %get-tuple-element.59.om_ref, f32[3,64,128]{2,1,0:T(8,128)S(1)} %get-tuple-element.90.u_ref), custom_call_target="tpu_custom_call" | custom-call | tf_op jit(solution)/shard_map/adjoint_edge/pallas_call | solution.py:527
  28.2 4.1 %collective-permute-start.11 = (f32[5,64,128]{2,1,0:T(8,128)S(1)}, f32[5,64,128]{2,1,0:T(8,128)S(1)}, u32[]{:S(2)}, u32[]{:S(2)}) collective-permute-start(f32[5,64,128]{2,1,0:T(8,128)S(1)} %get-tuple-element.111), channel_id=1, source_target_pairs={{0,15},{1,2},{2,1},{3,4},{4,3},{5,6},{6,5},{7,8},{8,7},{9,10},{10,... | collective-permute-start | bytes 491528 | tf_op jit(solution)/shard_map/ppermute | solution.py:555
  32.3 3.8 %finish.1 = (f32[19,64,4,128]{3,2,1,0:T(4,128)}, f32[19,64,128]{2,1,0:T(8,128)S(1)}, f32[19,256,128]{2,1,0:T(8,128)}) custom-call(f32[19,64,128]{2,1,0:T(8,128)S(1)} %get-tuple-element.91.far, f32[19,2,64,128]{3,2,1,0:T(8,128)S(1)} %get-tuple-element.92.inner, f32[19,64,128]{2,1,0:T(8,128)S(1)} %get-tuple-element.96.near, ...), custom_call_target="tpu_custom_call" | custom-call | tf_op jit(solution)/shard_map/finish/pallas_call | solution.py:527
  36.2 1.0 %far_last.1 = f32[19,64,4,128]{3,2,1,0:T(4,128)} custom-call(f32[19,64,128]{2,1,0:T(8,128)S(1)} %get-tuple-element.110.ready, f32[5,64,128]{2,1,0:T(8,128)S(1)} %collective-permute-done.11.other, f32[4,64,128]{2,1,0:T(8,128)S(1)} %get-tuple-element.59.om_ref, f32[3,64,128]{2,1,0:T(8,128)S(1)} %get-tuple-element.112.u_ref, ...), custom_call_target="tpu_custom_call", output_to_operand_aliasing={{}: (4, {})} | custom-call | tf_op jit(solution)/shard_map/far_last/pallas_call | solution.py:527
  (19 shorter events, 0.5 us)
Async XLA Ops:
  0.6 7.4 %copy-start.1 = (f32[19,4,8192]{2,1,0:T(4,128)S(1)}, f32[19,4,8192]{2,1,0:T(4,128)}, u32[]{:S(2)}) copy-start(f32[19,4,8192]{2,1,0:T(4,128)} %param.5) | copy-start | bytes 7471108
  2.5 6.7 %copy-start = (f32[19,4,8192]{2,1,0:T(4,128)S(1)}, f32[19,4,8192]{2,1,0:T(4,128)}, u32[]{:S(2)}) copy-start(f32[19,4,8192]{2,1,0:T(4,128)} %param.3) | copy-start | bytes 7471108
  2.5 8.5 %collective-permute-start = (f32[5,64,128]{2,1,0:T(8,128)S(1)}, f32[5,64,128]{2,1,0:T(8,128)S(1)}, u32[]{:S(2)}, u32[]{:S(2)}) collective-permute-start(f32[5,64,128]{2,1,0:T(8,128)S(1)} %get-tuple-element.66), channel_id=1, source_target_pairs={{0,15},{1,2},{2,1},{3,4},{4,3},{5,6},{6,5},{7,8},{8,7},{9,10},{10,... | collective-permute-start | bytes 491528 | tf_op jit(solution)/shard_map/ppermute | solution.py:555
  8.0 3.0 %collective-permute-start.1 = (f32[5,64,128]{2,1,0:T(8,128)S(1)}, f32[5,64,128]{2,1,0:T(8,128)S(1)}, u32[]{:S(2)}, u32[]{:S(2)}) collective-permute-start(f32[5,64,128]{2,1,0:T(8,128)S(1)} %get-tuple-element.67), channel_id=1, source_target_pairs={{0,1},{1,0},{2,3},{3,2},{4,5},{5,4},{6,7},{7,6},{8,9},{9,8},{10,11... | collective-permute-start | bytes 491528 | tf_op jit(solution)/shard_map/ppermute | solution.py:554
  8.4 9.2 %collective-permute-start.3 = (f32[5,64,128]{2,1,0:T(8,128)S(1)}, f32[5,64,128]{2,1,0:T(8,128)S(1)}, u32[]{:S(2)}, u32[]{:S(2)}) collective-permute-start(f32[5,64,128]{2,1,0:T(8,128)S(1)} %get-tuple-element.78), channel_id=1, source_target_pairs={{0,15},{1,2},{2,1},{3,4},{4,3},{5,6},{6,5},{7,8},{8,7},{9,10},{10,... | collective-permute-start | bytes 491528 | tf_op jit(solution)/shard_map/ppermute | solution.py:555
  9.2 8.4 %collective-permute-start.4 = (f32[5,64,128]{2,1,0:T(8,128)S(1)}, f32[5,64,128]{2,1,0:T(8,128)S(1)}, u32[]{:S(2)}, u32[]{:S(2)}) collective-permute-start(f32[5,64,128]{2,1,0:T(8,128)S(1)} %get-tuple-element.79), channel_id=1, source_target_pairs={{0,1},{1,0},{2,3},{3,2},{4,5},{5,4},{6,7},{7,6},{8,9},{9,8},{10,11... | collective-permute-start | bytes 491528 | tf_op jit(solution)/shard_map/ppermute | solution.py:554
  11.7 7.2 %collective-permute-start.5 = (f32[5,64,128]{2,1,0:T(8,128)S(1)}, f32[5,64,128]{2,1,0:T(8,128)S(1)}, u32[]{:S(2)}, u32[]{:S(2)}) collective-permute-start(f32[5,64,128]{2,1,0:T(8,128)S(1)} %get-tuple-element.84), channel_id=1, source_target_pairs={{0,1},{1,0},{2,3},{3,2},{4,5},{5,4},{6,7},{7,6},{8,9},{9,8},{10,11... | collective-permute-start | bytes 491528 | tf_op jit(solution)/shard_map/ppermute | solution.py:554
  12.2 7.5 %collective-permute-start.2 = (f32[5,64,128]{2,1,0:T(8,128)S(1)}, f32[5,64,128]{2,1,0:T(8,128)S(1)}, u32[]{:S(2)}, u32[]{:S(2)}) collective-permute-start(f32[5,64,128]{2,1,0:T(8,128)S(1)} %get-tuple-element.72), channel_id=1, source_target_pairs={{0,15},{1,2},{2,1},{3,4},{4,3},{5,6},{6,5},{7,8},{8,7},{9,10},{10,... | collective-permute-start | bytes 491528 | tf_op jit(solution)/shard_map/ppermute | solution.py:555
  19.4 6.9 %collective-permute-start.7 = (f32[5,64,128]{2,1,0:T(8,128)S(1)}, f32[5,64,128]{2,1,0:T(8,128)S(1)}, u32[]{:S(2)}, u32[]{:S(2)}) collective-permute-start(f32[5,64,128]{2,1,0:T(8,128)S(1)} %get-tuple-element.94), channel_id=1, source_target_pairs={{0,1},{1,0},{2,3},{3,2},{4,5},{5,4},{6,7},{7,6},{8,9},{9,8},{10,11... | collective-permute-start | bytes 491528 | tf_op jit(solution)/shard_map/ppermute | solution.py:554
  20.2 7.6 %collective-permute-start.6 = (f32[5,64,128]{2,1,0:T(8,128)S(1)}, f32[5,64,128]{2,1,0:T(8,128)S(1)}, u32[]{:S(2)}, u32[]{:S(2)}) collective-permute-start(f32[5,64,128]{2,1,0:T(8,128)S(1)} %get-tuple-element.89), channel_id=1, source_target_pairs={{0,15},{1,2},{2,1},{3,4},{4,3},{5,6},{6,5},{7,8},{8,7},{9,10},{10,... | collective-permute-start | bytes 491528 | tf_op jit(solution)/shard_map/ppermute | solution.py:555
  24.8 7.5 %collective-permute-start.9 = (f32[5,64,128]{2,1,0:T(8,128)S(1)}, f32[5,64,128]{2,1,0:T(8,128)S(1)}, u32[]{:S(2)}, u32[]{:S(2)}) collective-permute-start(f32[5,64,128]{2,1,0:T(8,128)S(1)} %get-tuple-element.107), channel_id=1, source_target_pairs={{0,15},{1,2},{2,1},{3,4},{4,3},{5,6},{6,5},{7,8},{8,7},{9,10},{10,... | collective-permute-start | bytes 491528 | tf_op jit(solution)/shard_map/ppermute | solution.py:555
  25.1 7.2 %collective-permute-start.10 = (f32[5,64,128]{2,1,0:T(8,128)S(1)}, f32[5,64,128]{2,1,0:T(8,128)S(1)}, u32[]{:S(2)}, u32[]{:S(2)}) collective-permute-start(f32[5,64,128]{2,1,0:T(8,128)S(1)} %get-tuple-element.108), channel_id=1, source_target_pairs={{0,1},{1,0},{2,3},{3,2},{4,5},{5,4},{6,7},{7,6},{8,9},{9,8},{10,11... | collective-permute-start | bytes 491528 | tf_op jit(solution)/shard_map/ppermute | solution.py:554
  26.7 5.6 %collective-permute-start.8 = (f32[5,64,128]{2,1,0:T(8,128)S(1)}, f32[5,64,128]{2,1,0:T(8,128)S(1)}, u32[]{:S(2)}, u32[]{:S(2)}) collective-permute-start(f32[5,64,128]{2,1,0:T(8,128)S(1)} %get-tuple-element.99), channel_id=1, source_target_pairs={{0,1},{1,0},{2,3},{3,2},{4,5},{5,4},{6,7},{7,6},{8,9},{9,8},{10,11... | collective-permute-start | bytes 491528 | tf_op jit(solution)/shard_map/ppermute | solution.py:554
  28.2 8.0 %collective-permute-start.11 = (f32[5,64,128]{2,1,0:T(8,128)S(1)}, f32[5,64,128]{2,1,0:T(8,128)S(1)}, u32[]{:S(2)}, u32[]{:S(2)}) collective-permute-start(f32[5,64,128]{2,1,0:T(8,128)S(1)} %get-tuple-element.111), channel_id=1, source_target_pairs={{0,15},{1,2},{2,1},{3,4},{4,3},{5,6},{6,5},{7,8},{8,7},{9,10},{10,... | collective-permute-start | bytes 491528 | tf_op jit(solution)/shard_map/ppermute | solution.py:555

commit v7 on v6

--- a/solution.py
+++ b/solution.py
@@ -222,24 +222,14 @@
     return pltpu.make_async_copy(chunk(source, r), chunk(target, r), sem.at[r])
 
 
-def first_edges(
-    pops, classes, om_ref, post_f, post_n, u_f, u_n, far_out, near_out, held_f, held_n, cls_ref, sem_f, sem_n, cls_sem
-):
+def first_far(pops, classes, om_ref, post, u_ref, out_ref, held, cls_ref, sem, cls_sem):
     fetch = pltpu.make_async_copy(classes, cls_ref, cls_sem)
-    sides = (
-        (FAR, held_f, sem_f, post_f, u_f, far_out),
-        (NEAR, held_n, sem_n, post_n, u_n, near_out),
-    )
 
     def run(flip):
-        def copy(p, held, sem, r):
+        def copy(r):
             return pltpu.make_async_copy(
-                pops.at[:, block(r), place(flip, p), :], held.at[:, block(r), :], sem.at[r]
+                pops.at[:, block(r), place(flip, FAR), :], held.at[:, block(r), :], sem.at[r]
             )
-
-        def start(r):
-            for p, held, sem, *_ in sides:
-                copy(p, held, sem, r).start()
 
         def body(r):
             for p in range(PLANES):
@@ -248,17 +238,15 @@
                 for entry in range(1, 4):
                     om = jnp.where(cls == entry, RATES[entry], om)
                 om_ref[p, block(r), :] = om
-            for p, held, sem, *_ in sides:
-                copy(p, held, sem, r).wait()
-            for p, held, sem, post, u_ref, out_ref in sides:
-                f = [held[mirrored(flip, k), block(r), :] for k in range(19)]
-                rho, u = state_of(f)
-                put(u_ref, u, r)
-                out = relaxed(f, rho, u, om_ref[p, block(r), :])
-                put(post, out, r)
-                put_crossing(out_ref, out, p, r, 1)
-
-        loop(start)
+            copy(r).wait()
+            f = [held[mirrored(flip, k), block(r), :] for k in range(19)]
+            rho, u = state_of(f)
+            put(u_ref, u, r)
+            out = relaxed(f, rho, u, om_ref[FAR, block(r), :])
+            put(post, out, r)
+            put_crossing(out_ref, out, FAR, r, 1)
+
+        loop(lambda r: copy(r).start())
         fetch.wait()
         loop(body)
 
@@ -266,14 +254,21 @@
     by_side(run)
 
 
-def first_inner(held, om_ref, post, u_ref):
+def first_rest(pops, om_ref, post_i, post_n, u_i, u_n, out_ref):
     def run(flip):
         def body(r):
-            for i, p in enumerate(INNER):
-                f = get_native(held, flip, p, r)
+            for p in (*INNER, NEAR):
+                f = get_native(pops, flip, p, r)
                 rho, u = state_of(f)
-                put(u_ref, u, r, (i,))
-                put(post, relaxed(f, rho, u, om_ref[p, block(r), :]), r, (i,))
+                out = relaxed(f, rho, u, om_ref[p, block(r), :])
+                if p == NEAR:
+                    put(u_n, u, r)
+                    put(post_n, out, r)
+                    put_crossing(out_ref, out, p, r, 1)
+                else:
+                    i = (INNER.index(p),)
+                    put(u_i, u, r, i)
+                    put(post_i, out, r, i)
 
         loop(body)
 
@@ -562,19 +557,22 @@
     pops, classes, cot = to_native(populations), to_native(relax_class), to_native(cotangent)
     inners, plane, cross = (INNERS, 1), (PLANE, 1), (CROSS, 1)
     speed, speeds, state = ((3, ROWS, LANES), 1), ((3, 2, ROWS, LANES), 1), ((4, ROWS, LANES), 1)
-    om, post_f, post_n, u0_f, u0_n, far, near = kernel(
-        first_edges,
-        [(RELAX, 1), plane, plane, speed, speed, cross, cross],
-        [pltpu.VMEM(PLANE, F32), pltpu.VMEM(PLANE, F32), pltpu.VMEM(classes.shape, jnp.int32)]
-        + [SEMS, SEMS, pltpu.SemaphoreType.DMA],
+    om, post_f, u0_f, far = kernel(
+        first_far,
+        [(RELAX, 1), plane, speed, cross],
+        [pltpu.VMEM(PLANE, F32), pltpu.VMEM(classes.shape, jnp.int32), SEMS, pltpu.SemaphoreType.DMA],
     )((pops.reshape(RESULT), 0), (classes, 0))
-    cot, far, near = lax.optimization_barrier((cot, far, near))
-    far, near = exchange(far, near)
+    cot, far = lax.optimization_barrier((cot, far))
+    far = lax.ppermute(far, "gx", far_pairs)
     cot_f, cot_i, cot_n, cfar, cnear = kernel(cotangent_planes, [plane, inners, plane, cross, cross])(
         cot
     )
+    pops, cfar, cnear = lax.optimization_barrier((pops, cfar, cnear))
     cfar, cnear = exchange(cfar, cnear)
-    post_i, u0_i = kernel(first_inner, [inners, speeds])(pops, om)
+    post_i, post_n, u0_i, u0_n, near = kernel(first_rest, [inners, plane, speeds, speed, cross])(
+        pops, om
+    )
+    near = lax.ppermute(near, "gx", near_pairs)
     inner = kernel(forward_inner, [inners, speeds, plane, plane])
 
     post_i, u1_i, ready_f, ready_n = inner(post_f, post_i, post_n, om)

time: 37.4 us -> 37.9 us (1.013)
  waiting for transfers between devices: 0.87 us -> 2.97 us
  starting transfers between devices: 20.3 us -> 18.8 us
    ppermute x6 -> x5, starting transfers between devices: 19.2 us -> 12 us  [exchange(): return (lax.ppermute(far, 'gx', far_pairs), near)]
    ppermute x0 -> x2, starting transfers between devices: none -> 5.55 us  [the longest x1 5.48 us: local(): far = lax.ppermute(far, 'gx', far_pairs)]
    ppermute x6 -> x5, waiting for transfers between devices: 0.86 us -> 2.96 us  [exchange(): return (lax.ppermute(far, 'gx', far_pairs), near)]
    ppermute x6 -> x5, starting transfers between devices: 1.13 us -> 1.22 us  [exchange(): near = lax.ppermute(near, 'gx', near_pairs)]
where the time goes in v7:
time: 37.9 us; the launch traced here: 37.7 us
  starting transfers between devices  18.8 us (50%)
  Pallas kernels  15.2 us (40%)
  waiting for transfers between devices  2.97 us (8%)
  between operations  0.82 us (2%)
    pallas_call x15, Pallas kernels, call(): pl.pallas_call(body, in_specs=[INSIDE if inside else OUTSIDE for _, insid...  15.2 us
    ppermute x5, starting transfers between devices, exchange(): return (lax.ppermute(far, 'gx', far_pairs), near)  12 us
    ppermute x1, starting transfers between devices, local(): far = lax.ppermute(far, 'gx', far_pairs)  5.48 us
    ppermute x5, waiting for transfers between devices, exchange(): return (lax.ppermute(far, 'gx', far_pairs), near)  2.96 us
    ppermute x5, starting transfers between devices, exchange(): near = lax.ppermute(near, 'gx', near_pairs)  1.22 us
  transfers between devices with their start and end apart: 12, of which 3 were waited for; matrix products, arithmetic and copies ran while one was open for 0% of the time, Pallas kernels for 33%

profile of v7, /device:TPU:0, one launch (start us, length us, event | category | flops | bytes accessed | tf_op | source)
XLA Modules:
  0.0 37.7 jit_solution(9821749620110187145)
XLA Ops:
  0.6 1.6 %first_far.1 = (f32[4,64,128]{2,1,0:T(8,128)S(1)}, f32[19,64,128]{2,1,0:T(8,128)S(1)}, f32[3,64,128]{2,1,0:T(8,128)S(1)}, f32[5,64,128]{2,1,0:T(8,128)S(1)}) custom-call(f32[19,64,4,128]{3,2,1,0:T(4,128)} %bitcast.23, s32[256,128]{1,0:T(8,128)} %bitcast.27), custom_call_target="tpu_custom_call" | custom-call | tf_op jit(solution)/shard_map/first_far/pallas_call | solution.py:522
  2.2 5.5 %collective-permute-start = (f32[5,64,128]{2,1,0:T(8,128)S(1)}, f32[5,64,128]{2,1,0:T(8,128)S(1)}, u32[]{:S(2)}, u32[]{:S(2)}) collective-permute-start(f32[5,64,128]{2,1,0:T(8,128)S(1)} %get-tuple-element.71), channel_id=1, source_target_pairs={{0,15},{1,2},{2,1},{3,4},{4,3},{5,6},{6,5},{7,8},{8,7},{9,10},{10,... | collective-permute-start | bytes 491528 | tf_op jit(solution)/shard_map/ppermute | solution.py:566
  7.7 0.4 %cotangent_planes.1 = (f32[19,64,128]{2,1,0:T(8,128)S(1)}, f32[19,2,64,128]{3,2,1,0:T(8,128)S(1)}, f32[19,64,128]{2,1,0:T(8,128)S(1)}, f32[5,64,128]{2,1,0:T(8,128)S(1)}, f32[5,64,128]{2,1,0:T(8,128)S(1)}) custom-call(f32[19,256,128]{2,1,0:T(8,128)S(1)} %bitcast.25), custom_call_target="tpu_custom_call" | custom-call | tf_op jit(solution)/shard_map/cotangent_planes/pallas_call | solution.py:522
  8.1 0.7 %first_rest.1 = (f32[19,2,64,128]{3,2,1,0:T(8,128)S(1)}, f32[19,64,128]{2,1,0:T(8,128)S(1)}, f32[3,2,64,128]{3,2,1,0:T(8,128)S(1)}, f32[3,64,128]{2,1,0:T(8,128)S(1)}, f32[5,64,128]{2,1,0:T(8,128)S(1)}) custom-call(f32[19,256,128]{2,1,0:T(8,128)S(1)} %bitcast.24, f32[4,64,128]{2,1,0:T(8,128)S(1)} %get-tuple-element.66.om_ref), custom_call_target="tpu_custom_call" | custom-call | tf_op jit(solution)/shard_map/first_rest/pallas_call | solution.py:522
  9.0 2.0 %collective-permute-start.3 = (f32[5,64,128]{2,1,0:T(8,128)S(1)}, f32[5,64,128]{2,1,0:T(8,128)S(1)}, u32[]{:S(2)}, u32[]{:S(2)}) collective-permute-start(f32[5,64,128]{2,1,0:T(8,128)S(1)} %get-tuple-element.82), channel_id=1, source_target_pairs={{0,15},{1,2},{2,1},{3,4},{4,3},{5,6},{6,5},{7,8},{8,7},{9,10},{10,... | collective-permute-start | bytes 491528 | tf_op jit(solution)/shard_map/ppermute | solution.py:550
  10.9 1.2 %forward_inner.2 = (f32[19,2,64,128]{3,2,1,0:T(8,128)S(1)}, f32[3,2,64,128]{3,2,1,0:T(8,128)S(1)}, f32[19,64,128]{2,1,0:T(8,128)S(1)}, f32[19,64,128]{2,1,0:T(8,128)S(1)}) custom-call(f32[19,64,128]{2,1,0:T(8,128)S(1)} %get-tuple-element.60.far, f32[19,2,64,128]{3,2,1,0:T(8,128)S(1)} %get-tuple-element.67.inner, f32[19,64,128]{2,1,0:T(8,128)S(1)} %get-tuple-element.68.near, ...), custom_call_target="tpu_custom_call" | custom-call | tf_op jit(solution)/shard_map/forward_inner/pallas_call | solution.py:522
  12.1 0.7 %forward_edges.1 = (f32[19,64,128]{2,1,0:T(8,128)S(1)}, f32[19,64,128]{2,1,0:T(8,128)S(1)}, f32[3,64,128]{2,1,0:T(8,128)S(1)}, f32[3,64,128]{2,1,0:T(8,128)S(1)}...) custom-call(f32[19,64,128]{2,1,0:T(8,128)S(1)} %get-tuple-element.69.ready_f, ...), custom_call_target="tpu_custom_call" | custom-call | tf_op jit(solution)/shard_map/forward_edges/pallas_call | solution.py:522
  12.8 0.6 %collective-permute-start.5 = (f32[5,64,128]{2,1,0:T(8,128)S(1)}, f32[5,64,128]{2,1,0:T(8,128)S(1)}, u32[]{:S(2)}, u32[]{:S(2)}) collective-permute-start(f32[5,64,128]{2,1,0:T(8,128)S(1)} %get-tuple-element.88), channel_id=1, source_target_pairs={{0,1},{1,0},{2,3},{3,2},{4,5},{5,4},{6,7},{7,6},{8,9},{9,8},{10,11... | collective-permute-start | bytes 491528 | tf_op jit(solution)/shard_map/ppermute | solution.py:549
  13.4 2.7 %collective-permute-start.2 = (f32[5,64,128]{2,1,0:T(8,128)S(1)}, f32[5,64,128]{2,1,0:T(8,128)S(1)}, u32[]{:S(2)}, u32[]{:S(2)}) collective-permute-start(f32[5,64,128]{2,1,0:T(8,128)S(1)} %get-tuple-element.77), channel_id=1, source_target_pairs={{0,15},{1,2},{2,1},{3,4},{4,3},{5,6},{6,5},{7,8},{8,7},{9,10},{10,... | collective-permute-start | bytes 491528 | tf_op jit(solution)/shard_map/ppermute | solution.py:550
  16.1 1.2 %forward_inner.3 = (f32[19,2,64,128]{3,2,1,0:T(8,128)S(1)}, f32[3,2,64,128]{3,2,1,0:T(8,128)S(1)}, f32[19,64,128]{2,1,0:T(8,128)S(1)}, f32[19,64,128]{2,1,0:T(8,128)S(1)}) custom-call(f32[19,64,128]{2,1,0:T(8,128)S(1)} %get-tuple-element.73.far, f32[19,2,64,128]{3,2,1,0:T(8,128)S(1)} %get-tuple-element.74.inner, f32[19,64,128]{2,1,0:T(8,128)S(1)} %get-tuple-element.75.near, ...), custom_call_target="tpu_custom_call" | custom-call | tf_op jit(solution)/shard_map/forward_inner/pallas_call | solution.py:522
  17.3 1.3 %adjoint_top.1 = (f32[19,2,64,128]{3,2,1,0:T(8,128)S(1)}, f32[19,64,128]{2,1,0:T(8,128)S(1)}, f32[19,64,128]{2,1,0:T(8,128)S(1)}) custom-call(f32[19,64,128]{2,1,0:T(8,128)S(1)} %get-tuple-element.78.far, f32[19,2,64,128]{3,2,1,0:T(8,128)S(1)} %get-tuple-element.79.inner, f32[19,64,128]{2,1,0:T(8,128)S(1)} %get-tuple-element.80.near, ...), custom_call_target="tpu_custom_call" | custom-call | tf_op jit(solution)/shard_map/adjoint_top/pallas_call | solution.py:522
  18.6 0.5 %turn_edge.3 = (f32[19,64,128]{2,1,0:T(8,128)S(1)}, f32[5,64,128]{2,1,0:T(8,128)S(1)}, f32[5,64,128]{2,1,0:T(8,128)S(1)}, f32[4,64,128]{2,1,0:T(8,128)S(1)}) custom-call(f32[19,64,128]{2,1,0:T(8,128)S(1)} %get-tuple-element.87.ready.ready_n, f32[5,64,128]{2,1,0:T(8,128)S(1)} %collective-permute-done.5.other, f32[4,64,128]{2,1,0:T(8,128)S(1)} %get-tuple-element.66.om_ref, ...), custom_call_target="tpu_custom_call" | custom-call | tf_op jit(solution)/shard_map/turn_edge/pallas_call | solution.py:522
  19.2 1.7 %collective-permute-done.2.other = f32[5,64,128]{2,1,0:T(8,128)S(1)} collective-permute-done((f32[5,64,128]{2,1,0:T(8,128)S(1)}, f32[5,64,128]{2,1,0:T(8,128)S(1)}, u32[]{:S(2)}, u32[]{:S(2)}) %collective-permute-start.2) | collective-permute-done | bytes 163872 | tf_op jit(solution)/shard_map/ppermute | solution.py:550
  20.9 0.5 %turn_edge.2 = (f32[19,64,128]{2,1,0:T(8,128)S(1)}, f32[5,64,128]{2,1,0:T(8,128)S(1)}, f32[5,64,128]{2,1,0:T(8,128)S(1)}, f32[4,64,128]{2,1,0:T(8,128)S(1)}) custom-call(f32[19,64,128]{2,1,0:T(8,128)S(1)} %get-tuple-element.76.ready.ready_f, f32[5,64,128]{2,1,0:T(8,128)S(1)} %collective-permute-done.2.other, f32[4,64,128]{2,1,0:T(8,128)S(1)} %get-tuple-element.66.om_ref, ...), custom_call_target="tpu_custom_call" | custom-call | tf_op jit(solution)/shard_map/turn_edge/pallas_call | solution.py:522
  21.3 2.8 %collective-permute-start.6 = (f32[5,64,128]{2,1,0:T(8,128)S(1)}, f32[5,64,128]{2,1,0:T(8,128)S(1)}, u32[]{:S(2)}, u32[]{:S(2)}) collective-permute-start(f32[5,64,128]{2,1,0:T(8,128)S(1)} %get-tuple-element.93), channel_id=1, source_target_pairs={{0,15},{1,2},{2,1},{3,4},{4,3},{5,6},{6,5},{7,8},{8,7},{9,10},{10,... | collective-permute-start | bytes 491528 | tf_op jit(solution)/shard_map/ppermute | solution.py:550
  24.5 1.8 %collective-permute-start.9 = (f32[5,64,128]{2,1,0:T(8,128)S(1)}, f32[5,64,128]{2,1,0:T(8,128)S(1)}, u32[]{:S(2)}, u32[]{:S(2)}) collective-permute-start(f32[5,64,128]{2,1,0:T(8,128)S(1)} %get-tuple-element.111), channel_id=1, source_target_pairs={{0,15},{1,2},{2,1},{3,4},{4,3},{5,6},{6,5},{7,8},{8,7},{9,10},{10,... | collective-permute-start | bytes 491528 | tf_op jit(solution)/shard_map/ppermute | solution.py:550
  26.3 1.2 %adjoint_inner.1 = (f32[19,2,64,128]{3,2,1,0:T(8,128)S(1)}, f32[19,64,128]{2,1,0:T(8,128)S(1)}, f32[19,64,128]{2,1,0:T(8,128)S(1)}) custom-call(f32[19,64,128]{2,1,0:T(8,128)S(1)} %get-tuple-element.85.far, f32[19,2,64,128]{3,2,1,0:T(8,128)S(1)} %get-tuple-element.86.inner, f32[19,64,128]{2,1,0:T(8,128)S(1)} %get-tuple-element.90.near, ...), custom_call_target="tpu_custom_call" | custom-call | tf_op jit(solution)/shard_map/adjoint_inner/pallas_call | solution.py:522
  27.5 0.4 %adjoint_edge.3 = (f32[19,64,128]{2,1,0:T(8,128)S(1)}, f32[5,64,128]{2,1,0:T(8,128)S(1)}) custom-call(f32[19,64,128]{2,1,0:T(8,128)S(1)} %get-tuple-element.97.ready, f32[5,64,128]{2,1,0:T(8,128)S(1)} %collective-permute-done.7.other, f32[4,64,128]{2,1,0:T(8,128)S(1)} %get-tuple-element.66.om_ref, f32[3,64,128]{2,1,0:T(8,128)S(1)} %get-tuple-element.99.u_ref), custom_call_target="tpu_custom_call" | custom-call | tf_op jit(solution)/shard_map/adjoint_edge/pallas_call | solution.py:522
  27.9 0.6 %collective-permute-start.8 = (f32[5,64,128]{2,1,0:T(8,128)S(1)}, f32[5,64,128]{2,1,0:T(8,128)S(1)}, u32[]{:S(2)}, u32[]{:S(2)}) collective-permute-start(f32[5,64,128]{2,1,0:T(8,128)S(1)} %get-tuple-element.103), channel_id=1, source_target_pairs={{0,1},{1,0},{2,3},{3,2},{4,5},{5,4},{6,7},{7,6},{8,9},{9,8},{10,11... | collective-permute-start | bytes 491528 | tf_op jit(solution)/shard_map/ppermute | solution.py:549
  28.8 0.4 %adjoint_edge.2 = (f32[19,64,128]{2,1,0:T(8,128)S(1)}, f32[5,64,128]{2,1,0:T(8,128)S(1)}) custom-call(f32[19,64,128]{2,1,0:T(8,128)S(1)} %get-tuple-element.92.ready, f32[5,64,128]{2,1,0:T(8,128)S(1)} %collective-permute-done.6.other, f32[4,64,128]{2,1,0:T(8,128)S(1)} %get-tuple-element.66.om_ref, f32[3,64,128]{2,1,0:T(8,128)S(1)} %get-tuple-element.94.u_ref), custom_call_target="tpu_custom_call" | custom-call | tf_op jit(solution)/shard_map/adjoint_edge/pallas_call | solution.py:522
  29.2 2.8 %collective-permute-start.11 = (f32[5,64,128]{2,1,0:T(8,128)S(1)}, f32[5,64,128]{2,1,0:T(8,128)S(1)}, u32[]{:S(2)}, u32[]{:S(2)}) collective-permute-start(f32[5,64,128]{2,1,0:T(8,128)S(1)} %get-tuple-element.115), channel_id=1, source_target_pairs={{0,15},{1,2},{2,1},{3,4},{4,3},{5,6},{6,5},{7,8},{8,7},{9,10},{10,... | collective-permute-start | bytes 491528 | tf_op jit(solution)/shard_map/ppermute | solution.py:550
  32.0 3.8 %finish.1 = (f32[19,64,4,128]{3,2,1,0:T(4,128)}, f32[19,64,128]{2,1,0:T(8,128)S(1)}, f32[19,256,128]{2,1,0:T(8,128)}) custom-call(f32[19,64,128]{2,1,0:T(8,128)S(1)} %get-tuple-element.95.far, f32[19,2,64,128]{3,2,1,0:T(8,128)S(1)} %get-tuple-element.96.inner, f32[19,64,128]{2,1,0:T(8,128)S(1)} %get-tuple-element.100.near, ...), custom_call_target="tpu_custom_call" | custom-call | tf_op jit(solution)/shard_map/finish/pallas_call | solution.py:522
  35.8 0.9 %collective-permute-done.11.other = f32[5,64,128]{2,1,0:T(8,128)S(1)} collective-permute-done((f32[5,64,128]{2,1,0:T(8,128)S(1)}, f32[5,64,128]{2,1,0:T(8,128)S(1)}, u32[]{:S(2)}, u32[]{:S(2)}) %collective-permute-start.11) | collective-permute-done | bytes 163872 | tf_op jit(solution)/shard_map/ppermute | solution.py:550
  36.7 1.0 %far_last.1 = f32[19,64,4,128]{3,2,1,0:T(4,128)} custom-call(f32[19,64,128]{2,1,0:T(8,128)S(1)} %get-tuple-element.114.ready, f32[5,64,128]{2,1,0:T(8,128)S(1)} %collective-permute-done.11.other, f32[4,64,128]{2,1,0:T(8,128)S(1)} %get-tuple-element.66.om_ref, f32[3,64,128]{2,1,0:T(8,128)S(1)} %get-tuple-element.116.u_ref, ...), custom_call_target="tpu_custom_call", output_to_operand_aliasing={{}: (4, {})} | custom-call | tf_op jit(solution)/shard_map/far_last/pallas_call | solution.py:522
  (19 shorter events, 0.9 us)
Async XLA Ops:
  0.6 7.1 %copy-start.1 = (f32[19,4,8192]{2,1,0:T(4,128)S(1)}, f32[19,4,8192]{2,1,0:T(4,128)}, u32[]{:S(2)}) copy-start(f32[19,4,8192]{2,1,0:T(4,128)} %param.5) | copy-start | bytes 7471108
  2.2 5.9 %copy-start = (f32[19,4,8192]{2,1,0:T(4,128)S(1)}, f32[19,4,8192]{2,1,0:T(4,128)}, u32[]{:S(2)}) copy-start(f32[19,4,8192]{2,1,0:T(4,128)} %param.3) | copy-start | bytes 7471108
  2.2 9.9 %collective-permute-start = (f32[5,64,128]{2,1,0:T(8,128)S(1)}, f32[5,64,128]{2,1,0:T(8,128)S(1)}, u32[]{:S(2)}, u32[]{:S(2)}) collective-permute-start(f32[5,64,128]{2,1,0:T(8,128)S(1)} %get-tuple-element.71), channel_id=1, source_target_pairs={{0,15},{1,2},{2,1},{3,4},{4,3},{5,6},{6,5},{7,8},{8,7},{9,10},{10,... | collective-permute-start | bytes 491528 | tf_op jit(solution)/shard_map/ppermute | solution.py:566
  8.9 3.2 %collective-permute-start.1 = (f32[5,64,128]{2,1,0:T(8,128)S(1)}, f32[5,64,128]{2,1,0:T(8,128)S(1)}, u32[]{:S(2)}, u32[]{:S(2)}) collective-permute-start(f32[5,64,128]{2,1,0:T(8,128)S(1)} %get-tuple-element.72), channel_id=1, source_target_pairs={{0,1},{1,0},{2,3},{3,2},{4,5},{5,4},{6,7},{7,6},{8,9},{9,8},{10,11... | collective-permute-start | bytes 491528 | tf_op jit(solution)/shard_map/ppermute | solution.py:575
  9.0 8.3 %collective-permute-start.3 = (f32[5,64,128]{2,1,0:T(8,128)S(1)}, f32[5,64,128]{2,1,0:T(8,128)S(1)}, u32[]{:S(2)}, u32[]{:S(2)}) collective-permute-start(f32[5,64,128]{2,1,0:T(8,128)S(1)} %get-tuple-element.82), channel_id=1, source_target_pairs={{0,15},{1,2},{2,1},{3,4},{4,3},{5,6},{6,5},{7,8},{8,7},{9,10},{10,... | collective-permute-start | bytes 491528 | tf_op jit(solution)/shard_map/ppermute | solution.py:550
  10.9 6.4 %collective-permute-start.4 = (f32[5,64,128]{2,1,0:T(8,128)S(1)}, f32[5,64,128]{2,1,0:T(8,128)S(1)}, u32[]{:S(2)}, u32[]{:S(2)}) collective-permute-start(f32[5,64,128]{2,1,0:T(8,128)S(1)} %get-tuple-element.83), channel_id=1, source_target_pairs={{0,1},{1,0},{2,3},{3,2},{4,5},{5,4},{6,7},{7,6},{8,9},{9,8},{10,11... | collective-permute-start | bytes 491528 | tf_op jit(solution)/shard_map/ppermute | solution.py:549
  12.8 5.8 %collective-permute-start.5 = (f32[5,64,128]{2,1,0:T(8,128)S(1)}, f32[5,64,128]{2,1,0:T(8,128)S(1)}, u32[]{:S(2)}, u32[]{:S(2)}) collective-permute-start(f32[5,64,128]{2,1,0:T(8,128)S(1)} %get-tuple-element.88), channel_id=1, source_target_pairs={{0,1},{1,0},{2,3},{3,2},{4,5},{5,4},{6,7},{7,6},{8,9},{9,8},{10,11... | collective-permute-start | bytes 491528 | tf_op jit(solution)/shard_map/ppermute | solution.py:549
  13.4 7.4 %collective-permute-start.2 = (f32[5,64,128]{2,1,0:T(8,128)S(1)}, f32[5,64,128]{2,1,0:T(8,128)S(1)}, u32[]{:S(2)}, u32[]{:S(2)}) collective-permute-start(f32[5,64,128]{2,1,0:T(8,128)S(1)} %get-tuple-element.77), channel_id=1, source_target_pairs={{0,15},{1,2},{2,1},{3,4},{4,3},{5,6},{6,5},{7,8},{8,7},{9,10},{10,... | collective-permute-start | bytes 491528 | tf_op jit(solution)/shard_map/ppermute | solution.py:550
  19.1 8.4 %collective-permute-start.7 = (f32[5,64,128]{2,1,0:T(8,128)S(1)}, f32[5,64,128]{2,1,0:T(8,128)S(1)}, u32[]{:S(2)}, u32[]{:S(2)}) collective-permute-start(f32[5,64,128]{2,1,0:T(8,128)S(1)} %get-tuple-element.98), channel_id=1, source_target_pairs={{0,1},{1,0},{2,3},{3,2},{4,5},{5,4},{6,7},{7,6},{8,9},{9,8},{10,11... | collective-permute-start | bytes 491528 | tf_op jit(solution)/shard_map/ppermute | solution.py:549
  21.3 7.5 %collective-permute-start.6 = (f32[5,64,128]{2,1,0:T(8,128)S(1)}, f32[5,64,128]{2,1,0:T(8,128)S(1)}, u32[]{:S(2)}, u32[]{:S(2)}) collective-permute-start(f32[5,64,128]{2,1,0:T(8,128)S(1)} %get-tuple-element.93), channel_id=1, source_target_pairs={{0,15},{1,2},{2,1},{3,4},{4,3},{5,6},{6,5},{7,8},{8,7},{9,10},{10,... | collective-permute-start | bytes 491528 | tf_op jit(solution)/shard_map/ppermute | solution.py:550
  24.5 7.5 %collective-permute-start.9 = (f32[5,64,128]{2,1,0:T(8,128)S(1)}, f32[5,64,128]{2,1,0:T(8,128)S(1)}, u32[]{:S(2)}, u32[]{:S(2)}) collective-permute-start(f32[5,64,128]{2,1,0:T(8,128)S(1)} %get-tuple-element.111), channel_id=1, source_target_pairs={{0,15},{1,2},{2,1},{3,4},{4,3},{5,6},{6,5},{7,8},{8,7},{9,10},{10,... | collective-permute-start | bytes 491528 | tf_op jit(solution)/shard_map/ppermute | solution.py:550
  26.3 5.7 %collective-permute-start.10 = (f32[5,64,128]{2,1,0:T(8,128)S(1)}, f32[5,64,128]{2,1,0:T(8,128)S(1)}, u32[]{:S(2)}, u32[]{:S(2)}) collective-permute-start(f32[5,64,128]{2,1,0:T(8,128)S(1)} %get-tuple-element.112), channel_id=1, source_target_pairs={{0,1},{1,0},{2,3},{3,2},{4,5},{5,4},{6,7},{7,6},{8,9},{9,8},{10,11... | collective-permute-start | bytes 491528 | tf_op jit(solution)/shard_map/ppermute | solution.py:549
  27.9 4.1 %collective-permute-start.8 = (f32[5,64,128]{2,1,0:T(8,128)S(1)}, f32[5,64,128]{2,1,0:T(8,128)S(1)}, u32[]{:S(2)}, u32[]{:S(2)}) collective-permute-start(f32[5,64,128]{2,1,0:T(8,128)S(1)} %get-tuple-element.103), channel_id=1, source_target_pairs={{0,1},{1,0},{2,3},{3,2},{4,5},{5,4},{6,7},{7,6},{8,9},{9,8},{10,11... | collective-permute-start | bytes 491528 | tf_op jit(solution)/shard_map/ppermute | solution.py:549
  29.2 7.5 %collective-permute-start.11 = (f32[5,64,128]{2,1,0:T(8,128)S(1)}, f32[5,64,128]{2,1,0:T(8,128)S(1)}, u32[]{:S(2)}, u32[]{:S(2)}) collective-permute-start(f32[5,64,128]{2,1,0:T(8,128)S(1)} %get-tuple-element.115), channel_id=1, source_target_pairs={{0,15},{1,2},{2,1},{3,4},{4,3},{5,6},{6,5},{7,8},{8,7},{9,10},{10,... | collective-permute-start | bytes 491528 | tf_op jit(solution)/shard_map/ppermute | solution.py:550
